TPU v7x, 32 devices: a whole 2x2x4 slice. The times are simulated.
32 devices in a mesh: batch: 4 (over x, core), seq: 8 (over z, y).
Axes of the slice: x: 2, y: 2, z: 4, core: 2. Of those that a mesh axis runs over, the one named last changes fastest.
Arguments:
- tokens: bfloat16 [4, 1024, 768], P('batch', 'seq'), may hold values from -6 to 6
- memory: bfloat16 [4, 1024, 768], P('batch', 'seq'), may hold values from -6 to 6
- target_segments: int32 [4, 1024], P('batch'), may hold values from 0 to 14, as said below
- memory_segments: int32 [4, 1024], P('batch'), may hold values from 0 to 14, as said below
- cotangent: bfloat16 [4, 1024, 768], P('batch', 'seq'), may hold values from -6 to 6
- selfquery: bfloat16 [768, 768], P(('batch', 'seq')), may hold values from -0.21875 to 0.21875
- selfkey: bfloat16 [768, 768], P(('batch', 'seq')), may hold values from -0.21875 to 0.21875
- selfvalue: bfloat16 [768, 768], P(('batch', 'seq')), may hold values from -0.21875 to 0.21875
- selfout: bfloat16 [768, 768], P(('batch', 'seq')), may hold values from -1.75 to 1.75
- selfqbias: bfloat16 [768], P(('batch', 'seq')), may hold values from -1.75 to 1.75
- selfvbias: bfloat16 [768], P(('batch', 'seq')), may hold values from -1.75 to 1.75
- selfobias: bfloat16 [768], P(('batch', 'seq')), may hold values from -3.5 to 3.5
- selfgain: bfloat16 [768], P(('batch', 'seq')), may hold values from 0.25 to 1.75
- selfshift: bfloat16 [768], P(('batch', 'seq')), may hold values from -1.75 to 1.75
- crossquery: bfloat16 [768, 768], P(('batch', 'seq')), may hold values from -0.21875 to 0.21875
- crosskey: bfloat16 [768, 768], P(('batch', 'seq')), may hold values from -0.21875 to 0.21875
- crossvalue: bfloat16 [768, 768], P(('batch', 'seq')), may hold values from -0.21875 to 0.21875
- crossout: bfloat16 [768, 768], P(('batch', 'seq')), may hold values from -1.75 to 1.75
- crossqbias: bfloat16 [768], P(('batch', 'seq')), may hold values from -1.75 to 1.75
- crossvbias: bfloat16 [768], P(('batch', 'seq')), may hold values from -1.75 to 1.75
- crossobias: bfloat16 [768], P(('batch', 'seq')), may hold values from -3.5 to 3.5
- crossgain: bfloat16 [768], P(('batch', 'seq')), may hold values from 0.25 to 1.75
- crossshift: bfloat16 [768], P(('batch', 'seq')), may hold values from -1.75 to 1.75
- innerweight: bfloat16 [768, 3072], P(('batch', 'seq')), may hold values from -0.21875 to 0.21875
- innerbias: bfloat16 [3072], P(('batch', 'seq')), may hold values from -1.75 to 1.75
- outerweight: bfloat16 [3072, 768], P(('batch', 'seq')), may hold values from -0.21875 to 0.21875
- outerbias: bfloat16 [768], P(('batch', 'seq')), may hold values from -1.75 to 1.75
- finalgain: bfloat16 [768], P(('batch', 'seq')), may hold values from 0.25 to 1.75
- finalshift: bfloat16 [768], P(('batch', 'seq')), may hold values from -1.75 to 1.75
Outputs:
- output: bfloat16 [4, 1024, 768], P('batch', 'seq')
- tokens_grad: float32 [4, 1024, 768], P('batch', 'seq')
- memory_grad: float32 [4, 1024, 768], P('batch', 'seq')
- selfquery_grad: float32 [768, 768], P(('batch', 'seq'))
- selfkey_grad: float32 [768, 768], P(('batch', 'seq'))
- selfvalue_grad: float32 [768, 768], P(('batch', 'seq'))
- selfout_grad: float32 [768, 768], P(('batch', 'seq'))
- selfqbias_grad: float32 [768], P(('batch', 'seq'))
- selfvbias_grad: float32 [768], P(('batch', 'seq'))
- selfobias_grad: float32 [768], P(('batch', 'seq'))
- selfgain_grad: float32 [768], P(('batch', 'seq'))
- selfshift_grad: float32 [768], P(('batch', 'seq'))
- crossquery_grad: float32 [768, 768], P(('batch', 'seq'))
- crosskey_grad: float32 [768, 768], P(('batch', 'seq'))
- crossvalue_grad: float32 [768, 768], P(('batch', 'seq'))
- crossout_grad: float32 [768, 768], P(('batch', 'seq'))
- crossqbias_grad: float32 [768], P(('batch', 'seq'))
- crossvbias_grad: float32 [768], P(('batch', 'seq'))
- crossobias_grad: float32 [768], P(('batch', 'seq'))
- crossgain_grad: float32 [768], P(('batch', 'seq'))
- crossshift_grad: float32 [768], P(('batch', 'seq'))
- innerweight_grad: float32 [768, 3072], P(('batch', 'seq'))
- innerbias_grad: float32 [3072], P(('batch', 'seq'))
- outerweight_grad: float32 [3072, 768], P(('batch', 'seq'))
- outerbias_grad: float32 [768], P(('batch', 'seq'))
- finalgain_grad: float32 [768], P(('batch', 'seq'))
- finalshift_grad: float32 [768], P(('batch', 'seq'))
Inputs may be any that keep to these rules, and one draw needn't show every extreme that they name: `target_segments`: along each row the numbers never fall until the padding 0 that ends it; every row holds each of 0 to 14, each document has at least 64 and at most 128 tokens. `memory_segments`: every row holds each of 0 to 14; the documents stand in falling order of their numbers, followed by the padding 0 that ends the row; each document has at least 64 and at most 128 tokens.
All inputs are finite; a program needn't handle non-finite values.
Results may differ from a plain program's by a relative error of at most 0.034.
Values may be sent and summed in bfloat16 or wider, within the bound.
A program may use at most 192 MiB of HBM per device.

v0:
```python
from functools import partial

import jax
import jax.numpy as jnp
from jax import lax
from jax.sharding import PartitionSpec as P

HD = 64


SCALE = 0.125
NEGATIVE = -1e30
EPSILON = 1e-05
block_limit = 1024


def spans(total):
    if total > block_limit and total % block_limit == 0:
        return (block_limit, total // block_limit)
    return (total, 1)


def heads_of(matrix):
    return matrix.reshape(matrix.shape[0], -1, HD)


def normalize(values, gain, shift):
    center = values - jnp.mean(values, axis=-1, keepdims=True)
    spread = jnp.mean(center * center, axis=-1, keepdims=True)
    return center * lax.rsqrt(spread + EPSILON) * gain + shift


def norm_back(values, gain, shift, grad):
    _, pullback = jax.vjp(normalize, values, gain, shift)
    return pullback(grad)


def matmul(left, right):
    return jnp.dot(left, right, preferred_element_type=jnp.float32)


def left_product(left, right):
    return lax.dot_general(
        left, right, (((0,), (0,)), ((), ())), preferred_element_type=jnp.float32
    )


def right_product(left, right):
    return lax.dot_general(
        left, right, (((1,), (1,)), ((), ())), preferred_element_type=jnp.float32
    )


def row_total(matrix):
    return jnp.sum(matrix.astype(jnp.float32), axis=0)


def allowed_mask(query_seg, query_pos, key_seg, key_pos, causal):
    same = query_seg[:, None] == key_seg[None, :]
    if causal:
        same = jnp.logical_and(same, key_pos[None, :] <= query_pos[:, None])
    return same


def block_terms(
    query_block, upstream_block, logsum_block, delta_block, allowed, key_block, value_block
):
    scores = (
        jnp.einsum("qhd,khd->hqk", query_block, key_block, preferred_element_type=jnp.float32)
        * SCALE
    )
    scores = jnp.where(allowed[None], scores, NEGATIVE)
    probs = jnp.where(allowed[None], jnp.exp(scores - logsum_block[:, :, None]), 0.0)
    dprobs = jnp.einsum(
        "qhd,khd->hqk", upstream_block, value_block, preferred_element_type=jnp.float32
    )
    dscores = (probs * (dprobs - delta_block[:, :, None]) * SCALE).astype(jnp.bfloat16)
    return (probs.astype(jnp.bfloat16), dscores)


def attend(queries, keys, values, query_seg, query_pos, key_ids, causal):
    row_count = queries.shape[0]
    head_count = queries.shape[1] // HD
    query_heads = heads_of(queries)
    all_keys, all_values = (
        lax.all_gather(keys, "seq", axis=0, tiled=True),
        lax.all_gather(values, "seq", axis=0, tiled=True),
    )
    block_rows, block_count = spans(all_keys.shape[0])

    def scored(index):
        offset = index * block_rows
        key_block = heads_of(lax.dynamic_slice_in_dim(all_keys, offset, block_rows, 0))
        key_pos = offset + jnp.arange(block_rows, dtype=jnp.int32)
        key_seg = lax.dynamic_slice_in_dim(key_ids, offset, block_rows, 0)
        allowed = allowed_mask(query_seg, query_pos, key_seg, key_pos, causal)[None]
        scores = (
            jnp.einsum("qhd,khd->hqk", query_heads, key_block, preferred_element_type=jnp.float32)
            * SCALE
        )
        return (jnp.where(allowed, scores, NEGATIVE), allowed)

    def stat_step(index, state):
        run_max, run_sum = state
        scores, allowed = scored(index)
        new_max = jnp.maximum(run_max, jnp.max(scores, axis=2))
        weights = jnp.where(allowed, jnp.exp(scores - new_max[:, :, None]), 0.0)
        run_sum = run_sum * jnp.exp(run_max - new_max) + jnp.sum(weights, axis=2)
        return (new_max, run_sum)

    run_max, run_sum = lax.fori_loop(
        0,
        block_count,
        stat_step,
        (
            jnp.full((head_count, row_count), NEGATIVE, jnp.float32),
            jnp.zeros((head_count, row_count), jnp.float32),
        ),
    )
    logsum = run_max + jnp.log(run_sum)

    def value_step(index, accum):
        scores, allowed = scored(index)
        probs = jnp.where(allowed, jnp.exp(scores - logsum[:, :, None]), 0.0).astype(jnp.bfloat16)
        value_block = heads_of(
            lax.dynamic_slice_in_dim(all_values, index * block_rows, block_rows, 0)
        )
        return accum + jnp.einsum(
            "hqk,khd->qhd", probs, value_block, preferred_element_type=jnp.float32
        )

    accum = lax.fori_loop(
        0, block_count, value_step, jnp.zeros((row_count, head_count, HD), jnp.float32)
    )
    outcome = accum.reshape(row_count, head_count * HD)
    return (outcome, logsum)


def head_delta(upstream, context):
    row_count = upstream.shape[0]
    return jnp.sum((upstream.astype(jnp.float32) * context).reshape(row_count, -1, HD), axis=2).T


def attend_back(queries, keys, values, upstream, logsum, delta, query_ids, key_ids, causal):
    row_count = queries.shape[0]
    head_count = queries.shape[1] // HD
    own_first = lax.axis_index("seq") * row_count
    own_pos = own_first + jnp.arange(row_count, dtype=jnp.int32)
    query_seg = lax.dynamic_slice_in_dim(query_ids, own_first, row_count, 0)
    key_seg = lax.dynamic_slice_in_dim(key_ids, own_first, row_count, 0)
    query_heads = heads_of(queries)
    upstream_heads = heads_of(upstream)
    empty = jnp.zeros((row_count, head_count, HD), jnp.float32)
    key_source = lax.all_gather(keys, "seq", axis=0, tiled=True)
    value_source = lax.all_gather(values, "seq", axis=0, tiled=True)
    block_rows, block_count = spans(key_source.shape[0])

    def key_step(index, running):
        local = index * block_rows
        key_block = heads_of(lax.dynamic_slice_in_dim(key_source, local, block_rows, 0))
        value_block = heads_of(lax.dynamic_slice_in_dim(value_source, local, block_rows, 0))
        block_seg = lax.dynamic_slice_in_dim(key_ids, local, block_rows, 0)
        block_pos = local + jnp.arange(block_rows, dtype=jnp.int32)
        allowed = allowed_mask(query_seg, own_pos, block_seg, block_pos, causal)
        probs, dscores = block_terms(
            query_heads, upstream_heads, logsum, delta, allowed, key_block, value_block
        )
        return running + jnp.einsum(
            "hqk,khd->qhd", dscores, key_block, preferred_element_type=jnp.float32
        )

    dqueries = lax.fori_loop(0, block_count, key_step, empty)
    all_logsum, all_delta = (
        lax.all_gather(logsum, "seq", axis=1, tiled=True),
        lax.all_gather(delta, "seq", axis=1, tiled=True),
    )
    key_heads = heads_of(keys)
    value_heads = heads_of(values)
    piece_queries = lax.all_gather(queries, "seq", axis=0, tiled=True)
    piece_upstream = lax.all_gather(upstream, "seq", axis=0, tiled=True)
    query_block_rows, block_count = spans(piece_queries.shape[0])

    def query_step(index, running):
        key_total, value_total = running
        local = index * query_block_rows
        query_block = heads_of(lax.dynamic_slice_in_dim(piece_queries, local, query_block_rows, 0))
        upstream_block = heads_of(
            lax.dynamic_slice_in_dim(piece_upstream, local, query_block_rows, 0)
        )
        logsum_block = lax.dynamic_slice_in_dim(all_logsum, local, query_block_rows, 1)
        delta_block = lax.dynamic_slice_in_dim(all_delta, local, query_block_rows, 1)
        block_seg = lax.dynamic_slice_in_dim(query_ids, local, query_block_rows, 0)
        block_pos = local + jnp.arange(query_block_rows, dtype=jnp.int32)
        allowed = allowed_mask(block_seg, block_pos, key_seg, own_pos, causal)
        probs, dscores = block_terms(
            query_block, upstream_block, logsum_block, delta_block, allowed, key_heads, value_heads
        )
        key_total = key_total + jnp.einsum(
            "hqk,qhd->khd", dscores, query_block, preferred_element_type=jnp.float32
        )
        value_total = value_total + jnp.einsum(
            "hqk,qhd->khd", probs, upstream_block, preferred_element_type=jnp.float32
        )
        return (key_total, value_total)

    key_grad, value_grad = lax.fori_loop(0, block_count, query_step, (empty, empty))
    key_grad = key_grad.reshape(row_count, -1)
    value_grad = value_grad.reshape(row_count, -1)
    return (dqueries.reshape(row_count, -1), key_grad, value_grad)


def shards(
    tokens,
    memory,
    target_segments,
    memory_segments,
    cotangent,
    selfquery,
    selfkey,
    selfvalue,
    selfout,
    selfqbias,
    selfvbias,
    selfobias,
    selfgain,
    selfshift,
    crossquery,
    crosskey,
    crossvalue,
    crossout,
    crossqbias,
    crossvbias,
    crossobias,
    crossgain,
    crossshift,
    innerweight,
    innerbias,
    outerweight,
    outerbias,
    finalgain,
    finalshift,
):
    inputs = tokens[0]
    source = memory[0]
    target_ids = target_segments[0]
    source_ids = memory_segments[0]
    row_count = inputs.shape[0]
    own_first = lax.axis_index("seq") * row_count
    own_pos = own_first + jnp.arange(row_count, dtype=jnp.int32)
    query_seg = lax.dynamic_slice_in_dim(target_ids, own_first, row_count, 0)
    (
        query_full,
        key_full,
        value_full,
        out_full,
        qbias_full,
        vbias_full,
        obias_full,
        sgain_full,
        sshift_full,
    ) = (
        lax.all_gather(selfquery, ("batch", "seq"), axis=0, tiled=True),
        lax.all_gather(selfkey, ("batch", "seq"), axis=0, tiled=True),
        lax.all_gather(selfvalue, ("batch", "seq"), axis=0, tiled=True),
        lax.all_gather(selfout, ("batch", "seq"), axis=0, tiled=True),
        lax.all_gather(selfqbias, ("batch", "seq"), axis=0, tiled=True),
        lax.all_gather(selfvbias, ("batch", "seq"), axis=0, tiled=True),
        lax.all_gather(selfobias, ("batch", "seq"), axis=0, tiled=True),
        lax.all_gather(selfgain, ("batch", "seq"), axis=0, tiled=True),
        lax.all_gather(selfshift, ("batch", "seq"), axis=0, tiled=True),
    )
    sgain = sgain_full.astype(jnp.float32)
    sshift = sshift_full.astype(jnp.float32)
    query_self = (matmul(inputs, query_full) + qbias_full.astype(jnp.float32)).astype(jnp.bfloat16)
    key_self = matmul(inputs, key_full).astype(jnp.bfloat16)
    value_self = (matmul(inputs, value_full) + vbias_full.astype(jnp.float32)).astype(jnp.bfloat16)
    attn_self, logsum_self = attend(
        query_self, key_self, value_self, query_seg, own_pos, target_ids, True
    )
    self_low = attn_self.astype(jnp.bfloat16)
    hidden_one = (
        inputs.astype(jnp.float32) + matmul(self_low, out_full) + obias_full.astype(jnp.float32)
    )
    first = normalize(hidden_one, sgain, sshift)
    first_low = first.astype(jnp.bfloat16)
    (
        cquery_full,
        ckey_full,
        cvalue_full,
        cout_full,
        cqbias_full,
        cvbias_full,
        cobias_full,
        cgain_full,
        cshift_full,
    ) = (
        lax.all_gather(crossquery, ("batch", "seq"), axis=0, tiled=True),
        lax.all_gather(crosskey, ("batch", "seq"), axis=0, tiled=True),
        lax.all_gather(crossvalue, ("batch", "seq"), axis=0, tiled=True),
        lax.all_gather(crossout, ("batch", "seq"), axis=0, tiled=True),
        lax.all_gather(crossqbias, ("batch", "seq"), axis=0, tiled=True),
        lax.all_gather(crossvbias, ("batch", "seq"), axis=0, tiled=True),
        lax.all_gather(crossobias, ("batch", "seq"), axis=0, tiled=True),
        lax.all_gather(crossgain, ("batch", "seq"), axis=0, tiled=True),
        lax.all_gather(crossshift, ("batch", "seq"), axis=0, tiled=True),
    )
    cgain = cgain_full.astype(jnp.float32)
    cshift = cshift_full.astype(jnp.float32)
    query_cross = (matmul(first_low, cquery_full) + cqbias_full.astype(jnp.float32)).astype(
        jnp.bfloat16
    )
    key_cross = matmul(source, ckey_full).astype(jnp.bfloat16)
    value_cross = (matmul(source, cvalue_full) + cvbias_full.astype(jnp.float32)).astype(
        jnp.bfloat16
    )
    attn_cross, logsum_cross = attend(
        query_cross, key_cross, value_cross, query_seg, own_pos, source_ids, False
    )
    cross_low = attn_cross.astype(jnp.bfloat16)
    hidden_two = first + matmul(cross_low, cout_full) + cobias_full.astype(jnp.float32)
    second = normalize(hidden_two, cgain, cshift)
    second_low = second.astype(jnp.bfloat16)
    inner_full, ibias_full, outer_full, obias_feed, fgain_full, fshift_full = (
        lax.all_gather(innerweight, ("batch", "seq"), axis=0, tiled=True),
        lax.all_gather(innerbias, ("batch", "seq"), axis=0, tiled=True),
        lax.all_gather(outerweight, ("batch", "seq"), axis=0, tiled=True),
        lax.all_gather(outerbias, ("batch", "seq"), axis=0, tiled=True),
        lax.all_gather(finalgain, ("batch", "seq"), axis=0, tiled=True),
        lax.all_gather(finalshift, ("batch", "seq"), axis=0, tiled=True),
    )
    fgain = fgain_full.astype(jnp.float32)
    fshift = fshift_full.astype(jnp.float32)
    smooth = partial(jax.nn.gelu, approximate=False)
    inner_pre = matmul(second_low, inner_full) + ibias_full.astype(jnp.float32)
    activation = smooth(inner_pre).astype(jnp.bfloat16)
    hidden_three = second + matmul(activation, outer_full) + obias_feed.astype(jnp.float32)
    output = normalize(hidden_three, fgain, fshift).astype(jnp.bfloat16)
    grad_hidden3, grad_fgain, grad_fshift = norm_back(
        hidden_three, fgain, fshift, cotangent[0].astype(jnp.float32)
    )
    branch_grad = grad_hidden3.astype(jnp.bfloat16)
    grad_outer = left_product(activation, branch_grad)
    grad_obias_feed = row_total(branch_grad)
    _, gelu_back = jax.vjp(smooth, inner_pre)
    inner_grad = gelu_back(right_product(branch_grad, outer_full))[0].astype(jnp.bfloat16)
    grad_inner = left_product(second_low, inner_grad)
    grad_ibias = row_total(inner_grad)
    grad_second = grad_hidden3 + right_product(inner_grad, inner_full)
    feed_grads = (
        lax.psum_scatter(grad_inner, ("batch", "seq"), scatter_dimension=0, tiled=True),
        lax.psum_scatter(grad_ibias, ("batch", "seq"), scatter_dimension=0, tiled=True),
        lax.psum_scatter(grad_outer, ("batch", "seq"), scatter_dimension=0, tiled=True),
        lax.psum_scatter(grad_obias_feed, ("batch", "seq"), scatter_dimension=0, tiled=True),
        lax.psum_scatter(grad_fgain, ("batch", "seq"), scatter_dimension=0, tiled=True),
        lax.psum_scatter(grad_fshift, ("batch", "seq"), scatter_dimension=0, tiled=True),
    )
    grad_hidden2, grad_cgain, grad_cshift = norm_back(hidden_two, cgain, cshift, grad_second)
    cross_branch = grad_hidden2.astype(jnp.bfloat16)
    grad_cout = left_product(cross_low, cross_branch)
    grad_cobias = row_total(cross_branch)
    cross_up = right_product(cross_branch, cout_full).astype(jnp.bfloat16)
    cross_delta = head_delta(cross_up, attn_cross)
    cq_grad, ck_grad, cv_grad = attend_back(
        query_cross,
        key_cross,
        value_cross,
        cross_up,
        logsum_cross,
        cross_delta,
        target_ids,
        source_ids,
        False,
    )
    cq_low = cq_grad.astype(jnp.bfloat16)
    ck_low = ck_grad.astype(jnp.bfloat16)
    cv_low = cv_grad.astype(jnp.bfloat16)
    grad_cquery = left_product(first_low, cq_low)
    grad_cqbias = row_total(cq_low)
    grad_ckey = left_product(source, ck_low)
    grad_cvalue = left_product(source, cv_low)
    grad_cvbias = row_total(cv_low)
    memory_grad = right_product(ck_low, ckey_full) + right_product(cv_low, cvalue_full)
    grad_first = grad_hidden2 + right_product(cq_low, cquery_full)
    cross_grads = (
        lax.psum_scatter(grad_cquery, ("batch", "seq"), scatter_dimension=0, tiled=True),
        lax.psum_scatter(grad_ckey, ("batch", "seq"), scatter_dimension=0, tiled=True),
        lax.psum_scatter(grad_cvalue, ("batch", "seq"), scatter_dimension=0, tiled=True),
        lax.psum_scatter(grad_cout, ("batch", "seq"), scatter_dimension=0, tiled=True),
        lax.psum_scatter(grad_cqbias, ("batch", "seq"), scatter_dimension=0, tiled=True),
        lax.psum_scatter(grad_cvbias, ("batch", "seq"), scatter_dimension=0, tiled=True),
        lax.psum_scatter(grad_cobias, ("batch", "seq"), scatter_dimension=0, tiled=True),
        lax.psum_scatter(grad_cgain, ("batch", "seq"), scatter_dimension=0, tiled=True),
        lax.psum_scatter(grad_cshift, ("batch", "seq"), scatter_dimension=0, tiled=True),
    )
    grad_hidden1, grad_sgain, grad_sshift = norm_back(hidden_one, sgain, sshift, grad_first)
    self_branch = grad_hidden1.astype(jnp.bfloat16)
    grad_out = left_product(self_low, self_branch)
    grad_obias = row_total(self_branch)
    self_up = right_product(self_branch, out_full).astype(jnp.bfloat16)
    self_delta = head_delta(self_up, attn_self)
    sq_grad, sk_grad, sv_grad = attend_back(
        query_self,
        key_self,
        value_self,
        self_up,
        logsum_self,
        self_delta,
        target_ids,
        target_ids,
        True,
    )
    sq_low = sq_grad.astype(jnp.bfloat16)
    sk_low = sk_grad.astype(jnp.bfloat16)
    sv_low = sv_grad.astype(jnp.bfloat16)
    grad_query = left_product(inputs, sq_low)
    grad_qbias = row_total(sq_low)
    grad_key = left_product(inputs, sk_low)
    grad_value = left_product(inputs, sv_low)
    grad_vbias = row_total(sv_low)
    tokens_grad = (
        grad_hidden1
        + right_product(sq_low, query_full)
        + right_product(sk_low, key_full)
        + right_product(sv_low, value_full)
    )
    self_grads = (
        lax.psum_scatter(grad_query, ("batch", "seq"), scatter_dimension=0, tiled=True),
        lax.psum_scatter(grad_key, ("batch", "seq"), scatter_dimension=0, tiled=True),
        lax.psum_scatter(grad_value, ("batch", "seq"), scatter_dimension=0, tiled=True),
        lax.psum_scatter(grad_out, ("batch", "seq"), scatter_dimension=0, tiled=True),
        lax.psum_scatter(grad_qbias, ("batch", "seq"), scatter_dimension=0, tiled=True),
        lax.psum_scatter(grad_vbias, ("batch", "seq"), scatter_dimension=0, tiled=True),
        lax.psum_scatter(grad_obias, ("batch", "seq"), scatter_dimension=0, tiled=True),
        lax.psum_scatter(grad_sgain, ("batch", "seq"), scatter_dimension=0, tiled=True),
        lax.psum_scatter(grad_sshift, ("batch", "seq"), scatter_dimension=0, tiled=True),
    )
    return (
        (output[None], tokens_grad[None], memory_grad[None])
        + tuple(self_grads)
        + tuple(cross_grads)
        + tuple(feed_grads)
    )


def solution(mesh):
    in_specs = (
        P("batch", "seq", None),
        P("batch", "seq", None),
        P("batch", None),
        P("batch", None),
        P("batch", "seq", None),
        P(("batch", "seq"), None),
        P(("batch", "seq"), None),
        P(("batch", "seq"), None),
        P(("batch", "seq"), None),
        P(("batch", "seq")),
        P(("batch", "seq")),
        P(("batch", "seq")),
        P(("batch", "seq")),
        P(("batch", "seq")),
        P(("batch", "seq"), None),
        P(("batch", "seq"), None),
        P(("batch", "seq"), None),
        P(("batch", "seq"), None),
        P(("batch", "seq")),
        P(("batch", "seq")),
        P(("batch", "seq")),
        P(("batch", "seq")),
        P(("batch", "seq")),
        P(("batch", "seq"), None),
        P(("batch", "seq")),
        P(("batch", "seq"), None),
        P(("batch", "seq")),
        P(("batch", "seq")),
        P(("batch", "seq")),
    )
    out_specs = (
        P("batch", "seq", None),
        P("batch", "seq", None),
        P("batch", "seq", None),
        P(("batch", "seq"), None),
        P(("batch", "seq"), None),
        P(("batch", "seq"), None),
        P(("batch", "seq"), None),
        P(("batch", "seq")),
        P(("batch", "seq")),
        P(("batch", "seq")),
        P(("batch", "seq")),
        P(("batch", "seq")),
        P(("batch", "seq"), None),
        P(("batch", "seq"), None),
        P(("batch", "seq"), None),
        P(("batch", "seq"), None),
        P(("batch", "seq")),
        P(("batch", "seq")),
        P(("batch", "seq")),
        P(("batch", "seq")),
        P(("batch", "seq")),
        P(("batch", "seq"), None),
        P(("batch", "seq")),
        P(("batch", "seq"), None),
        P(("batch", "seq")),
        P(("batch", "seq")),
        P(("batch", "seq")),
    )
    return jax.shard_map(shards, mesh=mesh, in_specs=in_specs, out_specs=out_specs, check_vma=False)
```

profile of v0, /device:TPU:0, one launch (start us, length us, event | category | flops | bytes accessed | tf_op | source)
XLA Modules:
  0.0 2078.9 jit_solution(7114225457800477952)
XLA Ops:
  10.8 57.2 %all-gather.25.cloned.1.call-done = bf16[768,768]{1,0:T(8,128)(2,1)} async-done(((bf16[24,768]{1,0:T(8,128)(2,1)}), bf16[768,768]{1,0:T(8,128)(2,1)}) %all-gather.25.cloned.1.call-update) | async-done | bytes 1179664 | tf_op jit(solution)/shard_map/all_gather | solution.py:263
  68.0 2.4 convolution_convert_fusion.3
  73.9 39.6 %all-reduce.29 = (bf16[3072]{0:T(1024)(128)(2,1)S(1)}, bf16[768]{0:T(1024)(128)(2,1)S(1)}, bf16[768]{0:T(1024)(128)(2,1)S(1)}, bf16[768]{0:T(1024)(128)(2,1)S(1)...) all-reduce(bf16[3072]{0:T(1024)(128)(2,1)S(1)} %dynamic-update-slic, ...), channel_id=1, replica_groups=mesh['batch'=4,'seq'=8] {'batch','seq'}, use_global_device_ids=true, to_apply=%add.10 | all-reduce | flops 13056 | bytes 52224
  113.5 10.5 all-gather.19.cloned.1.call-done
  124.1 2.3 fusion.49
  127.9 52.2 %all-gather.37.cloned.1.call-done = bf16[768,768]{1,0:T(8,128)(2,1)} async-done(((bf16[24,768]{1,0:T(8,128)(2,1)}), bf16[768,768]{1,0:T(8,128)(2,1)}) %all-gather.37.cloned.1.call-update) | async-done | bytes 1179664 | tf_op jit(solution)/shard_map/all_gather | solution.py:298
  180.1 2.3 convolution_convert_fusion.2
  182.5 53.5 %all-gather.31.cloned.1.call-done = bf16[768,768]{1,0:T(8,128)(2,1)} async-done(((bf16[24,768]{1,0:T(8,128)(2,1)}), bf16[768,768]{1,0:T(8,128)(2,1)}) %all-gather.31.cloned.1.call-update) | async-done | bytes 1179664 | tf_op jit(solution)/shard_map/all_gather | solution.py:299
  236.0 2.3 fusion.51
  243.5 48.3 %all-gather.23.cloned.1.call-done = bf16[768,768]{1,0:T(8,128)(2,1)} async-done(((bf16[24,768]{1,0:T(8,128)(2,1)}), bf16[768,768]{1,0:T(8,128)(2,1)}) %all-gather.23.cloned.1.call-update) | async-done | bytes 1179664 | tf_op jit(solution)/shard_map/all_gather | solution.py:262
  294.4 42.6 %all-gather.27.cloned.1.call-done = bf16[1024,768]{1,0:T(8,128)(2,1)} async-done(((bf16[128,768]{1,0:T(8,128)(2,1)}), bf16[1024,768]{1,0:T(8,128)(2,1)}) %all-gather.27.cloned.1.call-update) | async-done | bytes 1572880 | tf_op jit(solution)/shard_map/all_gather | solution.py:86
  340.0 2.0 select_reduce_fusion.1
  342.6 40.1 %all-gather.21.cloned.1.call-done = bf16[1024,768]{1,0:T(8,128)(2,1)} async-done(((bf16[128,768]{1,0:T(8,128)(2,1)}), bf16[1024,768]{1,0:T(8,128)(2,1)}) %all-gather.21.cloned.1.call-update) | async-done | bytes 1572880 | tf_op jit(solution)/shard_map/all_gather | solution.py:87
  382.7 2.6 copy.104
  385.3 5.0 fusion.12
  391.3 47.4 %all-gather.29.cloned.1.call-done = bf16[768,768]{1,0:T(8,128)(2,1)} async-done(((bf16[24,768]{1,0:T(8,128)(2,1)}), bf16[768,768]{1,0:T(8,128)(2,1)}) %all-gather.29.cloned.1.call-update) | async-done | bytes 1179664 | tf_op jit(solution)/shard_map/all_gather | solution.py:265
  440.6 54.0 %all-gather.35.cloned.1.call-done = bf16[768,768]{1,0:T(8,128)(2,1)} async-done(((bf16[24,768]{1,0:T(8,128)(2,1)}), bf16[768,768]{1,0:T(8,128)(2,1)}) %all-gather.35.cloned.1.call-update) | async-done | bytes 1179664 | tf_op jit(solution)/shard_map/all_gather | solution.py:297
  496.5 43.3 %all-gather.39.cloned.1.call-done = bf16[1024,768]{1,0:T(8,128)(2,1)} async-done(((bf16[128,768]{1,0:T(8,128)(2,1)}), bf16[1024,768]{1,0:T(8,128)(2,1)}) %all-gather.39.cloned.1.call-update) | async-done | bytes 1572880 | tf_op jit(solution)/shard_map/all_gather | solution.py:86
  539.8 2.6 copy.109
  542.4 2.7 fusion.5
  545.1 2.0 select_reduce_fusion
  547.9 37.7 %all-gather.33.cloned.1.call-done = bf16[1024,768]{1,0:T(8,128)(2,1)} async-done(((bf16[128,768]{1,0:T(8,128)(2,1)}), bf16[1024,768]{1,0:T(8,128)(2,1)}) %all-gather.33.cloned.1.call-update) | async-done | bytes 1572880 | tf_op jit(solution)/shard_map/all_gather | solution.py:87
  585.6 2.6 copy.107
  588.2 5.0 fusion.10
  594.1 47.3 %all-gather.41.cloned.1.call-done = bf16[768,768]{1,0:T(8,128)(2,1)} async-done(((bf16[24,768]{1,0:T(8,128)(2,1)}), bf16[768,768]{1,0:T(8,128)(2,1)}) %all-gather.41.cloned.1.call-update) | async-done | bytes 1179664 | tf_op jit(solution)/shard_map/all_gather | solution.py:300
  643.9 63.0 %all-gather.43.cloned.1.call-done = bf16[768,3072]{1,0:T(8,128)(2,1)} async-done(((bf16[24,3072]{1,0:T(8,128)(2,1)}), bf16[768,3072]{1,0:T(8,128)(2,1)}) %all-gather.43.cloned.1.call-update) | async-done | bytes 4718608 | tf_op jit(solution)/shard_map/all_gather | solution.py:324
  706.9 8.8 multiply_convert_fusion.8
  715.7 56.5 %all-gather.45.cloned.1.call-done = bf16[3072,768]{1,0:T(8,128)(2,1)} async-done(((bf16[96,768]{1,0:T(8,128)(2,1)}), bf16[3072,768]{1,0:T(8,128)(2,1)}) %all-gather.45.cloned.1.call-update) | async-done | bytes 4718608 | tf_op jit(solution)/shard_map/all_gather | solution.py:326
  772.2 3.4 fusion.125
  778.3 2.4 convert_reduce_fusion
  780.7 2.4 multiply_reduce_fusion
  785.8 2.0 copy.112
  789.6 8.4 convert_reduce_fusion.5
  798.1 2.9 multiply_reduce_fusion.1
  807.4 7.9 convert_reduce_fusion.8
  816.7 2.0 copy.129
  822.5 2.1 fusion.116
  831.2 30.6 %all_gather.141 = f32[12,1024]{1,0:T(8,128)S(1)} all-gather(f32[12,128]{1,0:T(8,128)S(1)} %copy-done.61), channel_id=1, replica_groups=mesh['batch'=4,'seq'=8] {'seq'}, dimensions={1}, use_global_device_ids=true | all-gather | bytes 55296 | tf_op jit(solution)/shard_map/all_gather | solution.py:174
  861.9 3.7 fusion.126
  865.6 30.8 %all_gather.143 = f32[12,1024]{1,0:T(8,128)S(1)} all-gather(f32[12,128]{1,0:T(8,128)S(1)} %bitcast.231), channel_id=1, replica_groups=mesh['batch'=4,'seq'=8] {'seq'}, dimensions={1}, use_global_device_ids=true | all-gather | bytes 55296 | tf_op jit(solution)/shard_map/all_gather | solution.py:175
  896.4 2.6 copy.118
  899.0 7.7 fusion.46
  910.6 5.8 convert_reduce_fusion.7
  917.5 1.9 copy.133
  920.7 30.7 %all_gather.145 = f32[12,1024]{1,0:T(8,128)S(1)} all-gather(f32[12,128]{1,0:T(8,128)S(1)} %copy-done.59), channel_id=1, replica_groups=mesh['batch'=4,'seq'=8] {'seq'}, dimensions={1}, use_global_device_ids=true | all-gather | bytes 55296 | tf_op jit(solution)/shard_map/all_gather | solution.py:174
  953.1 3.7 fusion.127
  956.8 30.7 %all_gather.147 = f32[12,1024]{1,0:T(8,128)S(1)} all-gather(f32[12,128]{1,0:T(8,128)S(1)} %bitcast.229), channel_id=1, replica_groups=mesh['batch'=4,'seq'=8] {'seq'}, dimensions={1}, use_global_device_ids=true | all-gather | bytes 55296 | tf_op jit(solution)/shard_map/all_gather | solution.py:175
  987.5 2.6 copy.122
  990.2 7.8 fusion.45
  998.5 2.0 copy.135
  1001.8 5.8 convert_reduce_fusion.4
  1008.0 2.0 copy.137
  1011.1 5.2 fusion.113
  1017.5 5.0 fusion.129
  1028.5 39.1 %all-reduce.28 = (f32[768]{0:T(1024)S(1)}, f32[768]{0:T(1024)S(1)}, f32[768]{0:T(1024)S(1)}, f32[768]{0:T(1024)S(1)}, f32[768]{0:T(1024)S(1)}, /*index=5*/f32[76...) all-reduce(f32[768]{0:T(1024)} %reduce_sum.311, ...), channel_id=6, replica_groups=mesh['batch'=4,'seq'=8] {'batch','seq'}, use_global_device_ids=true, to_apply=%region_23.24.clone | all-reduce | flops 13056 | bytes 104448
  1080.4 82.2 %reduce-scatter.21.cloned.1.call-done = f32[24,768]{1,0:T(8,128)} async-done(((f32[768,768]{1,0:T(8,128)}), f32[24,768]{1,0:T(8,128)}) %reduce-scatter.21.cloned.1.call-update) | async-done | bytes 73744 | tf_op jit(solution)/shard_map/reduce_scatter | solution.py:430
  1162.7 103.9 %reduce-scatter.23.cloned.1.call-done = f32[24,768]{1,0:T(8,128)} async-done(((f32[768,768]{1,0:T(8,128)}), f32[24,768]{1,0:T(8,128)}) %reduce-scatter.23.cloned.1.call-update) | async-done | bytes 73744 | tf_op jit(solution)/shard_map/reduce_scatter | solution.py:385
  1266.6 104.7 %reduce-scatter.25.cloned.1.call-done = f32[24,768]{1,0:T(8,128)} async-done(((f32[768,768]{1,0:T(8,128)}), f32[24,768]{1,0:T(8,128)}) %reduce-scatter.25.cloned.1.call-update) | async-done | bytes 73744 | tf_op jit(solution)/shard_map/reduce_scatter | solution.py:388
  1371.3 103.9 %reduce-scatter.33.cloned.1.call-done = f32[24,768]{1,0:T(8,128)} async-done(((f32[768,768]{1,0:T(8,128)}), f32[24,768]{1,0:T(8,128)}) %reduce-scatter.33.cloned.1.call-update) | async-done | bytes 73744
  1475.2 104.7 %reduce-scatter.35.cloned.1.call-done = f32[24,768]{1,0:T(8,128)} async-done(((f32[768,768]{1,0:T(8,128)}), f32[24,768]{1,0:T(8,128)}) %reduce-scatter.35.cloned.1.call-update) | async-done | bytes 73744
  1579.9 103.8 %reduce-scatter.37.cloned.1.call-done = f32[24,768]{1,0:T(8,128)} async-done(((f32[768,768]{1,0:T(8,128)}), f32[24,768]{1,0:T(8,128)}) %reduce-scatter.37.cloned.1.call-update) | async-done | bytes 73744
  1683.7 104.7 %reduce-scatter.39.cloned.1.call-done = f32[24,768]{1,0:T(8,128)} async-done(((f32[768,768]{1,0:T(8,128)}), f32[24,768]{1,0:T(8,128)}) %reduce-scatter.39.cloned.1.call-update) | async-done | bytes 73744
  1788.4 140.9 %reduce-scatter.27.cloned.1.call-done = f32[24,3072]{1,0:T(8,128)} async-done(((f32[768,3072]{1,0:T(8,128)}), f32[24,3072]{1,0:T(8,128)}) %reduce-scatter.27.cloned.1.call-update) | async-done | bytes 294928 | tf_op jit(solution)/shard_map/reduce_scatter | solution.py:350
  1929.3 142.3 %reduce-scatter.29.cloned.1.call-done = f32[96,768]{1,0:T(8,128)} async-done(((f32[3072,768]{1,0:T(8,128)}), f32[96,768]{1,0:T(8,128)}) %reduce-scatter.29.cloned.1.call-update) | async-done | bytes 294928 | tf_op jit(solution)/shard_map/reduce_scatter | solution.py:352
  (424 shorter events, 84.5 us)
Async XLA Ops:
  7.2 172.9 %copy-start = (bf16[1,128,768]{2,1,0:T(8,128)(2,1)S(1)}, bf16[1,128,768]{2,1,0:T(8,128)(2,1)}, u32[]{:S(2)}) copy-start(bf16[1,128,768]{2,1,0:T(8,128)(2,1)} %param.30) | copy-start | bytes 589828
  7.2 116.9 %copy-start.3 = (bf16[1,128,768]{2,1,0:T(8,128)(2,1)S(1)}, bf16[1,128,768]{2,1,0:T(8,128)(2,1)}, u32[]{:S(2)}) copy-start(bf16[1,128,768]{2,1,0:T(8,128)(2,1)} %param.29) | copy-start | bytes 589828
  7.2 63.3 %copy-start.97 = (bf16[24]{0:T(256)(128)(2,1)S(1)}, bf16[24]{0:T(256)(128)(2,1)}, u32[]{:S(2)}) copy-start(bf16[24]{0:T(256)(128)(2,1)} %param.40) | copy-start | bytes 148
  7.2 63.5 %copy-start.98 = (bf16[24]{0:T(256)(128)(2,1)S(1)}, bf16[24]{0:T(256)(128)(2,1)}, u32[]{:S(2)}) copy-start(bf16[24]{0:T(256)(128)(2,1)} %param.39) | copy-start | bytes 148
  7.3 63.8 %copy-start.99 = (bf16[24]{0:T(256)(128)(2,1)S(1)}, bf16[24]{0:T(256)(128)(2,1)}, u32[]{:S(2)}) copy-start(bf16[24]{0:T(256)(128)(2,1)} %param.38) | copy-start | bytes 148
  7.3 64.0 %copy-start.100 = (bf16[24]{0:T(256)(128)(2,1)S(1)}, bf16[24]{0:T(256)(128)(2,1)}, u32[]{:S(2)}) copy-start(bf16[24]{0:T(256)(128)(2,1)} %param.49) | copy-start | bytes 148
  7.3 64.2 %copy-start.101 = (bf16[24]{0:T(256)(128)(2,1)S(1)}, bf16[24]{0:T(256)(128)(2,1)}, u32[]{:S(2)}) copy-start(bf16[24]{0:T(256)(128)(2,1)} %param.42) | copy-start | bytes 148
  7.3 64.4 %copy-start.102 = (bf16[24]{0:T(256)(128)(2,1)S(1)}, bf16[24]{0:T(256)(128)(2,1)}, u32[]{:S(2)}) copy-start(bf16[24]{0:T(256)(128)(2,1)} %param.41) | copy-start | bytes 148
  7.3 64.7 %copy-start.103 = (bf16[24]{0:T(256)(128)(2,1)S(1)}, bf16[24]{0:T(256)(128)(2,1)}, u32[]{:S(2)}) copy-start(bf16[24]{0:T(256)(128)(2,1)} %param.48) | copy-start | bytes 148
  7.3 64.9 %copy-start.104 = (bf16[24]{0:T(256)(128)(2,1)S(1)}, bf16[24]{0:T(256)(128)(2,1)}, u32[]{:S(2)}) copy-start(bf16[24]{0:T(256)(128)(2,1)} %param.47) | copy-start | bytes 148
  7.3 65.1 %copy-start.105 = (bf16[24]{0:T(256)(128)(2,1)S(1)}, bf16[24]{0:T(256)(128)(2,1)}, u32[]{:S(2)}) copy-start(bf16[24]{0:T(256)(128)(2,1)} %param.51) | copy-start | bytes 148
  7.3 65.3 %copy-start.106 = (bf16[24]{0:T(256)(128)(2,1)S(1)}, bf16[24]{0:T(256)(128)(2,1)}, u32[]{:S(2)}) copy-start(bf16[24]{0:T(256)(128)(2,1)} %param.50) | copy-start | bytes 148
  7.3 65.6 %copy-start.107 = (bf16[24]{0:T(256)(128)(2,1)S(1)}, bf16[24]{0:T(256)(128)(2,1)}, u32[]{:S(2)}) copy-start(bf16[24]{0:T(256)(128)(2,1)} %param.55) | copy-start | bytes 148
  7.3 65.8 %copy-start.108 = (bf16[24]{0:T(256)(128)(2,1)S(1)}, bf16[24]{0:T(256)(128)(2,1)}, u32[]{:S(2)}) copy-start(bf16[24]{0:T(256)(128)(2,1)} %param.57) | copy-start | bytes 148
  7.4 66.0 %copy-start.109 = (bf16[24]{0:T(256)(128)(2,1)S(1)}, bf16[24]{0:T(256)(128)(2,1)}, u32[]{:S(2)}) copy-start(bf16[24]{0:T(256)(128)(2,1)} %param.56) | copy-start | bytes 148
  7.4 66.3 %copy-start.110 = (bf16[96]{0:T(256)(128)(2,1)S(1)}, bf16[96]{0:T(256)(128)(2,1)}, u32[]{:S(2)}) copy-start(bf16[96]{0:T(256)(128)(2,1)} %param.53) | copy-start | bytes 580
  7.4 60.7 %all-gather.25.cloned.1.call-start = ((), (), s32[]{:S(2)}) async-start(), calls=%async_computation.13 | async-start | bytes 1216512 | tf_op jit(solution)/shard_map/all_gather | solution.py:263
  8.1 116.0 %all-gather.19.cloned.1.call-start = ((), (), s32[]{:S(2)}) async-start(), calls=%async_computation.10 | async-start | bytes 1216512 | tf_op jit(solution)/shard_map/all_gather | solution.py:264
  8.9 171.2 %all-gather.37.cloned.1.call-start = ((), (), s32[]{:S(2)}) async-start(), calls=%async_computation.19 | async-start | bytes 1216512 | tf_op jit(solution)/shard_map/all_gather | solution.py:298
  9.6 226.4 %all-gather.31.cloned.1.call-start = ((), (), s32[]{:S(2)}) async-start(), calls=%async_computation.16 | async-start | bytes 1216512 | tf_op jit(solution)/shard_map/all_gather | solution.py:299
  10.2 281.6 %all-gather.23.cloned.1.call-start = ((), (), s32[]{:S(2)}) async-start(), calls=%async_computation.12 | async-start | bytes 1216512 | tf_op jit(solution)/shard_map/all_gather | solution.py:262
  10.8 326.2 %all-gather.27.cloned.1.call-start = ((), (), s32[]{:S(2)}) async-start(), calls=%async_computation.14 | async-start | bytes 1769472 | tf_op jit(solution)/shard_map/all_gather | solution.py:86
  70.5 312.3 %all-gather.21.cloned.1.call-start = ((), (), s32[]{:S(2)}) async-start(), calls=%async_computation.11 | async-start | bytes 1769472 | tf_op jit(solution)/shard_map/all_gather | solution.py:87
  126.4 312.3 %all-gather.29.cloned.1.call-start = ((), (), s32[]{:S(2)}) async-start(), calls=%async_computation.15 | async-start | bytes 1216512 | tf_op jit(solution)/shard_map/all_gather | solution.py:265
  127.1 367.5 %all-gather.35.cloned.1.call-start = ((), (), s32[]{:S(2)}) async-start(), calls=%async_computation.18 | async-start | bytes 1216512 | tf_op jit(solution)/shard_map/all_gather | solution.py:297
  127.9 411.9 %all-gather.39.cloned.1.call-start = ((), (), s32[]{:S(2)}) async-start(), calls=%async_computation.20 | async-start | bytes 1769472 | tf_op jit(solution)/shard_map/all_gather | solution.py:86
  182.4 60.3 %copy-start.66 = (s32[1,1024]{1,0:T(1,128)S(1)}, s32[1,1024]{1,0:T(1,128)}, u32[]{:S(2)}) copy-start(s32[1,1024]{1,0:T(1,128)} %param.31) | copy-start | bytes 12292
  182.4 60.3 %copy-start.86 = (s32[1,1024]{1,0:T(1,128)S(1)}, s32[1,1024]{1,0:T(1,128)}, u32[]{:S(2)}) copy-start(s32[1,1024]{1,0:T(1,128)} %param.32) | copy-start | bytes 12292
  182.4 403.2 %all-gather.33.cloned.1.call-start = ((), (), s32[]{:S(2)}) async-start(), calls=%async_computation.17 | async-start | bytes 1769472 | tf_op jit(solution)/shard_map/all_gather | solution.py:87
  238.3 403.1 %all-gather.41.cloned.1.call-start = ((), (), s32[]{:S(2)}) async-start(), calls=%async_computation.21 | async-start | bytes 1216512 | tf_op jit(solution)/shard_map/all_gather | solution.py:300
  238.8 468.0 %all-gather.43.cloned.1.call-start = ((), (), s32[]{:S(2)}) async-start(), calls=%async_computation.22 | async-start | bytes 4866048 | tf_op jit(solution)/shard_map/all_gather | solution.py:324
  239.6 532.6 %all-gather.45.cloned.1.call-start = ((), (), s32[]{:S(2)}) async-start(), calls=%async_computation.23 | async-start | bytes 4866048 | tf_op jit(solution)/shard_map/all_gather | solution.py:326
  240.2 589.3 %all-gather.47.cloned.1.call-start = ((), (), s32[]{:S(2)}) async-start(), calls=%async_computation.24 | async-start | bytes 1769472 | tf_op jit(solution)/shard_map/all_gather | solution.py:179
  242.7 96.0 %copy-start.89 = (s32[128]{0:T(128)}, s32[128]{0:T(128)S(1)}, u32[]{:S(2)}) copy-start(s32[128]{0:T(128)S(1)} %iota_add_fusion) | copy-start | bytes 1540
  243.2 95.5 %copy-start.87 = (s32[128]{0:T(128)}, s32[128]{0:T(128)S(1)}, u32[]{:S(2)}) copy-start(s32[128]{0:T(128)S(1)} %get-tuple-element.443) | copy-start | bytes 1540
  243.5 141.9 %copy-start.38 = (pred[128,1024]{1,0:T(8,128)(4,1)}, pred[128,1024]{1,0:T(8,128)(4,1)S(1)}, u32[]{:S(2)}) copy-start(pred[128,1024]{1,0:T(8,128)(4,1)S(1)} %get-tuple-element.416) | copy-start | bytes 393220
  243.5 344.7 %copy-start.39 = (pred[128,1024]{1,0:T(8,128)(4,1)}, pred[128,1024]{1,0:T(8,128)(4,1)S(1)}, u32[]{:S(2)}) copy-start(pred[128,1024]{1,0:T(8,128)(4,1)S(1)} %get-tuple-element.415) | copy-start | bytes 393220
  294.1 602.3 %all-gather.49.cloned.1.call-start = ((), (), s32[]{:S(2)}) async-start(), calls=%async_computation.25 | async-start | bytes 1769472 | tf_op jit(solution)/shard_map/all_gather | solution.py:180
  342.6 42.8 %copy-start.60 = (f32[12,128]{1,0:T(8,128)}, f32[12,128]{1,0:T(8,128)S(1)}, u32[]{:S(2)}) copy-start(f32[12,128]{1,0:T(8,128)S(1)} %log_add_fusion.1) | copy-start | bytes 18436
  390.3 50.3 %copy-start.15 = (f32[12,64,128]{2,1,0:T(8,128)}, f32[12,64,128]{2,1,0:T(8,128)S(1)}, u32[]{:S(2)}) copy-start(f32[12,64,128]{2,1,0:T(8,128)S(1)} %fusion.12) | copy-start | bytes 1179652
  440.4 201.0 %copy-start.68 = (f32[128]{0:T(128)}, f32[128]{0:T(128)S(1)}, u32[]{:S(2)}) copy-start(f32[128]{0:T(128)S(1)} %broadcast_multiply_fusion.2) | copy-start | bytes 1540
  440.6 101.8 %copy-start.93 = (f32[128]{0:T(128)}, f32[128]{0:T(128)S(1)}, u32[]{:S(2)}) copy-start(f32[128]{0:T(128)S(1)} %multiply_reduce_fusion.6) | copy-start | bytes 1540
  440.6 200.8 %copy-start.79 = (f32[128]{0:T(128)}, f32[128]{0:T(128)S(1)}, u32[]{:S(2)}) copy-start(f32[128]{0:T(128)S(1)} %fusion.86) | copy-start | bytes 1540
  496.3 46.1 %copy-start.27 = (bf16[128,768]{1,0:T(8,128)(2,1)}, bf16[128,768]{1,0:T(8,128)(2,1)S(1)}, u32[]{:S(2)}) copy-start(bf16[128,768]{1,0:T(8,128)(2,1)S(1)} %fusion.52) | copy-start | bytes 589828
  547.9 40.3 %copy-start.57 = (f32[12,128]{1,0:T(8,128)}, f32[12,128]{1,0:T(8,128)S(1)}, u32[]{:S(2)}) copy-start(f32[12,128]{1,0:T(8,128)S(1)} %log_add_fusion) | copy-start | bytes 18436
  593.2 50.0 %copy-start.17 = (f32[12,64,128]{2,1,0:T(8,128)}, f32[12,64,128]{2,1,0:T(8,128)S(1)}, u32[]{:S(2)}) copy-start(f32[12,64,128]{2,1,0:T(8,128)S(1)} %fusion.10) | copy-start | bytes 1179652
  715.7 59.9 %copy-start.11 = (bf16[128,3072]{1,0:T(8,128)(2,1)}, bf16[128,3072]{1,0:T(8,128)(2,1)S(1)}, u32[]{:S(2)}) copy-start(bf16[128,3072]{1,0:T(8,128)(2,1)S(1)} %get-tuple-element.410) | copy-start | bytes 2359300
  804.0 147.3 %all-gather.51.cloned.1.call-start = ((), (), s32[]{:S(2)}) async-start(), calls=%async_computation.26 | async-start | bytes 1769472 | tf_op jit(solution)/shard_map/all_gather | solution.py:179
  804.6 182.9 %all-gather.53.cloned.1.call-start = ((), (), s32[]{:S(2)}) async-start(), calls=%async_computation.27 | async-start | bytes 1769472 | tf_op jit(solution)/shard_map/all_gather | solution.py:180
  805.2 275.3 %reduce-scatter.31.cloned.1.call-start = ((), (), s32[]{:S(2)}) async-start(), calls=%async_computation.33 | async-start | bytes 2433024
  818.7 344.0 %reduce-scatter.21.cloned.1.call-start = ((), (), s32[]{:S(2)}) async-start(), calls=%async_computation.28 | async-start | bytes 2433024 | tf_op jit(solution)/shard_map/reduce_scatter | solution.py:430
  821.6 445.0 %reduce-scatter.23.cloned.1.call-start = ((), (), s32[]{:S(2)}) async-start(), calls=%async_computation.29 | async-start | bytes 2433024 | tf_op jit(solution)/shard_map/reduce_scatter | solution.py:385
  824.6 546.7 %reduce-scatter.25.cloned.1.call-start = ((), (), s32[]{:S(2)}) async-start(), calls=%async_computation.30 | async-start | bytes 2433024 | tf_op jit(solution)/shard_map/reduce_scatter | solution.py:388
  827.6 647.6 %reduce-scatter.33.cloned.1.call-start = ((), (), s32[]{:S(2)}) async-start(), calls=%async_computation.34 | async-start | bytes 2433024
  829.1 69.8 %copy-start.52 = (pred[1024,128]{1,0:T(8,128)(4,1)}, pred[1024,128]{1,0:T(8,128)(4,1)S(1)}, u32[]{:S(2)}) copy-start(pred[1024,128]{1,0:T(8,128)(4,1)S(1)} %get-tuple-element.414) | copy-start | bytes 393220
  861.9 37.1 %copy-start.54 = (f32[12,1024]{1,0:T(8,128)}, f32[12,1024]{1,0:T(8,128)S(1)}, u32[]{:S(2)}) copy-start(f32[12,1024]{1,0:T(8,128)S(1)} %all_gather.141) | copy-start | bytes 147460
  909.2 670.7 %reduce-scatter.35.cloned.1.call-start = ((), (), s32[]{:S(2)}) async-start(), calls=%async_computation.35 | async-start | bytes 2433024
  919.4 764.3 %reduce-scatter.37.cloned.1.call-start = ((), (), s32[]{:S(2)}) async-start(), calls=%async_computation.36 | async-start | bytes 2433024
  1000.4 788.0 %reduce-scatter.39.cloned.1.call-start = ((), (), s32[]{:S(2)}) async-start(), calls=%async_computation.37 | async-start | bytes 2433024
  1010.0 919.3 %reduce-scatter.27.cloned.1.call-start = ((), (), s32[]{:S(2)}) async-start(), calls=%async_computation.31 | async-start | bytes 9732096 | tf_op jit(solution)/shard_map/reduce_scatter | solution.py:350
  1016.4 1055.2 %reduce-scatter.29.cloned.1.call-start = ((), (), s32[]{:S(2)}) async-start(), calls=%async_computation.32 | async-start | bytes 9732096 | tf_op jit(solution)/shard_map/reduce_scatter | solution.py:352
  1022.6 53.2 %copy-start.4 = (bf16[768,768]{1,0:T(8,128)(2,1)S(1)}, bf16[768,768]{1,0:T(8,128)(2,1)}, u32[]{:S(2)}) copy-start(bf16[768,768]{1,0:T(8,128)(2,1)} %all-gather.25.cloned.1.call-done) | copy-start | bytes 3538948
  1026.8 50.4 %copy-start.5 = (bf16[768,768]{1,0:T(8,128)(2,1)S(1)}, bf16[768,768]{1,0:T(8,128)(2,1)}, u32[]{:S(2)}) copy-start(bf16[768,768]{1,0:T(8,128)(2,1)} %all-gather.19.cloned.1.call-done) | copy-start | bytes 3538948
  1026.9 50.4 %copy-start.43 = (bf16[12,64,128]{2,1,0:T(8,128)(2,1)S(1)}, bf16[12,64,128]{2,1,0:T(8,128)(2,1)}, u32[]{:S(2)}) copy-start(bf16[12,64,128]{2,1,0:T(8,128)(2,1)} %copy-done.42) | copy-start | bytes 589828
  (81 other events, 222.9 us)
Sparse Core Ops, SparseCore 0:
  11.1 56.8 all-gather.24
  71.0 53.0 all-gather.18
  127.0 53.0 all-gather.36
  182.9 53.0 all-gather.30
  238.7 53.0 all-gather.22
  293.8 43.0 all-gather.26
  339.7 42.9 all-gather.20
  385.6 52.9 all-gather.28
  441.6 53.0 all-gather.34
  496.7 43.0 all-gather.38
  542.6 42.9 all-gather.32
  588.4 52.9 all-gather.40
  644.3 62.5 all-gather.42
  709.6 62.4 all-gather.44
  774.2 42.9 all-gather.46
  819.8 43.4 all-gather.48
  865.3 42.9 all-gather.50
  910.4 43.9 all-gather.52
  960.3 97.6 reduce-scatter.30
  1064.5 98.1 reduce-scatter.20
  1168.5 98.0 reduce-scatter.22
  1273.3 97.9 reduce-scatter.24
  1377.2 97.9 reduce-scatter.32
  1481.8 98.0 reduce-scatter.34
  1585.7 97.9 reduce-scatter.36
  1690.3 98.0 reduce-scatter.38
  1794.8 134.5 reduce-scatter.26
  1936.8 134.7 reduce-scatter.28
where the time goes:
time: 2090 us; the launch traced here: 2080 us
  waiting for transfers between devices  1650 us (79%)
  blocking collectives  202 us (10%)
  matrix products  128 us (6%)
  local copies, waits for them, and re-layouts  64.3 us (3%)
    unnamed x33, waiting for transfers between devices  425 us
    reduce_scatter x1, waiting for transfers between devices, shards(): lax.psum_scatter(grad_outer, ('batch', 'seq'), scatter_dimension=0, tiled...  142 us
    reduce_scatter x1, waiting for transfers between devices, shards(): lax.psum_scatter(grad_inner, ('batch', 'seq'), scatter_dimension=0, tiled...  141 us
    reduce_scatter x1, waiting for transfers between devices, shards(): lax.psum_scatter(grad_cout, ('batch', 'seq'), scatter_dimension=0, tiled=...  105 us
    reduce_scatter x1, waiting for transfers between devices, shards(): lax.psum_scatter(grad_cquery, ('batch', 'seq'), scatter_dimension=0, tile...  104 us
    all_gather x2, waiting for transfers between devices, attend(): lax.all_gather(keys, 'seq', axis=0, tiled=True)  85.9 us
    reduce_scatter x1, waiting for transfers between devices, shards(): lax.psum_scatter(grad_out, ('batch', 'seq'), scatter_dimension=0, tiled=T...  82.2 us
    unnamed x2, blocking collectives  78.7 us
  transfers between devices with their start and end apart: 28, of which 23 were waited for; matrix products, arithmetic and copies ran while one was open for 9% of the time, Pallas kernels for 0%

commit v1 on v0

--- a/solution.py
+++ b/solution.py
@@ -3,11 +3,13 @@
 import jax
 import jax.numpy as jnp
 from jax import lax
+from jax.experimental import pallas as pl
+from jax.experimental.pallas import tpu as pltpu
 from jax.sharding import PartitionSpec as P
 
+BATCH, SEQ = ("batch", "seq")
+BOTH = (BATCH, SEQ)
 HD = 64
-
-
 SCALE = 0.125
 NEGATIVE = -1e30
 EPSILON = 1e-05
@@ -83,8 +85,8 @@
     head_count = queries.shape[1] // HD
     query_heads = heads_of(queries)
     all_keys, all_values = (
-        lax.all_gather(keys, "seq", axis=0, tiled=True),
-        lax.all_gather(values, "seq", axis=0, tiled=True),
+        lax.all_gather(keys, SEQ, axis=0, tiled=True),
+        lax.all_gather(values, SEQ, axis=0, tiled=True),
     )
     block_rows, block_count = spans(all_keys.shape[0])
 
@@ -144,15 +146,15 @@
 def attend_back(queries, keys, values, upstream, logsum, delta, query_ids, key_ids, causal):
     row_count = queries.shape[0]
     head_count = queries.shape[1] // HD
-    own_first = lax.axis_index("seq") * row_count
+    own_first = lax.axis_index(SEQ) * row_count
     own_pos = own_first + jnp.arange(row_count, dtype=jnp.int32)
     query_seg = lax.dynamic_slice_in_dim(query_ids, own_first, row_count, 0)
     key_seg = lax.dynamic_slice_in_dim(key_ids, own_first, row_count, 0)
     query_heads = heads_of(queries)
     upstream_heads = heads_of(upstream)
     empty = jnp.zeros((row_count, head_count, HD), jnp.float32)
-    key_source = lax.all_gather(keys, "seq", axis=0, tiled=True)
-    value_source = lax.all_gather(values, "seq", axis=0, tiled=True)
+    key_source = lax.all_gather(keys, SEQ, axis=0, tiled=True)
+    value_source = lax.all_gather(values, SEQ, axis=0, tiled=True)
     block_rows, block_count = spans(key_source.shape[0])
 
     def key_step(index, running):
@@ -171,13 +173,13 @@
 
     dqueries = lax.fori_loop(0, block_count, key_step, empty)
     all_logsum, all_delta = (
-        lax.all_gather(logsum, "seq", axis=1, tiled=True),
-        lax.all_gather(delta, "seq", axis=1, tiled=True),
+        lax.all_gather(logsum, SEQ, axis=1, tiled=True),
+        lax.all_gather(delta, SEQ, axis=1, tiled=True),
     )
     key_heads = heads_of(keys)
     value_heads = heads_of(values)
-    piece_queries = lax.all_gather(queries, "seq", axis=0, tiled=True)
-    piece_upstream = lax.all_gather(upstream, "seq", axis=0, tiled=True)
+    piece_queries = lax.all_gather(queries, SEQ, axis=0, tiled=True)
+    piece_upstream = lax.all_gather(upstream, SEQ, axis=0, tiled=True)
     query_block_rows, block_count = spans(piece_queries.shape[0])
 
     def query_step(index, running):
@@ -245,7 +247,7 @@
     target_ids = target_segments[0]
     source_ids = memory_segments[0]
     row_count = inputs.shape[0]
-    own_first = lax.axis_index("seq") * row_count
+    own_first = lax.axis_index(SEQ) * row_count
     own_pos = own_first + jnp.arange(row_count, dtype=jnp.int32)
     query_seg = lax.dynamic_slice_in_dim(target_ids, own_first, row_count, 0)
     (
@@ -259,15 +261,15 @@
         sgain_full,
         sshift_full,
     ) = (
-        lax.all_gather(selfquery, ("batch", "seq"), axis=0, tiled=True),
-        lax.all_gather(selfkey, ("batch", "seq"), axis=0, tiled=True),
-        lax.all_gather(selfvalue, ("batch", "seq"), axis=0, tiled=True),
-        lax.all_gather(selfout, ("batch", "seq"), axis=0, tiled=True),
-        lax.all_gather(selfqbias, ("batch", "seq"), axis=0, tiled=True),
-        lax.all_gather(selfvbias, ("batch", "seq"), axis=0, tiled=True),
-        lax.all_gather(selfobias, ("batch", "seq"), axis=0, tiled=True),
-        lax.all_gather(selfgain, ("batch", "seq"), axis=0, tiled=True),
-        lax.all_gather(selfshift, ("batch", "seq"), axis=0, tiled=True),
+        lax.all_gather(selfquery, BOTH, axis=0, tiled=True),
+        lax.all_gather(selfkey, BOTH, axis=0, tiled=True),
+        lax.all_gather(selfvalue, BOTH, axis=0, tiled=True),
+        lax.all_gather(selfout, BOTH, axis=0, tiled=True),
+        lax.all_gather(selfqbias, BOTH, axis=0, tiled=True),
+        lax.all_gather(selfvbias, BOTH, axis=0, tiled=True),
+        lax.all_gather(selfobias, BOTH, axis=0, tiled=True),
+        lax.all_gather(selfgain, BOTH, axis=0, tiled=True),
+        lax.all_gather(selfshift, BOTH, axis=0, tiled=True),
     )
     sgain = sgain_full.astype(jnp.float32)
     sshift = sshift_full.astype(jnp.float32)
@@ -294,15 +296,15 @@
         cgain_full,
         cshift_full,
     ) = (
-        lax.all_gather(crossquery, ("batch", "seq"), axis=0, tiled=True),
-        lax.all_gather(crosskey, ("batch", "seq"), axis=0, tiled=True),
-        lax.all_gather(crossvalue, ("batch", "seq"), axis=0, tiled=True),
-        lax.all_gather(crossout, ("batch", "seq"), axis=0, tiled=True),
-        lax.all_gather(crossqbias, ("batch", "seq"), axis=0, tiled=True),
-        lax.all_gather(crossvbias, ("batch", "seq"), axis=0, tiled=True),
-        lax.all_gather(crossobias, ("batch", "seq"), axis=0, tiled=True),
-        lax.all_gather(crossgain, ("batch", "seq"), axis=0, tiled=True),
-        lax.all_gather(crossshift, ("batch", "seq"), axis=0, tiled=True),
+        lax.all_gather(crossquery, BOTH, axis=0, tiled=True),
+        lax.all_gather(crosskey, BOTH, axis=0, tiled=True),
+        lax.all_gather(crossvalue, BOTH, axis=0, tiled=True),
+        lax.all_gather(crossout, BOTH, axis=0, tiled=True),
+        lax.all_gather(crossqbias, BOTH, axis=0, tiled=True),
+        lax.all_gather(crossvbias, BOTH, axis=0, tiled=True),
+        lax.all_gather(crossobias, BOTH, axis=0, tiled=True),
+        lax.all_gather(crossgain, BOTH, axis=0, tiled=True),
+        lax.all_gather(crossshift, BOTH, axis=0, tiled=True),
     )
     cgain = cgain_full.astype(jnp.float32)
     cshift = cshift_full.astype(jnp.float32)
@@ -321,12 +323,12 @@
     second = normalize(hidden_two, cgain, cshift)
     second_low = second.astype(jnp.bfloat16)
     inner_full, ibias_full, outer_full, obias_feed, fgain_full, fshift_full = (
-        lax.all_gather(innerweight, ("batch", "seq"), axis=0, tiled=True),
-        lax.all_gather(innerbias, ("batch", "seq"), axis=0, tiled=True),
-        lax.all_gather(outerweight, ("batch", "seq"), axis=0, tiled=True),
-        lax.all_gather(outerbias, ("batch", "seq"), axis=0, tiled=True),
-        lax.all_gather(finalgain, ("batch", "seq"), axis=0, tiled=True),
-        lax.all_gather(finalshift, ("batch", "seq"), axis=0, tiled=True),
+        lax.all_gather(innerweight, BOTH, axis=0, tiled=True),
+        lax.all_gather(innerbias, BOTH, axis=0, tiled=True),
+        lax.all_gather(outerweight, BOTH, axis=0, tiled=True),
+        lax.all_gather(outerbias, BOTH, axis=0, tiled=True),
+        lax.all_gather(finalgain, BOTH, axis=0, tiled=True),
+        lax.all_gather(finalshift, BOTH, axis=0, tiled=True),
     )
     fgain = fgain_full.astype(jnp.float32)
     fshift = fshift_full.astype(jnp.float32)
@@ -347,12 +349,12 @@
     grad_ibias = row_total(inner_grad)
     grad_second = grad_hidden3 + right_product(inner_grad, inner_full)
     feed_grads = (
-        lax.psum_scatter(grad_inner, ("batch", "seq"), scatter_dimension=0, tiled=True),
-        lax.psum_scatter(grad_ibias, ("batch", "seq"), scatter_dimension=0, tiled=True),
-        lax.psum_scatter(grad_outer, ("batch", "seq"), scatter_dimension=0, tiled=True),
-        lax.psum_scatter(grad_obias_feed, ("batch", "seq"), scatter_dimension=0, tiled=True),
-        lax.psum_scatter(grad_fgain, ("batch", "seq"), scatter_dimension=0, tiled=True),
-        lax.psum_scatter(grad_fshift, ("batch", "seq"), scatter_dimension=0, tiled=True),
+        lax.psum_scatter(grad_inner, BOTH, scatter_dimension=0, tiled=True),
+        lax.psum_scatter(grad_ibias, BOTH, scatter_dimension=0, tiled=True),
+        lax.psum_scatter(grad_outer, BOTH, scatter_dimension=0, tiled=True),
+        lax.psum_scatter(grad_obias_feed, BOTH, scatter_dimension=0, tiled=True),
+        lax.psum_scatter(grad_fgain, BOTH, scatter_dimension=0, tiled=True),
+        lax.psum_scatter(grad_fshift, BOTH, scatter_dimension=0, tiled=True),
     )
     grad_hidden2, grad_cgain, grad_cshift = norm_back(hidden_two, cgain, cshift, grad_second)
     cross_branch = grad_hidden2.astype(jnp.bfloat16)
@@ -382,15 +384,15 @@
     memory_grad = right_product(ck_low, ckey_full) + right_product(cv_low, cvalue_full)
     grad_first = grad_hidden2 + right_product(cq_low, cquery_full)
     cross_grads = (
-        lax.psum_scatter(grad_cquery, ("batch", "seq"), scatter_dimension=0, tiled=True),
-        lax.psum_scatter(grad_ckey, ("batch", "seq"), scatter_dimension=0, tiled=True),
-        lax.psum_scatter(grad_cvalue, ("batch", "seq"), scatter_dimension=0, tiled=True),
-        lax.psum_scatter(grad_cout, ("batch", "seq"), scatter_dimension=0, tiled=True),
-        lax.psum_scatter(grad_cqbias, ("batch", "seq"), scatter_dimension=0, tiled=True),
-        lax.psum_scatter(grad_cvbias, ("batch", "seq"), scatter_dimension=0, tiled=True),
-        lax.psum_scatter(grad_cobias, ("batch", "seq"), scatter_dimension=0, tiled=True),
-        lax.psum_scatter(grad_cgain, ("batch", "seq"), scatter_dimension=0, tiled=True),
-        lax.psum_scatter(grad_cshift, ("batch", "seq"), scatter_dimension=0, tiled=True),
+        lax.psum_scatter(grad_cquery, BOTH, scatter_dimension=0, tiled=True),
+        lax.psum_scatter(grad_ckey, BOTH, scatter_dimension=0, tiled=True),
+        lax.psum_scatter(grad_cvalue, BOTH, scatter_dimension=0, tiled=True),
+        lax.psum_scatter(grad_cout, BOTH, scatter_dimension=0, tiled=True),
+        lax.psum_scatter(grad_cqbias, BOTH, scatter_dimension=0, tiled=True),
+        lax.psum_scatter(grad_cvbias, BOTH, scatter_dimension=0, tiled=True),
+        lax.psum_scatter(grad_cobias, BOTH, scatter_dimension=0, tiled=True),
+        lax.psum_scatter(grad_cgain, BOTH, scatter_dimension=0, tiled=True),
+        lax.psum_scatter(grad_cshift, BOTH, scatter_dimension=0, tiled=True),
     )
     grad_hidden1, grad_sgain, grad_sshift = norm_back(hidden_one, sgain, sshift, grad_first)
     self_branch = grad_hidden1.astype(jnp.bfloat16)
@@ -424,15 +426,15 @@
         + right_product(sv_low, value_full)
     )
     self_grads = (
-        lax.psum_scatter(grad_query, ("batch", "seq"), scatter_dimension=0, tiled=True),
-        lax.psum_scatter(grad_key, ("batch", "seq"), scatter_dimension=0, tiled=True),
-        lax.psum_scatter(grad_value, ("batch", "seq"), scatter_dimension=0, tiled=True),
-        lax.psum_scatter(grad_out, ("batch", "seq"), scatter_dimension=0, tiled=True),
-        lax.psum_scatter(grad_qbias, ("batch", "seq"), scatter_dimension=0, tiled=True),
-        lax.psum_scatter(grad_vbias, ("batch", "seq"), scatter_dimension=0, tiled=True),
-        lax.psum_scatter(grad_obias, ("batch", "seq"), scatter_dimension=0, tiled=True),
-        lax.psum_scatter(grad_sgain, ("batch", "seq"), scatter_dimension=0, tiled=True),
-        lax.psum_scatter(grad_sshift, ("batch", "seq"), scatter_dimension=0, tiled=True),
+        lax.psum_scatter(grad_query, BOTH, scatter_dimension=0, tiled=True),
+        lax.psum_scatter(grad_key, BOTH, scatter_dimension=0, tiled=True),
+        lax.psum_scatter(grad_value, BOTH, scatter_dimension=0, tiled=True),
+        lax.psum_scatter(grad_out, BOTH, scatter_dimension=0, tiled=True),
+        lax.psum_scatter(grad_qbias, BOTH, scatter_dimension=0, tiled=True),
+        lax.psum_scatter(grad_vbias, BOTH, scatter_dimension=0, tiled=True),
+        lax.psum_scatter(grad_obias, BOTH, scatter_dimension=0, tiled=True),
+        lax.psum_scatter(grad_sgain, BOTH, scatter_dimension=0, tiled=True),
+        lax.psum_scatter(grad_sshift, BOTH, scatter_dimension=0, tiled=True),
     )
     return (
         (output[None], tokens_grad[None], memory_grad[None])
@@ -442,65 +444,967 @@
     )
 
 
+LOW = jnp.bfloat16
+WIDE = jnp.float32
+MESH = pl.DeviceIdType.MESH
+VMEM_BYTES = 64 << 20
+ALL2 = pl.ds(0, 2)
+ALL4 = pl.ds(0, 4)
+
+
+def place():
+    b, s = lax.axis_index(BATCH), lax.axis_index(SEQ)
+    return (lax.div(b, 2), lax.rem(b, 2), lax.rem(s, 2), lax.div(s, 2))
+
+
+def device(x, c, y, z):
+    return (2 * x + c, 2 * z + y)
+
+
+class Peers:
+    def __init__(self):
+        self.x, self.c, self.y, self.z = place()
+        x, c, y, z = self.x, self.c, self.y, self.z
+        b, s = lax.axis_index(BATCH), lax.axis_index(SEQ)
+        self.across_x = device(1 - x, c, y, z)
+        self.across_y = device(x, c, 1 - y, z)
+        self.sibling = device(x, 1 - c, y, z)
+        self.along_z = [device(x, c, y, lax.rem(z + k, 4)) for k in (1, 2, 3)]
+        self.after = (b, lax.rem(s + 1, 8))
+        self.before = (b, lax.rem(s + 7, 8))
+        self.mirror = (b, 7 - s)
+
+    def all(self):
+        return [
+            self.across_x, self.across_y, self.sibling, *self.along_z, self.after, self.before, self.mirror,
+        ]
+
+    def meet(self):
+        barrier = pltpu.get_barrier_semaphore()
+        for peer in self.all():
+            pl.semaphore_signal(barrier, inc=1, device_id=peer, device_id_type=MESH)
+        pl.semaphore_wait(barrier, len(self.all()))
+
+
+class Wires:
+    def __init__(self, send, recv):
+        self.send, self.recv, self.used = send, recv, 0
+
+    def copies(self, pairs, target):
+        made = []
+        for source, landing in pairs:
+            made.append(
+                pltpu.make_async_remote_copy(
+                    src_ref=source,
+                    dst_ref=landing,
+                    send_sem=self.send.at[self.used],
+                    recv_sem=self.recv.at[self.used],
+                    device_id=target,
+                    device_id_type=MESH,
+                )
+            )
+            self.used += 1
+        return made
+
+
+def start(copies):
+    for copy in copies:
+        copy.start()
+
+
+def landed(copies):
+    for copy in copies:
+        copy.wait_recv()
+
+
+def sent(copies):
+    for copy in copies:
+        copy.wait_send()
+
+
+class Gather:
+    def __init__(self, peers, wires, mats, rests, outer, vectors):
+        self.peers, self.wires = peers, wires
+        self.mats, self.rests, self.outer, self.vectors = mats, rests, outer, vectors
+        self.steps = [{} for _ in range(8)]
+        self.done = []
+
+    def parts(self, unit, x, c, z, y):
+        both = y is None
+        if unit >= 6:
+            rows = pl.ds(48 * (unit - 6), 48)
+            return [self.outer.at[x, c, z, ALL2 if both else y, rows]]
+        mats = pl.ds(2 * unit, 2)
+        if both:
+            refs = [self.mats.at[mats, x, c, z, pl.ds(0, 16)], self.mats.at[mats, x, c, z, pl.ds(32, 16)]]
+        else:
+            refs = [self.mats.at[mats, x, c, z, pl.ds(pl.multiple_of(32 * y, 16), 16)]]
+        refs.append(self.rests.at[unit, x, c, z, ALL2 if both else y])
+        if unit == 0:
+            refs.append(self.vectors.at[x, c, z, ALL2 if both else y])
+        return refs
+
+    def send(self, unit, name, spot, target):
+        pairs = [(part, part) for part in self.parts(unit, *spot)]
+        copies = self.wires.copies(pairs, target)
+        start(copies)
+        self.steps[unit][name] = copies
+        self.done += copies
+
+    def z_start(self, unit):
+        p = self.peers
+        for k, peer in enumerate(p.along_z):
+            self.send(unit, ("z", k), (p.x, p.c, p.z, p.y), peer)
+
+    def first(self, unit):
+        p = self.peers
+        for k in range(3):
+            landed(self.steps[unit]["z", k])
+        self.send(unit, "first", (p.x, p.c, ALL4, p.y), p.across_y if unit % 2 else p.across_x)
+
+    def second(self, unit):
+        p = self.peers
+        landed(self.steps[unit]["first"])
+        if unit % 2:
+            self.send(unit, "second", (p.x, p.c, ALL4, None), p.across_x)
+            self.send(unit, "near", (p.x, p.c, ALL4, None), p.sibling)
+        else:
+            self.send(unit, "second", (ALL2, p.c, ALL4, p.y), p.across_y)
+            self.send(unit, "near", (ALL2, p.c, ALL4, p.y), p.sibling)
+
+    def third(self, unit):
+        p = self.peers
+        landed(self.steps[unit]["second"])
+        if unit % 2:
+            self.send(unit, "far", (1 - p.x, p.c, ALL4, None), p.sibling)
+        else:
+            self.send(unit, "far", (ALL2, p.c, ALL4, 1 - p.y), p.sibling)
+
+    def last(self, unit):
+        landed(self.steps[unit]["near"])
+        landed(self.steps[unit]["far"])
+
+
+def gather_pack(y, x, c, z, squares, inner, outer, small, mats, rests, whole_outer, vectors):
+    def split(values):
+        values = values.astype(WIDE)
+        body = jnp.where(y == 0, values[0:16], values[8:24])
+        rest = jnp.where(y == 0, values[16:24], values[0:8])
+        return (body.astype(LOW), rest)
+
+    for unit in range(6):
+        rests_of = []
+        for k in range(2):
+            m = 2 * unit + k
+            values = squares[m][...] if m < 8 else inner[:, 768 * (m - 8) : 768 * (m - 7)]
+            body, rest = split(values)
+            mats[m, x, c, z, pl.ds(pl.multiple_of(32 * y, 16), 16), :] = body
+            rests_of.append(rest)
+        rests[unit, x, c, z, y] = jnp.concatenate(rests_of, axis=0).astype(LOW)
+    whole_outer[x, c, z, y] = outer[...]
+    index = (2 * x + c) * 8 + 2 * z + y
+    wide = small[...].astype(WIDE)
+    row = lax.broadcasted_iota(jnp.int32, (16, 128), 0)
+    by24 = pltpu.roll(wide, lax.rem(24 * index, 128), 1)
+    by96 = pltpu.roll(wide, lax.rem(96 * index, 128), 1)
+    vectors[x, c, z, y] = jnp.where(row == 13, by96, by24).astype(LOW)
+
+
+def merge_rests(unit, mats, rests):
+    def one(step, carry):
+        x, c, z = lax.div(step, 8), lax.rem(lax.div(step, 4), 2), lax.rem(step, 4)
+        low_half = rests[unit, x, c, z, 0].astype(WIDE)
+        high_half = rests[unit, x, c, z, 1].astype(WIDE)
+        mats[2 * unit, x, c, z, 16:32, :] = jnp.concatenate(
+            [low_half[0:8], high_half[0:8]], axis=0
+        ).astype(LOW)
+        mats[2 * unit + 1, x, c, z, 16:32, :] = jnp.concatenate(
+            [low_half[8:16], high_half[8:16]], axis=0
+        ).astype(LOW)
+        return carry
+
+    lax.fori_loop(0, 16, one, 0)
+
+
+def gather_kernel(*refs):
+    squares, refs = refs[:8], refs[8:]
+    inner, outer, small, tokens, memory = refs[:5]
+    mats, whole_outer, vectors, tokens_two, memory_three = refs[5:10]
+    rests, send, recv = refs[10:]
+    peers = Peers()
+    x, c, y, z = peers.x, peers.c, peers.y, peers.z
+    gather_pack(y, x, c, z, squares, inner, outer, small, mats, rests, whole_outer, vectors)
+    tokens_two[128:256, :] = tokens[...]
+    peers.meet()
+    wires = Wires(send, recv)
+    weights = Gather(peers, wires, mats, rests, whole_outer, vectors)
+    weights.z_start(0)
+    weights.z_start(1)
+    left = wires.copies([(tokens, tokens_two.at[pl.ds(0, 128)])], peers.after)
+    mirrored = wires.copies([(memory, memory_three.at[1])], peers.mirror)
+    start(left)
+    start(mirrored)
+    weights.z_start(2)
+    weights.z_start(3)
+    spread = []
+    for pair in range(6):
+        if pair < 4:
+            for unit in (2 * pair, 2 * pair + 1):
+                weights.first(unit)
+            if pair + 2 < 4:
+                weights.z_start(2 * pair + 4)
+                weights.z_start(2 * pair + 5)
+        if 1 <= pair < 5:
+            for unit in (2 * pair - 2, 2 * pair - 1):
+                weights.second(unit)
+        if pair == 1:
+            landed(mirrored)
+            spread = wires.copies([(memory_three.at[1], memory_three.at[2])], peers.after)
+            spread += wires.copies([(memory_three.at[1], memory_three.at[0])], peers.before)
+            start(spread)
+        if pair >= 2:
+            for unit in (2 * pair - 4, 2 * pair - 3):
+                weights.third(unit)
+    for unit in range(8):
+        weights.last(unit)
+        if unit < 6:
+            merge_rests(unit, mats, rests)
+    landed(left)
+    landed(spread)
+    sent(weights.done + left + mirrored + spread)
+
+
+def vmem():
+    return pl.BlockSpec(memory_space=pltpu.VMEM)
+
+
+def gather_call(squares, inner, outer, small, tokens, memory):
+    shapes = [
+        jax.ShapeDtypeStruct((12, 2, 2, 4, 48, 768), LOW),
+        jax.ShapeDtypeStruct((2, 2, 4, 2, 96, 768), LOW),
+        jax.ShapeDtypeStruct((2, 2, 4, 2, 16, 128), LOW),
+        jax.ShapeDtypeStruct((256, 768), LOW),
+        jax.ShapeDtypeStruct((3, 128, 768), LOW),
+    ]
+    return pl.pallas_call(
+        gather_kernel,
+        out_shape=shapes,
+        in_specs=[vmem()] * 13,
+        out_specs=[vmem()] * 5,
+        scratch_shapes=[
+            pltpu.VMEM((6, 2, 2, 4, 2, 16, 768), LOW),
+            pltpu.SemaphoreType.DMA((160,)),
+            pltpu.SemaphoreType.DMA((160,)),
+        ],
+        compiler_params=pltpu.CompilerParams(
+            collective_id=0, has_side_effects=True, vmem_limit_bytes=VMEM_BYTES
+        ),
+    )(*squares, inner, outer, small, tokens, memory)
+
+
+def dot(left, right):
+    return jnp.dot(left, right, preferred_element_type=WIDE)
+
+
+def dot_nt(left, right):
+    return lax.dot_general(left, right, (((1,), (1,)), ((), ())), preferred_element_type=WIDE)
+
+
+def dot_tn(left, right):
+    return lax.dot_general(left, right, (((0,), (0,)), ((), ())), preferred_element_type=WIDE)
+
+
+def strip(n):
+    return slice(256 * n, 256 * n + 256)
+
+
+def columns(mats, m, n):
+    return mats[m, :, :, :, :, strip(n)].reshape(768, 256)
+
+
+def rows(mats, m, x):
+    return mats[m, x].reshape(384, 768)
+
+
+def outer_columns(outer, j, n):
+    return outer[j // 2, j % 2, :, :, :, strip(n)].reshape(768, 256)
+
+
+def outer_rows(outer, j, half):
+    return outer[j // 2, j % 2, 2 * half : 2 * half + 2].reshape(384, 768)
+
+
+def unpack_vectors(vectors, vec, inner_bias):
+    lane = lax.broadcasted_iota(jnp.int32, (16, 128), 1)
+
+    def shard(d):
+        b, s = d // 8, d % 8
+        return vectors[b // 2, b % 2, s // 2, s % 2].astype(WIDE)
+
+    for width, tiles, ref in ((24, 6, vec), (96, 24, inner_bias)):
+        for t in range(tiles):
+            first = (128 * t) // width
+            final = (128 * t + 127) // width
+            total = shard(first)
+            for d in range(first + 1, final + 1):
+                total = jnp.where(lane >= width * d - 128 * t, shard(d), total)
+            if width == 24:
+                ref[:, 128 * t : 128 * t + 128] = total
+            else:
+                ref[0:1, 128 * t : 128 * t + 128] = total[13:14]
+
+
+def pack_vectors(vec, inner_bias, c, place_at):
+    lane = lax.broadcasted_iota(jnp.int32, (16, 128), 1)
+    row = lax.broadcasted_iota(jnp.int32, (16, 128), 0)
+
+    def shard(ref, width, d):
+        t, offset = width * d // 128, width * d % 128
+        block = ref[:, 128 * t : 128 * t + 128]
+        if offset + width > 128:
+            block = jnp.where(lane >= offset, block, ref[:, 128 * t + 128 : 128 * t + 256])
+        return block
+
+    for d in range(32):
+        b, s = d // 8, d % 8
+        block = shard(vec, 24, d)
+        t, offset = 96 * d // 128, 96 * d % 128
+        bias = inner_bias[0:1, 128 * t : 128 * t + 128]
+        if offset + 96 > 128:
+            bias = jnp.where(lane[0:1] >= offset, bias, inner_bias[0:1, 128 * t + 128 : 128 * t + 256])
+        place_at(b % 2, b // 2, s // 2, s % 2, jnp.where(row == 13, jnp.broadcast_to(bias, (16, 128)), block))
+
+
+def centered(values):
+    center = values - jnp.mean(values, axis=-1, keepdims=True)
+    scale = lax.rsqrt(jnp.mean(center * center, axis=-1, keepdims=True) + EPSILON)
+    return (center * scale, scale)
+
+
+def norm_grad(unit_values, scale, gain, grad):
+    scaled = grad * gain
+    mean = jnp.mean(scaled, axis=-1, keepdims=True)
+    along = jnp.mean(scaled * unit_values, axis=-1, keepdims=True)
+    return (scaled - mean - unit_values * along) * scale
+
+
+def total_rows(values):
+    return jnp.sum(values.astype(WIDE), axis=0, keepdims=True)
+
+
+def lane_halves():
+    lane = lax.broadcasted_iota(jnp.int32, (128, 128), 1)
+    low_half = jnp.where(lane < 64, 1.0, 0.0).astype(LOW)
+    high_half = jnp.where(lane < 64, 0.0, 1.0).astype(LOW)
+    return (lane < 64, low_half, high_half)
+
+
+def pair_rows(block, low_half, high_half):
+    return jnp.concatenate([block * low_half, block * high_half], axis=0)
+
+
+def attention(queries, keys, values, mask, probs, context):
+    pick, low_half, high_half = lane_halves()
+
+    def heads(h, carry):
+        here = pl.ds(pl.multiple_of(128 * h, 128), 128)
+        both = pair_rows(queries[:, here], low_half, high_half)
+        bias = mask[...]
+        scores = dot_nt(both, keys[:, here]) * SCALE + jnp.concatenate([bias, bias], axis=0)
+        weights = jnp.exp(scores - jnp.max(scores, axis=1, keepdims=True))
+        weights = weights * (1.0 / jnp.sum(weights, axis=1, keepdims=True))
+        rounded = weights.astype(LOW)
+        probs[h] = rounded
+        mixed = dot(rounded, values[:, here])
+        context[:, here] = jnp.where(pick, mixed[:128], mixed[128:]).astype(LOW)
+        return carry
+
+    lax.fori_loop(0, 6, heads, 0)
+
+
+def attention_back(queries, keys, values, upstream, probs, dqueries, dkeys, dvalues, count):
+    pick, low_half, high_half = lane_halves()
+
+    def heads(h, carry):
+        here = pl.ds(pl.multiple_of(128 * h, 128), 128)
+        both = pair_rows(queries[:, here], low_half, high_half)
+        both_up = pair_rows(upstream[:, here], low_half, high_half)
+        dprobs = dot_nt(both_up, values[:, here])
+        weights = probs[h].astype(WIDE)
+        delta = jnp.sum(weights * dprobs, axis=1, keepdims=True)
+        dscores = (weights * (dprobs - delta) * SCALE).astype(LOW)
+        mixed = dot(dscores, keys[:, here])
+        dqueries[:, here] = jnp.where(pick, mixed[:128], mixed[128:]).astype(LOW)
+        dkeys[0:count, here] = dot_tn(dscores, both).astype(LOW)
+        dvalues[0:count, here] = dot_tn(probs[h], both_up).astype(LOW)
+        return carry
+
+    lax.fori_loop(0, 6, heads, 0)
+
+
+class Grads:
+    ORDER = (6, 7, 4, 5, 2, 3, 0, 1)
+
+    def __init__(self, peers, wires, held, r0, r1_even, r1_odd, r2, out, mine, credit):
+        self.peers, self.wires, self.held = peers, wires, held
+        self.r0, self.r1_even, self.r1_odd, self.r2, self.out = r0, r1_even, r1_odd, r2, out
+        self.mine, self.credit = mine, credit
+        self.stage = {}
+        self.open = []
+        self.first_sends = {}
+
+    def at(self, unit):
+        return self.ORDER.index(unit)
+
+    def slot(self, unit, c):
+        return jnp.where(c == self.peers.c, unit, 8 + self.at(unit) % 4)
+
+    def ready(self, unit):
+        turn = self.at(unit)
+        if turn >= 4:
+            sent(self.first_sends.pop(self.ORDER[turn - 4]))
+
+    def ship(self, pairs, target):
+        copies = self.wires.copies(pairs, target)
+        start(copies)
+        self.open += copies
+        return copies
+
+    def step0(self, unit):
+        turn = self.at(unit)
+        if turn >= 4:
+            pl.semaphore_wait(self.credit, 1)
+        ring = turn % 4
+        copies = self.wires.copies([(self.held.at[8 + ring], self.r0.at[ring])], self.peers.sibling)
+        start(copies)
+        self.first_sends[unit] = copies
+        self.stage[unit] = copies
+
+    def step1(self, unit):
+        p, held = self.peers, self.held
+        landed(self.stage[unit])
+        turn = self.at(unit)
+        ring = turn % 4
+
+        def add(i, carry):
+            j, k = lax.div(i, 4), lax.rem(i, 4)
+            held[unit, j, k] = held[unit, j, k] + self.r0[ring, j, k]
+            return carry
+
+        lax.fori_loop(0, 8, add, 0)
+        if turn < 4:
+            pl.semaphore_signal(self.credit, inc=1, device_id=p.sibling, device_id_type=MESH)
+        if unit % 2:
+            pairs = [(held.at[unit, 1 - p.x], self.r1_odd.at[unit // 2])]
+            self.stage[unit] = self.ship(pairs, p.across_x)
+        else:
+            pairs = [(held.at[unit, ALL2, ALL4, 1 - p.y], self.r1_even.at[unit // 2])]
+            self.stage[unit] = self.ship(pairs, p.across_y)
+
+    def step2(self, unit):
+        p, held = self.peers, self.held
+        landed(self.stage[unit])
+
+        def add(i, carry):
+            if unit % 2:
+                held[unit, p.x, i] = held[unit, p.x, i] + self.r1_odd[unit // 2, i]
+            else:
+                for j in range(2):
+                    held[unit, j, i, p.y] = held[unit, j, i, p.y] + self.r1_even[unit // 2, j, i]
+            return carry
+
+        lax.fori_loop(0, 4, add, 0)
+        if unit % 2:
+            pairs = [(held.at[unit, p.x, ALL4, 1 - p.y], self.r2.at[unit])]
+            self.stage[unit] = self.ship(pairs, p.across_y)
+        else:
+            pairs = [(held.at[unit, 1 - p.x, ALL4, p.y], self.r2.at[unit])]
+            self.stage[unit] = self.ship(pairs, p.across_x)
+
+    def step3(self, unit):
+        p, held = self.peers, self.held
+        landed(self.stage[unit])
+
+        def add(i, carry):
+            held[unit, p.x, i, p.y] = held[unit, p.x, i, p.y] + self.r2[unit, i]
+            return carry
+
+        lax.fori_loop(0, 4, add, 0)
+        copies = []
+        for k in (1, 2, 3):
+            source = held.at[unit, p.x, lax.rem(p.z + k, 4), p.y]
+            copies += self.ship([(source, self.out.at[unit, k - 1])], p.along_z[k - 1])
+        self.stage[unit] = copies
+        self.mine[unit] = held[unit, p.x, p.z, p.y]
+
+    def finish(self):
+        for unit in self.ORDER:
+            landed(self.stage[unit])
+        for copies in self.first_sends.values():
+            sent(copies)
+        sent(self.open)
+
+    def pair_grad(self, unit, first_left, first_right, second_left, second_right):
+        self.ready(unit)
+        for x in range(2):
+            here = slice(384 * x, 384 * x + 384)
+            one_left = jnp.transpose(first_left[:, here])
+            two_left = jnp.transpose(second_left[:, here])
+            for n in range(3):
+                s = strip(n)
+                one = dot(one_left, first_right[:, s])
+                two = dot(two_left, second_right[:, s])
+                for c in range(2):
+                    slot = self.slot(unit, c)
+                    for z in range(4):
+                        for y in range(2):
+                            base = 24 * (8 * c + 2 * z + y)
+                            body = base + 8 * y
+                            rest = base + 16 * (1 - y)
+                            self.held[slot, x, z, y, 0:16, s] = one[body : body + 16].astype(LOW)
+                            self.held[slot, x, z, y, 16:32, s] = two[body : body + 16].astype(LOW)
+                            self.held[slot, x, z, y, 32:48, s] = jnp.concatenate(
+                                [one[rest : rest + 8], two[rest : rest + 8]], axis=0
+                            ).astype(LOW)
+
+    def outer_grad(self, hidden, upstream):
+        for j in range(4):
+            x, c = j // 2, j % 2
+            for half in range(2):
+                here = slice(768 * j + 384 * half, 768 * j + 384 * half + 384)
+                left = jnp.transpose(hidden[:, here])
+                for n in range(3):
+                    s = strip(n)
+                    one = dot(left, upstream[:, s])
+                    for unit in (6, 7):
+                        slot = self.slot(unit, c)
+                        for k in range(4):
+                            base = 96 * k + 48 * (unit - 6)
+                            z, y = 2 * half + k // 2, k % 2
+                            self.held[slot, x, z, y, :, s] = one[base : base + 48].astype(LOW)
+
+
+def layer_kernel(*refs):
+    mats, outer, vectors, tokens, memory, cotangent, mask_self, mask_cross = refs[:8]
+    output, out, mine, vout, left_out, memory_out, tokens_part = refs[8:15]
+    scratch = refs[15:]
+    (
+        vec, inner_bias, query, key, value, probs, context, unit1, first_low,
+        query2, key2, value2, probs2, context2, unit2, second_low,
+        hidden, slope, total, grad, branch, upstream, dquery, dkey, dvalue,
+        gvec, ginner,
+        held, r0, r1_even, r1_odd, r2, vheld, v0, v1, v2, left_part, memory_parts,
+        from_after, from_before, sum_up, credit, send, recv,
+    ) = scratch
+    peers = Peers()
+    peers.meet()
+    wires = Wires(send, recv)
+    grads = Grads(peers, wires, held, r0, r1_even, r1_odd, r2, out, mine, credit)
+    own = slice(128, 256)
+
+    unpack_vectors(vectors, vec, inner_bias)
+
+    def vector(j):
+        return vec[j : j + 1, :]
+
+    for n in range(3):
+        s = strip(n)
+        query[:, s] = (dot(tokens[own, :], columns(mats, 0, n)) + vec[0:1, s]).astype(LOW)
+        key[:, s] = dot(tokens[...], columns(mats, 1, n)).astype(LOW)
+        value[:, s] = (dot(tokens[...], columns(mats, 2, n)) + vec[1:2, s]).astype(LOW)
+    attention(query, key, value, mask_self, probs, context)
+    for n in range(3):
+        s = strip(n)
+        total[:, s] = (
+            tokens[own, s].astype(WIDE) + dot(context[...], columns(mats, 3, n)) + vec[2:3, s]
+        )
+    unit, scale1 = centered(total[...])
+    unit1[...] = unit
+    first = unit * vector(3) + vector(4)
+    total[...] = first
+    first_low[...] = first.astype(LOW)
+    for n in range(3):
+        s = strip(n)
+        query2[:, s] = (dot(first_low[...], columns(mats, 4, n)) + vec[5:6, s]).astype(LOW)
+        key2[:, s] = dot(memory[...], columns(mats, 5, n)).astype(LOW)
+        value2[:, s] = (dot(memory[...], columns(mats, 6, n)) + vec[6:7, s]).astype(LOW)
+    attention(query2, key2, value2, mask_cross, probs2, context2)
+    for n in range(3):
+        s = strip(n)
+        total[:, s] = total[:, s] + dot(context2[...], columns(mats, 7, n)) + vec[7:8, s]
+    unit, scale2 = centered(total[...])
+    unit2[...] = unit
+    second = unit * vector(8) + vector(9)
+    total[...] = second + vector(10)
+    second_low[...] = second.astype(LOW)
+    for j in range(4):
+        for n in range(3):
+            s = slice(768 * j + 256 * n, 768 * j + 256 * n + 256)
+            pre = dot(second_low[...], columns(mats, 8 + j, n)) + inner_bias[0:1, s]
+            normal = 0.5 + 0.5 * lax.erf(pre * 0.7071067811865476)
+            hidden[:, s] = (pre * normal).astype(LOW)
+            slope[:, s] = (
+                normal + pre * (0.3989422804014327 * jnp.exp(-0.5 * pre * pre))
+            ).astype(LOW)
+        for n in range(3):
+            s = strip(n)
+            total[:, s] = total[:, s] + dot(
+                hidden[:, 768 * j : 768 * j + 768], outer_columns(outer, j, n)
+            )
+    unit, scale3 = centered(total[...])
+    output[...] = (unit * vector(11) + vector(12)).astype(LOW)
+    arrived = cotangent[...].astype(WIDE)
+    gvec[11:12, :] = total_rows(arrived * unit)
+    gvec[12:13, :] = total_rows(arrived)
+    dhidden = norm_grad(unit, scale3, vector(11), arrived)
+    grad[...] = dhidden
+    branch[...] = dhidden.astype(LOW)
+    gvec[10:11, :] = total_rows(branch[...])
+    grads.outer_grad(hidden, branch)
+    grads.step0(6)
+    grads.step0(7)
+    for j in range(4):
+        for half in range(2):
+            s = slice(768 * j + 384 * half, 768 * j + 384 * half + 384)
+            raised = dot_nt(branch[...], outer_rows(outer, j, half)) * slope[:, s].astype(WIDE)
+            raised = raised.astype(LOW)
+            slope[:, s] = raised
+            ginner[0:1, s] = total_rows(raised)
+    for unit in (4, 5):
+        spans_of = [slope.at[:, pl.ds(768 * j, 768)] for j in (2 * unit - 8, 2 * unit - 7)]
+        grads.pair_grad(unit, second_low, spans_of[0], second_low, spans_of[1])
+        grads.step0(unit)
+    for x in range(2):
+        s = slice(384 * x, 384 * x + 384)
+        summed = grad[:, s]
+        for j in range(4):
+            summed = summed + dot_nt(slope[:, 768 * j : 768 * j + 768], rows(mats, 8 + j, x))
+        grad[:, s] = summed
+    grads.step1(6)
+    grads.step1(7)
+    arrived = grad[...]
+    unit = unit2[...]
+    gvec[8:9, :] = total_rows(arrived * unit)
+    gvec[9:10, :] = total_rows(arrived)
+    dhidden = norm_grad(unit, scale2, vector(8), arrived)
+    grad[...] = dhidden
+    branch[...] = dhidden.astype(LOW)
+    gvec[7:8, :] = total_rows(branch[...])
+    for x in range(2):
+        upstream[:, 384 * x : 384 * x + 384] = dot_nt(branch[...], rows(mats, 7, x)).astype(LOW)
+    grads.step1(4)
+    grads.step1(5)
+    attention_back(query2, key2, value2, upstream, probs2, dquery, dkey, dvalue, 384)
+    grads.step2(6)
+    grads.step2(7)
+    gvec[5:6, :] = total_rows(dquery[...])
+    gvec[6:7, :] = total_rows(dvalue[...])
+    for x in range(2):
+        s = slice(384 * x, 384 * x + 384)
+        grad[:, s] = grad[:, s] + dot_nt(dquery[...], rows(mats, 4, x))
+        backed = dot_nt(dkey[...], rows(mats, 5, x)) + dot_nt(dvalue[...], rows(mats, 6, x))
+        for block in range(3):
+            memory_parts[block, :, s] = backed[128 * block : 128 * block + 128].astype(LOW)
+    near = grads.ship([(memory_parts.at[0], from_after)], peers.after)
+    near += grads.ship([(memory_parts.at[2], from_before)], peers.before)
+    grads.pair_grad(2, first_low, dquery, memory, dkey)
+    grads.step0(2)
+    grads.pair_grad(3, memory, dvalue, context2, branch)
+    grads.step0(3)
+    grads.step2(4)
+    grads.step2(5)
+    grads.step3(6)
+    grads.step3(7)
+    arrived = grad[...]
+    unit = unit1[...]
+    gvec[3:4, :] = total_rows(arrived * unit)
+    gvec[4:5, :] = total_rows(arrived)
+    dhidden = norm_grad(unit, scale1, vector(3), arrived)
+    grad[...] = dhidden
+    branch[...] = dhidden.astype(LOW)
+    gvec[2:3, :] = total_rows(branch[...])
+    for x in range(2):
+        upstream[:, 384 * x : 384 * x + 384] = dot_nt(branch[...], rows(mats, 3, x)).astype(LOW)
+    grads.step1(2)
+    grads.step1(3)
+    attention_back(query, key, value, upstream, probs, dquery, dkey, dvalue, 256)
+    dkey_two, dvalue_two = dkey.at[pl.ds(0, 256)], dvalue.at[pl.ds(0, 256)]
+    grads.pair_grad(0, tokens.at[pl.ds(128, 128)], dquery, tokens, dkey_two)
+    grads.step0(0)
+    grads.pair_grad(1, tokens, dvalue_two, context, branch)
+    grads.step0(1)
+    gvec[0:1, :] = total_rows(dquery[...])
+    gvec[1:2, :] = total_rows(dvalue_two[...])
+    gvec[13:16, :] = jnp.zeros((3, 768), WIDE)
+
+    def put(c, x, z, y, block):
+        vheld[c, x, z, y] = block
+
+    pack_vectors(gvec, ginner, peers.c, put)
+    c, x, y, z = peers.c, peers.x, peers.y, peers.z
+    vstage = grads.ship([(vheld.at[1 - c], v0)], peers.sibling)
+    grads.step3(4)
+    grads.step3(5)
+    grads.step2(2)
+    grads.step2(3)
+    for x_ in range(2):
+        s = slice(384 * x_, 384 * x_ + 384)
+        backed = dot_nt(dkey_two[...], rows(mats, 1, x_)) + dot_nt(dvalue_two[...], rows(mats, 2, x_))
+        left_part[:, s] = backed[0:128].astype(LOW)
+        tokens_part[:, s] = grad[:, s] + dot_nt(dquery[...], rows(mats, 0, x_)) + backed[128:256]
+    left = grads.ship([(left_part, left_out)], peers.before)
+    grads.step1(0)
+    grads.step1(1)
+    landed(near)
+    sum_up[...] = (
+        memory_parts[1].astype(WIDE) + from_after[...].astype(WIDE) + from_before[...].astype(WIDE)
+    ).astype(LOW)
+    home = grads.ship([(sum_up, memory_out)], peers.mirror)
+    landed(vstage)
+    vheld[c] = vheld[c] + v0[...]
+    vstage = grads.ship([(vheld.at[c, ALL2, ALL4, 1 - y], v1)], peers.across_y)
+    grads.step3(2)
+    grads.step3(3)
+    grads.step2(0)
+    grads.step2(1)
+    landed(vstage)
+    for j in range(2):
+        for k in range(4):
+            vheld[c, j, k, y] = vheld[c, j, k, y] + v1[j, k]
+    vstage = grads.ship([(vheld.at[c, 1 - x, ALL4, y], v2)], peers.across_x)
+    grads.step3(0)
+    grads.step3(1)
+    landed(vstage)
+    for k in range(4):
+        vheld[c, x, k, y] = vheld[c, x, k, y] + v2[k]
+    vstage = []
+    for k in (1, 2, 3):
+        source = vheld.at[c, x, lax.rem(z + k, 4), y]
+        vstage += grads.ship([(source, vout.at[k])], peers.along_z[k - 1])
+    vout[0] = vheld[c, x, z, y]
+    landed(vstage + left + home)
+    grads.finish()
+
+
+def layer_call(mats, outer, vectors, tokens, memory, cotangent, mask_self, mask_cross):
+    shapes = [
+        jax.ShapeDtypeStruct((128, 768), LOW),
+        jax.ShapeDtypeStruct((8, 3, 48, 768), LOW),
+        jax.ShapeDtypeStruct((8, 48, 768), LOW),
+        jax.ShapeDtypeStruct((4, 16, 128), WIDE),
+        jax.ShapeDtypeStruct((128, 768), LOW),
+        jax.ShapeDtypeStruct((128, 768), LOW),
+        jax.ShapeDtypeStruct((128, 768), WIDE),
+    ]
+    low = [
+        (128, 768), (256, 768), (256, 768), (6, 256, 256), (128, 768),
+    ]
+    scratch = [pltpu.VMEM((16, 768), WIDE), pltpu.VMEM((8, 3072), WIDE)]
+    scratch += [pltpu.VMEM(shape, LOW) for shape in low]
+    scratch += [pltpu.VMEM((128, 768), WIDE), pltpu.VMEM((128, 768), LOW)]
+    scratch += [pltpu.VMEM(s, LOW) for s in [(128, 768), (384, 768), (384, 768), (6, 256, 384), (128, 768)]]
+    scratch += [pltpu.VMEM((128, 768), WIDE), pltpu.VMEM((128, 768), LOW)]
+    scratch += [pltpu.VMEM((128, 3072), LOW)] * 2
+    scratch += [pltpu.VMEM((128, 768), WIDE)] * 2
+    scratch += [pltpu.VMEM(s, LOW) for s in [(128, 768), (128, 768), (128, 768), (384, 768), (384, 768)]]
+    scratch += [pltpu.VMEM((16, 768), WIDE), pltpu.VMEM((8, 3072), WIDE)]
+    scratch += [
+        pltpu.VMEM((12, 2, 4, 2, 48, 768), LOW),
+        pltpu.VMEM((4, 2, 4, 2, 48, 768), LOW),
+        pltpu.VMEM((4, 2, 4, 48, 768), LOW),
+        pltpu.VMEM((4, 4, 2, 48, 768), LOW),
+        pltpu.VMEM((8, 4, 48, 768), LOW),
+        pltpu.VMEM((2, 2, 4, 2, 16, 128), WIDE),
+        pltpu.VMEM((2, 4, 2, 16, 128), WIDE),
+        pltpu.VMEM((2, 4, 16, 128), WIDE),
+        pltpu.VMEM((4, 16, 128), WIDE),
+        pltpu.VMEM((128, 768), LOW),
+        pltpu.VMEM((3, 128, 768), LOW),
+        pltpu.VMEM((128, 768), LOW),
+        pltpu.VMEM((128, 768), LOW),
+        pltpu.VMEM((128, 768), LOW),
+        pltpu.SemaphoreType.REGULAR,
+        pltpu.SemaphoreType.DMA((80,)),
+        pltpu.SemaphoreType.DMA((80,)),
+    ]
+    return pl.pallas_call(
+        layer_kernel,
+        out_shape=shapes,
+        in_specs=[vmem()] * 8,
+        out_specs=[vmem(), pl.BlockSpec(memory_space=pl.ANY)] + [vmem()] * 5,
+        scratch_shapes=scratch,
+        compiler_params=pltpu.CompilerParams(
+            collective_id=1, has_side_effects=True, vmem_limit_bytes=VMEM_BYTES
+        ),
+    )(mats, outer, vectors, tokens, memory, cotangent, mask_self, mask_cross)
+
+
+def final_kernel(parts, mine, vparts, left, memory_low, tokens_part, *outs):
+    tokens_grad, memory_grad, small = outs[:3]
+    squares, inner, outer = outs[3:11], outs[11], outs[12]
+    b, s = lax.axis_index(BATCH), lax.axis_index(SEQ)
+    even = lax.rem(s, 2) == 0
+    tokens_grad[...] = tokens_part[...] + left[...].astype(WIDE)
+    memory_grad[...] = memory_low[...].astype(WIDE)
+
+    def summed(unit):
+        return (
+            mine[unit].astype(WIDE) + parts[unit, 0].astype(WIDE)
+            + parts[unit, 1].astype(WIDE) + parts[unit, 2].astype(WIDE)
+        )
+
+    for unit in range(6):
+        total = summed(unit)
+        for k in range(2):
+            body, rest = total[16 * k : 16 * k + 16], total[32 + 8 * k : 40 + 8 * k]
+            matrix = jnp.where(
+                even, jnp.concatenate([body, rest], axis=0), jnp.concatenate([rest, body], axis=0)
+            )
+            m = 2 * unit + k
+            if m < 8:
+                squares[m][...] = matrix
+            else:
+                inner[:, 768 * (m - 8) : 768 * (m - 7)] = matrix
+    outer[0:48, :] = summed(6)
+    outer[48:96, :] = summed(7)
+    index = 8 * b + s
+    vectors = vparts[0] + vparts[1] + vparts[2] + vparts[3]
+    row = lax.broadcasted_iota(jnp.int32, (16, 128), 0)
+    by24 = pltpu.roll(vectors, lax.rem(128 * 24 - 24 * index, 128), 1)
+    by96 = pltpu.roll(vectors, lax.rem(128 * 96 - 96 * index, 128), 1)
+    small[...] = jnp.where(row == 13, by96, by24)
+
+
+def final_call(parts, mine, vparts, left, memory_low, tokens_part):
+    shapes = [
+        jax.ShapeDtypeStruct((128, 768), WIDE),
+        jax.ShapeDtypeStruct((128, 768), WIDE),
+        jax.ShapeDtypeStruct((16, 128), WIDE),
+    ]
+    shapes += [jax.ShapeDtypeStruct((24, 768), WIDE)] * 8
+    shapes += [jax.ShapeDtypeStruct((24, 3072), WIDE), jax.ShapeDtypeStruct((96, 768), WIDE)]
+    return pl.pallas_call(
+        final_kernel,
+        out_shape=shapes,
+        in_specs=[vmem()] * 6,
+        out_specs=[vmem()] * 13,
+        compiler_params=pltpu.CompilerParams(vmem_limit_bytes=32 << 20),
+    )(parts, mine, vparts, left, memory_low, tokens_part)
+
+
+def masks(target_ids, source_ids):
+    first = lax.axis_index(SEQ) * 128
+    query_ids = lax.dynamic_slice_in_dim(target_ids, first, 128, 0)
+    padded = jnp.concatenate([jnp.full((128,), -1, jnp.int32), target_ids])
+    key_ids = lax.dynamic_slice_in_dim(padded, first, 256, 0)
+    offset = jnp.arange(256, dtype=jnp.int32)[None, :] - 128
+    causal = offset <= jnp.arange(128, dtype=jnp.int32)[:, None]
+    allowed = jnp.logical_and(query_ids[:, None] == key_ids[None, :], causal)
+    begin = lax.rem(6 + 8 - lax.axis_index(SEQ), 8) * 128
+    doubled = jnp.concatenate([source_ids, source_ids])
+    cross_ids = lax.dynamic_slice_in_dim(doubled, begin, 384, 0)
+    crossed = query_ids[:, None] == cross_ids[None, :]
+    return (
+        jnp.where(allowed, 0.0, NEGATIVE).astype(WIDE),
+        jnp.where(crossed, 0.0, NEGATIVE).astype(WIDE),
+    )
+
+
+def fast_shards(tokens, memory, target_segments, memory_segments, cotangent, *weights):
+    squares = weights[0:4] + weights[9:13]
+    inner, inner_bias, outer = weights[18:21]
+    smalls = list(weights[4:9]) + list(weights[13:18]) + list(weights[21:24])
+    packed = jnp.zeros((16, 128), LOW)
+    packed = jnp.concatenate(
+        [
+            jnp.pad(jnp.stack(smalls), ((0, 0), (0, 104))),
+            jnp.pad(inner_bias[None], ((0, 0), (0, 32))),
+            jnp.zeros((2, 128), LOW),
+        ]
+    )
+    mask_self, mask_cross = masks(target_segments[0], memory_segments[0])
+    mats, whole_outer, vectors, tokens_two, memory_three = gather_call(
+        squares, inner, outer, packed, tokens[0], memory[0]
+    )
+    output, parts, mine, vparts, left, memory_low, tokens_part = layer_call(
+        mats, whole_outer, vectors, tokens_two, memory_three.reshape(384, 768), cotangent[0], mask_self, mask_cross
+    )
+    results = final_call(parts, mine, vparts, left, memory_low, tokens_part)
+    tokens_grad, memory_grad, small = results[:3]
+    matrices, inner_grad, outer_grad = results[3:11], results[11], results[12]
+    vector = [small[j, 0:24] for j in range(13)]
+    return (
+        (output[None], tokens_grad[None], memory_grad[None])
+        + tuple(matrices[0:4]) + tuple(vector[0:5])
+        + tuple(matrices[4:8]) + tuple(vector[5:10])
+        + (inner_grad, small[13, 0:96], outer_grad) + tuple(vector[10:13])
+    )
+
+
+def fits(mesh):
+    return mesh.shape[BATCH] == 4 and mesh.shape[SEQ] == 8
+
+
 def solution(mesh):
     in_specs = (
-        P("batch", "seq", None),
-        P("batch", "seq", None),
-        P("batch", None),
-        P("batch", None),
-        P("batch", "seq", None),
-        P(("batch", "seq"), None),
-        P(("batch", "seq"), None),
-        P(("batch", "seq"), None),
-        P(("batch", "seq"), None),
-        P(("batch", "seq")),
-        P(("batch", "seq")),
-        P(("batch", "seq")),
-        P(("batch", "seq")),
-        P(("batch", "seq")),
-        P(("batch", "seq"), None),
-        P(("batch", "seq"), None),
-        P(("batch", "seq"), None),
-        P(("batch", "seq"), None),
-        P(("batch", "seq")),
-        P(("batch", "seq")),
-        P(("batch", "seq")),
-        P(("batch", "seq")),
-        P(("batch", "seq")),
-        P(("batch", "seq"), None),
-        P(("batch", "seq")),
-        P(("batch", "seq"), None),
-        P(("batch", "seq")),
-        P(("batch", "seq")),
-        P(("batch", "seq")),
+        P(BATCH, SEQ, None),
+        P(BATCH, SEQ, None),
+        P(BATCH, None),
+        P(BATCH, None),
+        P(BATCH, SEQ, None),
+        P(BOTH, None),
+        P(BOTH, None),
+        P(BOTH, None),
+        P(BOTH, None),
+        P(BOTH),
+        P(BOTH),
+        P(BOTH),
+        P(BOTH),
+        P(BOTH),
+        P(BOTH, None),
+        P(BOTH, None),
+        P(BOTH, None),
+        P(BOTH, None),
+        P(BOTH),
+        P(BOTH),
+        P(BOTH),
+        P(BOTH),
+        P(BOTH),
+        P(BOTH, None),
+        P(BOTH),
+        P(BOTH, None),
+        P(BOTH),
+        P(BOTH),
+        P(BOTH),
     )
     out_specs = (
-        P("batch", "seq", None),
-        P("batch", "seq", None),
-        P("batch", "seq", None),
-        P(("batch", "seq"), None),
-        P(("batch", "seq"), None),
-        P(("batch", "seq"), None),
-        P(("batch", "seq"), None),
-        P(("batch", "seq")),
-        P(("batch", "seq")),
-        P(("batch", "seq")),
-        P(("batch", "seq")),
-        P(("batch", "seq")),
-        P(("batch", "seq"), None),
-        P(("batch", "seq"), None),
-        P(("batch", "seq"), None),
-        P(("batch", "seq"), None),
-        P(("batch", "seq")),
-        P(("batch", "seq")),
-        P(("batch", "seq")),
-        P(("batch", "seq")),
-        P(("batch", "seq")),
-        P(("batch", "seq"), None),
-        P(("batch", "seq")),
-        P(("batch", "seq"), None),
-        P(("batch", "seq")),
-        P(("batch", "seq")),
-        P(("batch", "seq")),
-    )
-    return jax.shard_map(shards, mesh=mesh, in_specs=in_specs, out_specs=out_specs, check_vma=False)
+        P(BATCH, SEQ, None),
+        P(BATCH, SEQ, None),
+        P(BATCH, SEQ, None),
+        P(BOTH, None),
+        P(BOTH, None),
+        P(BOTH, None),
+        P(BOTH, None),
+        P(BOTH),
+        P(BOTH),
+        P(BOTH),
+        P(BOTH),
+        P(BOTH),
+        P(BOTH, None),
+        P(BOTH, None),
+        P(BOTH, None),
+        P(BOTH, None),
+        P(BOTH),
+        P(BOTH),
+        P(BOTH),
+        P(BOTH),
+        P(BOTH),
+        P(BOTH, None),
+        P(BOTH),
+        P(BOTH, None),
+        P(BOTH),
+        P(BOTH),
+        P(BOTH),
+    )
+    quick = fits(mesh)
+    return jax.shard_map(fast_shards if quick else shards, mesh=mesh, in_specs=in_specs, out_specs=out_specs, check_vma=False)

time: 2090 us -> 304 us (0.15)
  waiting for transfers between devices: 1650 us -> 0 us
  Pallas kernels: 0 us -> 287 us
  blocking collectives: 202 us -> 0 us
  matrix products: 128 us -> 0 us
  local copies, waits for them, and re-layouts: 64.3 us -> 11.1 us
    all_gather x18 -> x0, waiting for transfers between devices: 654 us -> none  [the longest x2 85.9 us: attend(): lax.all_gather(keys, 'seq', axis=0, tiled=True)]
    reduce_scatter x5 -> x0, waiting for transfers between devices: 574 us -> none  [the longest x1 142 us: shards(): lax.psum_scatter(grad_outer, ('batch', 'seq'), scatter_dimension=0, tiled...]
    unnamed x33 -> x0, waiting for transfers between devices: 425 us -> none
    pallas_call x0 -> x3, Pallas kernels: none -> 287 us  [the longest x1 143 us: layer_call(): pl.pallas_call(layer_kernel, out_shape=shapes, in_specs=[vmem()] * 8, out...]
    dot_general x42 -> x0, matrix products: 128 us -> none  [the longest x10 28.1 us: matmul(): return jnp.dot(left, right, preferred_element_type=jnp.float32)]
    all_gather x4 -> x0, blocking collectives: 123 us -> none  [the longest x2 61.6 us: attend_back(): lax.all_gather(delta, 'seq', axis=1, tiled=True)]
    unnamed x2 -> x0, blocking collectives: 78.7 us -> none
    unnamed x281 -> x13, local copies, waits for them, and re-layouts: 35.1 us -> 7.75 us
  transfers between devices with their start and end apart: 28 -> 0, of which waited for: 23 -> 0; matrix products, arithmetic and copies ran while one was open for 9% -> 0% of each run, Pallas kernels for 0% -> 0%
where the time goes in v1:
time: 304 us; the launch traced here: 303 us
  Pallas kernels  287 us (94%)
  local copies, waits for them, and re-layouts  11.1 us (4%)
  other arithmetic  4.42 us (1%)
    pallas_call x1, Pallas kernels, layer_call(): pl.pallas_call(layer_kernel, out_shape=shapes, in_specs=[vmem()] * 8, out...  143 us
    pallas_call x1, Pallas kernels, gather_call(): pl.pallas_call(gather_kernel, out_shape=shapes, in_specs=[vmem()] * 13, o...  142 us
    unnamed x13, local copies, waits for them, and re-layouts  7.75 us

profile of v1, /device:TPU:0, one launch (start us, length us, event | category | flops | bytes accessed | tf_op | source)
XLA Modules:
  0.0 303.1 jit_solution(9035343368254591837)
XLA Ops:
  0.7 0.7 dynamic-slice_bitcast_fusion
  1.3 0.1 pad.15.clone
  1.4 0.8 fusion.7
  2.3 0.8 pad_dynamic-slice_fusion.2
  3.0 1.5 stack.55
  4.6 1.3 fusion.6.refs_10_
  5.9 0.7 fusion.1.refs_6_
  6.6 0.8 compare_select_fusion.refs_7_
  7.4 142.4 %shard_map.484 = (bf16[12,2,2,4,48,768]{5,4,3,2,1,0:T(8,128)(2,1)}, bf16[2,2,4,2,96,768]{5,4,3,2,1,0:T(8,128)(2,1)}, bf16[2,2,4,2,16,128]{5,4,3,2,1,0:T(8,128)(2...) custom-call(bf16[24,768]{1,0:T(8,128)(2,1)} %refs_0_.1, bf16[24,768]{1,0:T(8,128)(2,1)} %refs_1_.1, ...), custom_call_target="tpu_custom_call" | custom-call | tf_op jit(solution)/shard_map/pallas_call | solution.py:689
  149.8 143.1 %shard_map.485 = (bf16[128,768]{1,0:T(8,128)(2,1)}, bf16[8,3,48,768]{3,2,1,0:T(8,128)(2,1)}, bf16[8,48,768]{2,1,0:T(8,128)(2,1)}, f32[4,16,128]{2,1,0:T(8,128)},...) custom-call(bf16[12,2,2,4,48,768]{5,4,3,2,1,0:T(8,128)(2,1)} %get-tuple-element.52.refs_0_, ...), custom_call_target="tpu_custom_call" | custom-call | tf_op jit(solution)/shard_map/pallas_call | solution.py:1230
  292.9 0.0 copy-start
  292.9 1.5 copy-done
  294.4 0.0 copy-start.1
  294.4 1.1 copy-done.1
  295.5 0.0 copy-start.2
  295.5 1.0 copy-done.2
  296.5 0.0 copy-start.3
  296.5 0.9 copy-done.3
  297.4 0.0 copy-start.4
  297.4 0.9 copy-done.4
  298.3 0.0 copy-start.5
  298.3 0.8 copy-done.5
  299.1 1.3 shard_map.486
  300.4 0.5 slice_bitcast_fusion.3
  300.9 0.6 slice_bitcast_fusion
  301.5 1.6 copy.57
  (1 shorter events, 0.0 us)
Async XLA Ops:
  292.9 1.5 copy-start
  294.4 1.1 copy-start.1
  295.5 1.0 copy-start.2
  296.5 0.9 copy-start.3
  297.4 0.9 copy-start.4
  298.3 0.8 copy-start.5

commit v2 on v1

--- a/solution.py
+++ b/solution.py
@@ -470,20 +470,29 @@
         self.across_y = device(x, c, 1 - y, z)
         self.sibling = device(x, 1 - c, y, z)
         self.along_z = [device(x, c, y, lax.rem(z + k, 4)) for k in (1, 2, 3)]
+        self.s = s
         self.after = (b, lax.rem(s + 1, 8))
         self.before = (b, lax.rem(s + 7, 8))
         self.mirror = (b, 7 - s)
-
-    def all(self):
-        return [
+        self.folds = [(b, lax.rem(14 - s, 8)), (b, lax.rem(16 - s, 8))]
+        self.alone = [self.folds[k][1] == s for k in range(2)]
+
+    def greet(self):
+        barrier = pltpu.get_barrier_semaphore()
+        always = [
             self.across_x, self.across_y, self.sibling, *self.along_z, self.after, self.before, self.mirror,
         ]
+        for peer in always:
+            pl.semaphore_signal(barrier, inc=1, device_id=peer, device_id_type=MESH)
+        for peer, alone in zip(self.folds, self.alone):
+            @pl.when(jnp.logical_not(alone))
+            def _():
+                pl.semaphore_signal(barrier, inc=1, device_id=peer, device_id_type=MESH)
 
     def meet(self):
         barrier = pltpu.get_barrier_semaphore()
-        for peer in self.all():
-            pl.semaphore_signal(barrier, inc=1, device_id=peer, device_id_type=MESH)
-        pl.semaphore_wait(barrier, len(self.all()))
+        others = [jnp.where(alone, 0, 1) for alone in self.alone]
+        pl.semaphore_wait(barrier, 9 + others[0] + others[1])
 
 
 class Wires:
@@ -523,11 +532,10 @@
 
 
 class Gather:
-    def __init__(self, peers, wires, mats, rests, outer, vectors):
+    def __init__(self, peers, wires, mats, pool, outer, vectors):
         self.peers, self.wires = peers, wires
-        self.mats, self.rests, self.outer, self.vectors = mats, rests, outer, vectors
+        self.mats, self.pool, self.outer, self.vectors = mats, pool, outer, vectors
         self.steps = [{} for _ in range(8)]
-        self.done = []
 
     def parts(self, unit, x, c, z, y):
         both = y is None
@@ -539,7 +547,9 @@
             refs = [self.mats.at[mats, x, c, z, pl.ds(0, 16)], self.mats.at[mats, x, c, z, pl.ds(32, 16)]]
         else:
             refs = [self.mats.at[mats, x, c, z, pl.ds(pl.multiple_of(32 * y, 16), 16)]]
-        refs.append(self.rests.at[unit, x, c, z, ALL2 if both else y])
+        depth = pl.ds(4 * c, 4) if z is ALL4 else 4 * c + z
+        side = 2 * (unit % 2)
+        refs.append(self.pool.at[depth, x, pl.ds(side, 2) if both else side + y, unit // 2])
         if unit == 0:
             refs.append(self.vectors.at[x, c, z, ALL2 if both else y])
         return refs
@@ -549,7 +559,6 @@
         copies = self.wires.copies(pairs, target)
         start(copies)
         self.steps[unit][name] = copies
-        self.done += copies
 
     def z_start(self, unit):
         p = self.peers
@@ -584,37 +593,48 @@
         landed(self.steps[unit]["near"])
         landed(self.steps[unit]["far"])
 
-
-def gather_pack(y, x, c, z, squares, inner, outer, small, mats, rests, whole_outer, vectors):
-    def split(values):
+    def close(self, units):
+        for unit in units:
+            for copies in self.steps[unit].values():
+                sent(copies)
+
+
+def gather_pack(unit, peers, squares, inner, outer, mats, pool, whole_outer):
+    x, c, y, z = peers.x, peers.c, peers.y, peers.z
+    if unit >= 6:
+        half = slice(48 * (unit - 6), 48 * (unit - 6) + 48)
+        whole_outer[x, c, z, y, half] = outer[half]
+        return
+    rests = []
+    for k in range(2):
+        m = 2 * unit + k
+        values = squares[m][...] if m < 8 else inner[:, 768 * (m - 8) : 768 * (m - 7)]
         values = values.astype(WIDE)
         body = jnp.where(y == 0, values[0:16], values[8:24])
-        rest = jnp.where(y == 0, values[16:24], values[0:8])
-        return (body.astype(LOW), rest)
-
-    for unit in range(6):
-        rests_of = []
-        for k in range(2):
-            m = 2 * unit + k
-            values = squares[m][...] if m < 8 else inner[:, 768 * (m - 8) : 768 * (m - 7)]
-            body, rest = split(values)
-            mats[m, x, c, z, pl.ds(pl.multiple_of(32 * y, 16), 16), :] = body
-            rests_of.append(rest)
-        rests[unit, x, c, z, y] = jnp.concatenate(rests_of, axis=0).astype(LOW)
-    whole_outer[x, c, z, y] = outer[...]
-    index = (2 * x + c) * 8 + 2 * z + y
-    wide = small[...].astype(WIDE)
+        rests.append(jnp.where(y == 0, values[16:24], values[0:8]))
+        mats[m, x, c, z, pl.ds(pl.multiple_of(32 * y, 16), 16), :] = body.astype(LOW)
+    pool[4 * c + z, x, 2 * (unit % 2) + y, unit // 2] = jnp.concatenate(rests, axis=0).astype(LOW)
+
+
+def gather_vectors(peers, smalls, board, vectors):
+    board[...] = jnp.zeros((16, 128), WIDE)
+    for j, small in enumerate(smalls):
+        board[j : j + 1, 0 : small.shape[1]] = small[...].astype(WIDE)
+    index = (2 * peers.x + peers.c) * 8 + peers.s
+    wide = board[...]
     row = lax.broadcasted_iota(jnp.int32, (16, 128), 0)
     by24 = pltpu.roll(wide, lax.rem(24 * index, 128), 1)
     by96 = pltpu.roll(wide, lax.rem(96 * index, 128), 1)
-    vectors[x, c, z, y] = jnp.where(row == 13, by96, by24).astype(LOW)
-
-
-def merge_rests(unit, mats, rests):
+    rolled = jnp.where(row == 13, by96, by24).astype(LOW)
+    vectors[peers.x, peers.c, peers.z, peers.y] = rolled
+
+
+def merge_rests(unit, mats, pool):
     def one(step, carry):
         x, c, z = lax.div(step, 8), lax.rem(lax.div(step, 4), 2), lax.rem(step, 4)
-        low_half = rests[unit, x, c, z, 0].astype(WIDE)
-        high_half = rests[unit, x, c, z, 1].astype(WIDE)
+        side = 2 * (unit % 2)
+        low_half = pool[4 * c + z, x, side, unit // 2].astype(WIDE)
+        high_half = pool[4 * c + z, x, side + 1, unit // 2].astype(WIDE)
         mats[2 * unit, x, c, z, 16:32, :] = jnp.concatenate(
             [low_half[0:8], high_half[0:8]], axis=0
         ).astype(LOW)
@@ -626,80 +646,8 @@
     lax.fori_loop(0, 16, one, 0)
 
 
-def gather_kernel(*refs):
-    squares, refs = refs[:8], refs[8:]
-    inner, outer, small, tokens, memory = refs[:5]
-    mats, whole_outer, vectors, tokens_two, memory_three = refs[5:10]
-    rests, send, recv = refs[10:]
-    peers = Peers()
-    x, c, y, z = peers.x, peers.c, peers.y, peers.z
-    gather_pack(y, x, c, z, squares, inner, outer, small, mats, rests, whole_outer, vectors)
-    tokens_two[128:256, :] = tokens[...]
-    peers.meet()
-    wires = Wires(send, recv)
-    weights = Gather(peers, wires, mats, rests, whole_outer, vectors)
-    weights.z_start(0)
-    weights.z_start(1)
-    left = wires.copies([(tokens, tokens_two.at[pl.ds(0, 128)])], peers.after)
-    mirrored = wires.copies([(memory, memory_three.at[1])], peers.mirror)
-    start(left)
-    start(mirrored)
-    weights.z_start(2)
-    weights.z_start(3)
-    spread = []
-    for pair in range(6):
-        if pair < 4:
-            for unit in (2 * pair, 2 * pair + 1):
-                weights.first(unit)
-            if pair + 2 < 4:
-                weights.z_start(2 * pair + 4)
-                weights.z_start(2 * pair + 5)
-        if 1 <= pair < 5:
-            for unit in (2 * pair - 2, 2 * pair - 1):
-                weights.second(unit)
-        if pair == 1:
-            landed(mirrored)
-            spread = wires.copies([(memory_three.at[1], memory_three.at[2])], peers.after)
-            spread += wires.copies([(memory_three.at[1], memory_three.at[0])], peers.before)
-            start(spread)
-        if pair >= 2:
-            for unit in (2 * pair - 4, 2 * pair - 3):
-                weights.third(unit)
-    for unit in range(8):
-        weights.last(unit)
-        if unit < 6:
-            merge_rests(unit, mats, rests)
-    landed(left)
-    landed(spread)
-    sent(weights.done + left + mirrored + spread)
-
-
 def vmem():
     return pl.BlockSpec(memory_space=pltpu.VMEM)
-
-
-def gather_call(squares, inner, outer, small, tokens, memory):
-    shapes = [
-        jax.ShapeDtypeStruct((12, 2, 2, 4, 48, 768), LOW),
-        jax.ShapeDtypeStruct((2, 2, 4, 2, 96, 768), LOW),
-        jax.ShapeDtypeStruct((2, 2, 4, 2, 16, 128), LOW),
-        jax.ShapeDtypeStruct((256, 768), LOW),
-        jax.ShapeDtypeStruct((3, 128, 768), LOW),
-    ]
-    return pl.pallas_call(
-        gather_kernel,
-        out_shape=shapes,
-        in_specs=[vmem()] * 13,
-        out_specs=[vmem()] * 5,
-        scratch_shapes=[
-            pltpu.VMEM((6, 2, 2, 4, 2, 16, 768), LOW),
-            pltpu.SemaphoreType.DMA((160,)),
-            pltpu.SemaphoreType.DMA((160,)),
-        ],
-        compiler_params=pltpu.CompilerParams(
-            collective_id=0, has_side_effects=True, vmem_limit_bytes=VMEM_BYTES
-        ),
-    )(*squares, inner, outer, small, tokens, memory)
 
 
 def dot(left, right):
@@ -845,9 +793,9 @@
 class Grads:
     ORDER = (6, 7, 4, 5, 2, 3, 0, 1)
 
-    def __init__(self, peers, wires, held, r0, r1_even, r1_odd, r2, out, mine, credit):
+    def __init__(self, peers, wires, held, r0, pool, r2, out, mine, credit):
         self.peers, self.wires, self.held = peers, wires, held
-        self.r0, self.r1_even, self.r1_odd, self.r2, self.out = r0, r1_even, r1_odd, r2, out
+        self.r0, self.pool, self.r2, self.out = r0, pool, r2, out
         self.mine, self.credit = mine, credit
         self.stage = {}
         self.open = []
@@ -895,10 +843,10 @@
         if turn < 4:
             pl.semaphore_signal(self.credit, inc=1, device_id=p.sibling, device_id_type=MESH)
         if unit % 2:
-            pairs = [(held.at[unit, 1 - p.x], self.r1_odd.at[unit // 2])]
+            pairs = [(held.at[unit, 1 - p.x, ALL4, k], self.pool.at[unit, k]) for k in range(2)]
             self.stage[unit] = self.ship(pairs, p.across_x)
         else:
-            pairs = [(held.at[unit, ALL2, ALL4, 1 - p.y], self.r1_even.at[unit // 2])]
+            pairs = [(held.at[unit, ALL2, ALL4, 1 - p.y], self.pool.at[unit])]
             self.stage[unit] = self.ship(pairs, p.across_y)
 
     def step2(self, unit):
@@ -907,10 +855,11 @@
 
         def add(i, carry):
             if unit % 2:
-                held[unit, p.x, i] = held[unit, p.x, i] + self.r1_odd[unit // 2, i]
+                for k in range(2):
+                    held[unit, p.x, i, k] = held[unit, p.x, i, k] + self.pool[unit, k, i]
             else:
                 for j in range(2):
-                    held[unit, j, i, p.y] = held[unit, j, i, p.y] + self.r1_even[unit // 2, j, i]
+                    held[unit, j, i, p.y] = held[unit, j, i, p.y] + self.pool[unit, j, i]
             return carry
 
         lax.fori_loop(0, 4, add, 0)
@@ -961,9 +910,9 @@
                             base = 24 * (8 * c + 2 * z + y)
                             body = base + 8 * y
                             rest = base + 16 * (1 - y)
-                            self.held[slot, x, z, y, 0:16, s] = one[body : body + 16].astype(LOW)
-                            self.held[slot, x, z, y, 16:32, s] = two[body : body + 16].astype(LOW)
-                            self.held[slot, x, z, y, 32:48, s] = jnp.concatenate(
+                            self.held[slot, x, z, y, 0, :, s] = one[body : body + 16].astype(LOW)
+                            self.held[slot, x, z, y, 1, :, s] = two[body : body + 16].astype(LOW)
+                            self.held[slot, x, z, y, 2, :, s] = jnp.concatenate(
                                 [one[rest : rest + 8], two[rest : rest + 8]], axis=0
                             ).astype(LOW)
 
@@ -981,32 +930,88 @@
                         for k in range(4):
                             base = 96 * k + 48 * (unit - 6)
                             z, y = 2 * half + k // 2, k % 2
-                            self.held[slot, x, z, y, :, s] = one[base : base + 48].astype(LOW)
+                            block = one[base : base + 48].reshape(3, 16, 256)
+                            self.held[slot, x, z, y, :, :, s] = block.astype(LOW)
 
 
 def layer_kernel(*refs):
-    mats, outer, vectors, tokens, memory, cotangent, mask_self, mask_cross = refs[:8]
-    output, out, mine, vout, left_out, memory_out, tokens_part = refs[8:15]
-    scratch = refs[15:]
+    squares, inner_own, outer_own, smalls = refs[0:8], refs[8], refs[9], refs[10:24]
+    tokens_own, memory_own, cotangent, target_ids, source_ids = refs[24:29]
+    output, out, mine, vout, left_out, memory_out, tokens_part = refs[29:36]
     (
+        mats, outer, vectors, tokens, memory, board, mask_self, mask_cross,
         vec, inner_bias, query, key, value, probs, context, unit1, first_low,
         query2, key2, value2, probs2, context2, unit2, second_low,
         hidden, slope, total, grad, branch, upstream, dquery, dkey, dvalue,
         gvec, ginner,
-        held, r0, r1_even, r1_odd, r2, vheld, v0, v1, v2, left_part, memory_parts,
-        from_after, from_before, sum_up, credit, send, recv,
-    ) = scratch
+        held, r0, pool, r2, vheld, v0, v1, v2, left_part, memory_parts,
+        credit, free, send, recv, local,
+    ) = refs[36:]
     peers = Peers()
+    peers.greet()
+    wires = Wires(send, recv)
+    weights = Gather(peers, wires, mats, pool, outer, vectors)
+    grads = Grads(peers, wires, held, r0, pool, r2, out, mine, credit)
+    own = slice(128, 256)
+
+    def pack(unit):
+        gather_pack(unit, peers, squares, inner_own, outer_own, mats, pool, outer)
+
+    pack(0)
+    gather_vectors(peers, smalls, board, vectors)
     peers.meet()
-    wires = Wires(send, recv)
-    grads = Grads(peers, wires, held, r0, r1_even, r1_odd, r2, out, mine, credit)
-    own = slice(128, 256)
-
-    unpack_vectors(vectors, vec, inner_bias)
+    weights.z_start(0)
+    pack(1)
+    weights.z_start(1)
+    tokens[own, :] = tokens_own[...]
+    left = wires.copies([(tokens_own, tokens.at[pl.ds(0, 128)])], peers.after)
+    mirrored = wires.copies([(memory_own, memory.at[pl.ds(128, 128)])], peers.mirror)
+    start(left + mirrored)
+    folds = [
+        wires.copies([(memory_own, memory.at[pl.ds(256 * k, 128)])], peers.folds[k]) for k in range(2)
+    ]
+    for k in range(2):
+        @pl.when(jnp.logical_not(peers.alone[k]))
+        def _():
+            start(folds[k])
+
+        @pl.when(peers.alone[k])
+        def _():
+            memory[pl.ds(256 * k, 128), :] = memory_own[...]
+
+    for unit in range(2, 8):
+        pack(unit)
+    fill_masks(peers, target_ids, source_ids, mask_self, mask_cross)
+
+    def turn(t):
+        if t < 4:
+            weights.first(2 * t)
+            weights.first(2 * t + 1)
+            if t < 3:
+                weights.z_start(2 * t + 2)
+                weights.z_start(2 * t + 3)
+        if 1 <= t < 5:
+            weights.second(2 * t - 2)
+            weights.second(2 * t - 1)
+        if t >= 2:
+            weights.third(2 * t - 4)
+            weights.third(2 * t - 3)
+
+    def arrive(pair):
+        for unit in (2 * pair, 2 * pair + 1):
+            weights.last(unit)
+            if unit < 6:
+                merge_rests(unit, mats, pool)
 
     def vector(j):
         return vec[j : j + 1, :]
 
+    turn(0)
+    turn(1)
+    turn(2)
+    arrive(0)
+    unpack_vectors(vectors, vec, inner_bias)
+    landed(left)
     for n in range(3):
         s = strip(n)
         query[:, s] = (dot(tokens[own, :], columns(mats, 0, n)) + vec[0:1, s]).astype(LOW)
@@ -1023,6 +1028,15 @@
     first = unit * vector(3) + vector(4)
     total[...] = first
     first_low[...] = first.astype(LOW)
+    turn(3)
+    arrive(1)
+    landed(mirrored)
+    for k in range(2):
+        @pl.when(jnp.logical_not(peers.alone[k]))
+        def _():
+            landed(folds[k])
+            sent(folds[k])
+
     for n in range(3):
         s = strip(n)
         query2[:, s] = (dot(first_low[...], columns(mats, 4, n)) + vec[5:6, s]).astype(LOW)
@@ -1037,6 +1051,11 @@
     second = unit * vector(8) + vector(9)
     total[...] = second + vector(10)
     second_low[...] = second.astype(LOW)
+    turn(4)
+    arrive(2)
+    weights.close(range(6))
+    for peer in (peers.across_x, peers.across_y):
+        pl.semaphore_signal(free, inc=1, device_id=peer, device_id_type=MESH)
     for j in range(4):
         for n in range(3):
             s = slice(768 * j + 256 * n, 768 * j + 256 * n + 256)
@@ -1046,11 +1065,17 @@
             slope[:, s] = (
                 normal + pre * (0.3989422804014327 * jnp.exp(-0.5 * pre * pre))
             ).astype(LOW)
-        for n in range(3):
-            s = strip(n)
-            total[:, s] = total[:, s] + dot(
-                hidden[:, 768 * j : 768 * j + 768], outer_columns(outer, j, n)
-            )
+    turn(5)
+    arrive(3)
+    weights.close(range(6, 8))
+    sent(left + mirrored)
+    for n in range(3):
+        s = strip(n)
+        summed = total[:, s]
+        for j in range(4):
+            here = slice(768 * j, 768 * j + 768)
+            summed = summed + dot(hidden[:, here], outer_columns(outer, j, n))
+        total[:, s] = summed
     unit, scale3 = centered(total[...])
     output[...] = (unit * vector(11) + vector(12)).astype(LOW)
     arrived = cotangent[...].astype(WIDE)
@@ -1080,6 +1105,7 @@
         for j in range(4):
             summed = summed + dot_nt(slope[:, 768 * j : 768 * j + 768], rows(mats, 8 + j, x))
         grad[:, s] = summed
+    pl.semaphore_wait(free, 2)
     grads.step1(6)
     grads.step1(7)
     arrived = grad[...]
@@ -1105,8 +1131,22 @@
         backed = dot_nt(dkey[...], rows(mats, 5, x)) + dot_nt(dvalue[...], rows(mats, 6, x))
         for block in range(3):
             memory_parts[block, :, s] = backed[128 * block : 128 * block + 128].astype(LOW)
-    near = grads.ship([(memory_parts.at[0], from_after)], peers.after)
-    near += grads.ship([(memory_parts.at[2], from_before)], peers.before)
+    home = grads.ship([(memory_parts.at[1], memory_out.at[1])], peers.mirror)
+    back = [
+        wires.copies([(memory_parts.at[2 * k], memory_out.at[2 * k])], peers.folds[k]) for k in range(2)
+    ]
+    stay = [
+        pltpu.make_async_copy(memory_parts.at[2 * k], memory_out.at[2 * k], local.at[k]) for k in range(2)
+    ]
+    for k in range(2):
+        @pl.when(jnp.logical_not(peers.alone[k]))
+        def _():
+            start(back[k])
+
+        @pl.when(peers.alone[k])
+        def _():
+            stay[k].start()
+
     grads.pair_grad(2, first_low, dquery, memory, dkey)
     grads.step0(2)
     grads.pair_grad(3, memory, dvalue, context2, branch)
@@ -1155,11 +1195,6 @@
     left = grads.ship([(left_part, left_out)], peers.before)
     grads.step1(0)
     grads.step1(1)
-    landed(near)
-    sum_up[...] = (
-        memory_parts[1].astype(WIDE) + from_after[...].astype(WIDE) + from_before[...].astype(WIDE)
-    ).astype(LOW)
-    home = grads.ship([(sum_up, memory_out)], peers.mirror)
     landed(vstage)
     vheld[c] = vheld[c] + v0[...]
     vstage = grads.ship([(vheld.at[c, ALL2, ALL4, 1 - y], v1)], peers.across_y)
@@ -1183,75 +1218,137 @@
         vstage += grads.ship([(source, vout.at[k])], peers.along_z[k - 1])
     vout[0] = vheld[c, x, z, y]
     landed(vstage + left + home)
+    for k in range(2):
+        @pl.when(jnp.logical_not(peers.alone[k]))
+        def _():
+            landed(back[k])
+            sent(back[k])
+
+        @pl.when(peers.alone[k])
+        def _():
+            stay[k].wait()
+
     grads.finish()
 
 
-def layer_call(mats, outer, vectors, tokens, memory, cotangent, mask_self, mask_cross):
+def fill_masks(peers, target_ids, source_ids, mask_self, mask_cross):
+    def ids(ref, block):
+        here = pl.ds(pl.multiple_of(128 * block, 128), 128)
+        return jnp.broadcast_to(ref[:, here].astype(WIDE), (128, 128))
+
+    s = peers.s
+    here = ids(target_ids, s)
+    queries = jnp.transpose(here)
+    row = lax.broadcasted_iota(jnp.int32, (128, 128), 0)
+    column = lax.broadcasted_iota(jnp.int32, (128, 128), 1)
+    before = jnp.where(s > 0, ids(target_ids, lax.rem(s + 7, 8)), -1.0)
+    mask_self[:, 0:128] = jnp.where(queries == before, 0.0, NEGATIVE)
+    seen = jnp.where(queries == here, 0.0, NEGATIVE)
+    mask_self[:, 128:256] = jnp.where(column <= row, seen, NEGATIVE)
+    for k in range(3):
+        block = ids(source_ids, lax.rem(14 + k - s, 8))
+        mask_cross[:, 128 * k : 128 * k + 128] = jnp.where(queries == block, 0.0, NEGATIVE)
+
+
+def layer_call(*inputs):
     shapes = [
         jax.ShapeDtypeStruct((128, 768), LOW),
-        jax.ShapeDtypeStruct((8, 3, 48, 768), LOW),
-        jax.ShapeDtypeStruct((8, 48, 768), LOW),
+        jax.ShapeDtypeStruct((8, 3, 3, 16, 768), LOW),
+        jax.ShapeDtypeStruct((8, 3, 16, 768), LOW),
         jax.ShapeDtypeStruct((4, 16, 128), WIDE),
         jax.ShapeDtypeStruct((128, 768), LOW),
-        jax.ShapeDtypeStruct((128, 768), LOW),
+        jax.ShapeDtypeStruct((3, 128, 768), LOW),
         jax.ShapeDtypeStruct((128, 768), WIDE),
     ]
-    low = [
-        (128, 768), (256, 768), (256, 768), (6, 256, 256), (128, 768),
+
+    def low(*shape):
+        return pltpu.VMEM(shape, LOW)
+
+    def wide(*shape):
+        return pltpu.VMEM(shape, WIDE)
+
+    scratch = [
+        low(12, 2, 2, 4, 48, 768),
+        low(2, 2, 4, 2, 96, 768),
+        low(2, 2, 4, 2, 16, 128),
+        low(256, 768),
+        low(384, 768),
+        wide(16, 128),
+        wide(128, 256),
+        wide(128, 384),
+        wide(16, 768),
+        wide(8, 3072),
+        low(128, 768),
+        low(256, 768),
+        low(256, 768),
+        low(6, 256, 256),
+        low(128, 768),
+        wide(128, 768),
+        low(128, 768),
+        low(128, 768),
+        low(384, 768),
+        low(384, 768),
+        low(6, 256, 384),
+        low(128, 768),
+        wide(128, 768),
+        low(128, 768),
+        low(128, 3072),
+        low(128, 3072),
+        wide(128, 768),
+        wide(128, 768),
+        low(128, 768),
+        low(128, 768),
+        low(128, 768),
+        low(384, 768),
+        low(384, 768),
+        wide(16, 768),
+        wide(8, 3072),
+        low(12, 2, 4, 2, 3, 16, 768),
+        low(4, 2, 4, 2, 3, 16, 768),
+        low(8, 2, 4, 3, 16, 768),
+        low(8, 4, 3, 16, 768),
+        wide(2, 2, 4, 2, 16, 128),
+        wide(2, 4, 2, 16, 128),
+        wide(2, 4, 16, 128),
+        wide(4, 16, 128),
+        low(128, 768),
+        low(3, 128, 768),
+        pltpu.SemaphoreType.REGULAR,
+        pltpu.SemaphoreType.REGULAR,
+        pltpu.SemaphoreType.DMA((240,)),
+        pltpu.SemaphoreType.DMA((240,)),
+        pltpu.SemaphoreType.DMA((2,)),
     ]
-    scratch = [pltpu.VMEM((16, 768), WIDE), pltpu.VMEM((8, 3072), WIDE)]
-    scratch += [pltpu.VMEM(shape, LOW) for shape in low]
-    scratch += [pltpu.VMEM((128, 768), WIDE), pltpu.VMEM((128, 768), LOW)]
-    scratch += [pltpu.VMEM(s, LOW) for s in [(128, 768), (384, 768), (384, 768), (6, 256, 384), (128, 768)]]
-    scratch += [pltpu.VMEM((128, 768), WIDE), pltpu.VMEM((128, 768), LOW)]
-    scratch += [pltpu.VMEM((128, 3072), LOW)] * 2
-    scratch += [pltpu.VMEM((128, 768), WIDE)] * 2
-    scratch += [pltpu.VMEM(s, LOW) for s in [(128, 768), (128, 768), (128, 768), (384, 768), (384, 768)]]
-    scratch += [pltpu.VMEM((16, 768), WIDE), pltpu.VMEM((8, 3072), WIDE)]
-    scratch += [
-        pltpu.VMEM((12, 2, 4, 2, 48, 768), LOW),
-        pltpu.VMEM((4, 2, 4, 2, 48, 768), LOW),
-        pltpu.VMEM((4, 2, 4, 48, 768), LOW),
-        pltpu.VMEM((4, 4, 2, 48, 768), LOW),
-        pltpu.VMEM((8, 4, 48, 768), LOW),
-        pltpu.VMEM((2, 2, 4, 2, 16, 128), WIDE),
-        pltpu.VMEM((2, 4, 2, 16, 128), WIDE),
-        pltpu.VMEM((2, 4, 16, 128), WIDE),
-        pltpu.VMEM((4, 16, 128), WIDE),
-        pltpu.VMEM((128, 768), LOW),
-        pltpu.VMEM((3, 128, 768), LOW),
-        pltpu.VMEM((128, 768), LOW),
-        pltpu.VMEM((128, 768), LOW),
-        pltpu.VMEM((128, 768), LOW),
-        pltpu.SemaphoreType.REGULAR,
-        pltpu.SemaphoreType.DMA((80,)),
-        pltpu.SemaphoreType.DMA((80,)),
-    ]
+    anywhere = pl.BlockSpec(memory_space=pl.ANY)
     return pl.pallas_call(
         layer_kernel,
         out_shape=shapes,
-        in_specs=[vmem()] * 8,
-        out_specs=[vmem(), pl.BlockSpec(memory_space=pl.ANY)] + [vmem()] * 5,
+        in_specs=[vmem()] * 29,
+        out_specs=[vmem(), anywhere, vmem(), vmem(), anywhere, anywhere, vmem()],
         scratch_shapes=scratch,
         compiler_params=pltpu.CompilerParams(
-            collective_id=1, has_side_effects=True, vmem_limit_bytes=VMEM_BYTES
+            collective_id=0, has_side_effects=True, vmem_limit_bytes=VMEM_BYTES
         ),
-    )(mats, outer, vectors, tokens, memory, cotangent, mask_self, mask_cross)
-
-
-def final_kernel(parts, mine, vparts, left, memory_low, tokens_part, *outs):
-    tokens_grad, memory_grad, small = outs[:3]
-    squares, inner, outer = outs[3:11], outs[11], outs[12]
+    )(*inputs)
+
+
+def final_kernel(output_low, parts, mine, vparts, left, memory_low, tokens_part, *outs):
+    output, tokens_grad, memory_grad, small = outs[:4]
+    squares, inner, outer = outs[4:12], outs[12], outs[13]
+    output[...] = output_low[...]
     b, s = lax.axis_index(BATCH), lax.axis_index(SEQ)
     even = lax.rem(s, 2) == 0
     tokens_grad[...] = tokens_part[...] + left[...].astype(WIDE)
-    memory_grad[...] = memory_low[...].astype(WIDE)
+    memory_grad[...] = (
+        memory_low[0].astype(WIDE) + memory_low[1].astype(WIDE) + memory_low[2].astype(WIDE)
+    )
 
     def summed(unit):
-        return (
+        total = (
             mine[unit].astype(WIDE) + parts[unit, 0].astype(WIDE)
             + parts[unit, 1].astype(WIDE) + parts[unit, 2].astype(WIDE)
         )
+        return total.reshape(48, 768)
 
     for unit in range(6):
         total = summed(unit)
@@ -1275,8 +1372,9 @@
     small[...] = jnp.where(row == 13, by96, by24)
 
 
-def final_call(parts, mine, vparts, left, memory_low, tokens_part):
+def final_call(*inputs):
     shapes = [
+        jax.ShapeDtypeStruct((128, 768), LOW),
         jax.ShapeDtypeStruct((128, 768), WIDE),
         jax.ShapeDtypeStruct((128, 768), WIDE),
         jax.ShapeDtypeStruct((16, 128), WIDE),
@@ -1286,58 +1384,39 @@
     return pl.pallas_call(
         final_kernel,
         out_shape=shapes,
-        in_specs=[vmem()] * 6,
-        out_specs=[vmem()] * 13,
-        compiler_params=pltpu.CompilerParams(vmem_limit_bytes=32 << 20),
-    )(parts, mine, vparts, left, memory_low, tokens_part)
-
-
-def masks(target_ids, source_ids):
-    first = lax.axis_index(SEQ) * 128
-    query_ids = lax.dynamic_slice_in_dim(target_ids, first, 128, 0)
-    padded = jnp.concatenate([jnp.full((128,), -1, jnp.int32), target_ids])
-    key_ids = lax.dynamic_slice_in_dim(padded, first, 256, 0)
-    offset = jnp.arange(256, dtype=jnp.int32)[None, :] - 128
-    causal = offset <= jnp.arange(128, dtype=jnp.int32)[:, None]
-    allowed = jnp.logical_and(query_ids[:, None] == key_ids[None, :], causal)
-    begin = lax.rem(6 + 8 - lax.axis_index(SEQ), 8) * 128
-    doubled = jnp.concatenate([source_ids, source_ids])
-    cross_ids = lax.dynamic_slice_in_dim(doubled, begin, 384, 0)
-    crossed = query_ids[:, None] == cross_ids[None, :]
-    return (
-        jnp.where(allowed, 0.0, NEGATIVE).astype(WIDE),
-        jnp.where(crossed, 0.0, NEGATIVE).astype(WIDE),
-    )
+        in_specs=[vmem()] * 7,
+        out_specs=[vmem()] * 14,
+        compiler_params=pltpu.CompilerParams(vmem_limit_bytes=VMEM_BYTES),
+    )(*inputs)
 
 
 def fast_shards(tokens, memory, target_segments, memory_segments, cotangent, *weights):
     squares = weights[0:4] + weights[9:13]
     inner, inner_bias, outer = weights[18:21]
-    smalls = list(weights[4:9]) + list(weights[13:18]) + list(weights[21:24])
-    packed = jnp.zeros((16, 128), LOW)
-    packed = jnp.concatenate(
-        [
-            jnp.pad(jnp.stack(smalls), ((0, 0), (0, 104))),
-            jnp.pad(inner_bias[None], ((0, 0), (0, 32))),
-            jnp.zeros((2, 128), LOW),
-        ]
-    )
-    mask_self, mask_cross = masks(target_segments[0], memory_segments[0])
-    mats, whole_outer, vectors, tokens_two, memory_three = gather_call(
-        squares, inner, outer, packed, tokens[0], memory[0]
-    )
-    output, parts, mine, vparts, left, memory_low, tokens_part = layer_call(
-        mats, whole_outer, vectors, tokens_two, memory_three.reshape(384, 768), cotangent[0], mask_self, mask_cross
-    )
-    results = final_call(parts, mine, vparts, left, memory_low, tokens_part)
-    tokens_grad, memory_grad, small = results[:3]
-    matrices, inner_grad, outer_grad = results[3:11], results[11], results[12]
+    smalls = list(weights[4:9]) + list(weights[13:18]) + list(weights[21:24]) + [inner_bias]
+    results = layer_call(
+        *squares,
+        inner,
+        outer,
+        *[small[None] for small in smalls],
+        tokens[0],
+        memory[0],
+        cotangent[0],
+        target_segments,
+        memory_segments,
+    )
+    results = final_call(*results)
+    output, tokens_grad, memory_grad, small = results[:4]
+    matrices, inner_grad, outer_grad = results[4:12], results[12], results[13]
     vector = [small[j, 0:24] for j in range(13)]
     return (
         (output[None], tokens_grad[None], memory_grad[None])
-        + tuple(matrices[0:4]) + tuple(vector[0:5])
-        + tuple(matrices[4:8]) + tuple(vector[5:10])
-        + (inner_grad, small[13, 0:96], outer_grad) + tuple(vector[10:13])
+        + tuple(matrices[0:4])
+        + tuple(vector[0:5])
+        + tuple(matrices[4:8])
+        + tuple(vector[5:10])
+        + (inner_grad, small[13, 0:96], outer_grad)
+        + tuple(vector[10:13])
     )
 
 

time: 304 us -> 258 us (0.85)
  Pallas kernels: 287 us -> 254 us
  local copies, waits for them, and re-layouts: 11.1 us -> 2.72 us
  other arithmetic: 4.42 us -> 0 us
    pallas_call x3 -> x2, Pallas kernels: 287 us -> 254 us  [the longest x1 250 us: layer_call(): pl.pallas_call(layer_kernel, out_shape=shapes, in_specs=[vmem()] * 29, ou...]
    unnamed x13 -> x0, local copies, waits for them, and re-layouts: 7.75 us -> none
where the time goes in v2:
time: 258 us; the launch traced here: 257 us
  Pallas kernels  254 us (98%)
  local copies, waits for them, and re-layouts  2.72 us (1%)
    pallas_call x1, Pallas kernels, layer_call(): pl.pallas_call(layer_kernel, out_shape=shapes, in_specs=[vmem()] * 29, ou...  250 us

profile of v2, /device:TPU:0, one launch (start us, length us, event | category | flops | bytes accessed | tf_op | source)
XLA Modules:
  0.0 257.5 jit_solution(5420865663491084213)
XLA Ops:
  0.7 250.5 %shard_map.484 = (bf16[128,768]{1,0:T(8,128)(2,1)}, bf16[8,3,3,16,768]{4,3,2,1,0:T(8,128)(2,1)}, bf16[8,3,16,768]{3,2,1,0:T(8,128)(2,1)}, f32[4,16,128]{2,1,0:T(...) custom-call(bf16[24,768]{1,0:T(8,128)(2,1)} %refs_0_.1, ...), custom_call_target="tpu_custom_call" | custom-call | tf_op jit(solution)/shard_map/pallas_call | solution.py:1323
  251.2 3.4 %shard_map.485 = (bf16[128,768]{1,0:T(8,128)(2,1)}, f32[128,768]{1,0:T(8,128)}, f32[128,768]{1,0:T(8,128)}, f32[16,128]{1,0:T(8,128)}, f32[24,768]{1,0:T(8,128)}...) custom-call(bf16[128,768]{1,0:T(8,128)(2,1)} %get-tuple-element.48.o, ...), custom_call_target="tpu_custom_call" | custom-call | tf_op jit(solution)/shard_map/pallas_call | solution.py:1384
  254.6 1.2 slice_bitcast_fusion.3
  255.8 1.5 slice_bitcast_fusion

commit v3 on v2

--- a/solution.py
+++ b/solution.py
@@ -448,8 +448,18 @@
 WIDE = jnp.float32
 MESH = pl.DeviceIdType.MESH
 VMEM_BYTES = 64 << 20
+WIRES = 192
 ALL2 = pl.ds(0, 2)
+ALL3 = pl.ds(0, 3)
 ALL4 = pl.ds(0, 4)
+ALL16 = pl.ds(0, 16)
+ALL768 = pl.ds(0, 768)
+SHARED = (2, 3, 4, 5)
+
+
+def shares(unit):
+    cut = 384 if unit in SHARED else 512
+    return (pl.ds(0, cut), pl.ds(cut, 768 - cut))
 
 
 def place():
@@ -459,6 +469,19 @@
 
 def device(x, c, y, z):
     return (2 * x + c, 2 * z + y)
+
+
+FORWARD = (
+    0, "prepare", 10, 1, 20, 11, 2, 30, 21, 12, 3, "tokens", 40, 31, 22, 13, 4, 50, 41, 32, 23, 14,
+    "memory", 60, 51, 42, 33, 24, 70, 61, 52, 43, 34, 25, "self", 71, 62, 53, 44, 35, 72, "project",
+    63, "cross", 54, 45, 73, 55, "feed1", "feed2", 64, 74,
+)
+BACKWARD = (
+    "slopes", 60, 70, "inner4", 61, 40, "inner5", 50, 41, 51, 71, "inner", "norm2", "cross",
+    "grads2", 20, 30, 42, 52, 62, 72, "inputs2", "norm1", 21, 31, "home", "self", "grads1", 0, 10,
+    22, 32, "v", "vy", "inputs1", 63, 73, 1, 11, 43, 53, "vx", 23, 33, 44, 54, "vp", 24, 2, 34,
+    "vm", 12, 3, 13,
+)
 
 
 class Peers:
@@ -469,7 +492,12 @@
         self.across_x = device(1 - x, c, y, z)
         self.across_y = device(x, c, 1 - y, z)
         self.sibling = device(x, 1 - c, y, z)
-        self.along_z = [device(x, c, y, lax.rem(z + k, 4)) for k in (1, 2, 3)]
+        odd = lax.rem(z, 2)
+        self.twin = z + 1 - 2 * odd
+        self.share_z = pl.ds(2 * odd, 2)
+        self.twin_share_z = pl.ds(2 - 2 * odd, 2)
+        self.across_z = device(x, c, y, 3 - z)
+        self.beside_z = device(x, c, y, self.twin)
         self.s = s
         self.after = (b, lax.rem(s + 1, 8))
         self.before = (b, lax.rem(s + 7, 8))
@@ -480,7 +508,7 @@
     def greet(self):
         barrier = pltpu.get_barrier_semaphore()
         always = [
-            self.across_x, self.across_y, self.sibling, *self.along_z, self.after, self.before, self.mirror,
+            self.across_x, self.across_y, self.across_z, self.beside_z, self.sibling, self.after, self.before, self.mirror,
         ]
         for peer in always:
             pl.semaphore_signal(barrier, inc=1, device_id=peer, device_id_type=MESH)
@@ -492,7 +520,7 @@
     def meet(self):
         barrier = pltpu.get_barrier_semaphore()
         others = [jnp.where(alone, 0, 1) for alone in self.alone]
-        pl.semaphore_wait(barrier, 9 + others[0] + others[1])
+        pl.semaphore_wait(barrier, 8 + others[0] + others[1])
 
 
 class Wires:
@@ -501,6 +529,7 @@
 
     def copies(self, pairs, target):
         made = []
+        assert self.used + len(pairs) <= WIRES
         for source, landing in pairs:
             made.append(
                 pltpu.make_async_remote_copy(
@@ -532,66 +561,56 @@
 
 
 class Gather:
-    def __init__(self, peers, wires, mats, pool, outer, vectors):
+    def __init__(self, peers, wires, held, outer, vectors):
         self.peers, self.wires = peers, wires
-        self.mats, self.pool, self.outer, self.vectors = mats, pool, outer, vectors
+        self.held, self.outer, self.vectors = held, outer, vectors
         self.steps = [{} for _ in range(8)]
 
-    def parts(self, unit, x, c, z, y):
+    def parts(self, unit, x, c, z, y, columns=ALL768):
         both = y is None
         if unit >= 6:
             rows = pl.ds(48 * (unit - 6), 48)
-            return [self.outer.at[x, c, z, ALL2 if both else y, rows]]
-        mats = pl.ds(2 * unit, 2)
-        if both:
-            refs = [self.mats.at[mats, x, c, z, pl.ds(0, 16)], self.mats.at[mats, x, c, z, pl.ds(32, 16)]]
-        else:
-            refs = [self.mats.at[mats, x, c, z, pl.ds(pl.multiple_of(32 * y, 16), 16)]]
-        depth = pl.ds(4 * c, 4) if z is ALL4 else 4 * c + z
-        side = 2 * (unit % 2)
-        refs.append(self.pool.at[depth, x, pl.ds(side, 2) if both else side + y, unit // 2])
-        if unit == 0:
+            return [self.outer.at[x, c, z, ALL2 if both else y, rows, columns]]
+        refs = [self.held.at[2 * unit + c, x, z, ALL2 if both else y, ALL3, ALL16, columns]]
+        if unit == 0 and columns.start == 0:
             refs.append(self.vectors.at[x, c, z, ALL2 if both else y])
         return refs
 
-    def send(self, unit, name, spot, target):
-        pairs = [(part, part) for part in self.parts(unit, *spot)]
-        copies = self.wires.copies(pairs, target)
-        start(copies)
-        self.steps[unit][name] = copies
-
-    def z_start(self, unit):
+    def send(self, unit, k, routes):
+        made = []
+        for target, spot in routes:
+            pairs = [(part, part) for part in self.parts(unit, *spot)]
+            made += self.wires.copies(pairs, target)
+        start(made)
+        self.steps[unit][k] = made
+
+    def hop(self, unit, k):
         p = self.peers
-        for k, peer in enumerate(p.along_z):
-            self.send(unit, ("z", k), (p.x, p.c, p.z, p.y), peer)
-
-    def first(self, unit):
-        p = self.peers
-        for k in range(3):
-            landed(self.steps[unit]["z", k])
-        self.send(unit, "first", (p.x, p.c, ALL4, p.y), p.across_y if unit % 2 else p.across_x)
-
-    def second(self, unit):
-        p = self.peers
-        landed(self.steps[unit]["first"])
-        if unit % 2:
-            self.send(unit, "second", (p.x, p.c, ALL4, None), p.across_x)
-            self.send(unit, "near", (p.x, p.c, ALL4, None), p.sibling)
+        x, c, y, z = p.x, p.c, p.y, p.z
+        if k > 0:
+            landed(self.steps[unit][k - 1])
+        if k == 0:
+            self.send(unit, 0, [(p.across_z, (x, c, z, y))])
+        elif k == 1:
+            self.send(unit, 1, [(p.beside_z, (x, c, z, y)), (p.beside_z, (x, c, 3 - z, y))])
+        elif k == 2:
+            column = (x, c, ALL4, y)
+            self.send(unit, 2, [(p.across_x, column), (p.across_y, column)])
+        elif k == 3:
+            over_x, over_y = shares(unit)
+            depth = p.share_z if unit in SHARED else ALL4
+            routes = [(p.across_x, (x, c, depth, 1 - y, over_x))]
+            routes += [(p.across_y, (1 - x, c, depth, y, over_y))]
+            self.send(unit, 3, routes)
+            self.send(unit, 6, [(p.sibling, (x, c, ALL4, None)), (p.sibling, (1 - x, c, ALL4, y))])
+        elif k == 4 and unit in SHARED:
+            self.send(unit, 4, [(p.beside_z, (1 - x, c, p.share_z, 1 - y))])
         else:
-            self.send(unit, "second", (ALL2, p.c, ALL4, p.y), p.across_y)
-            self.send(unit, "near", (ALL2, p.c, ALL4, p.y), p.sibling)
-
-    def third(self, unit):
-        p = self.peers
-        landed(self.steps[unit]["second"])
-        if unit % 2:
-            self.send(unit, "far", (1 - p.x, p.c, ALL4, None), p.sibling)
-        else:
-            self.send(unit, "far", (ALL2, p.c, ALL4, 1 - p.y), p.sibling)
+            self.send(unit, 5, [(p.sibling, (1 - x, c, ALL4, 1 - y))])
 
     def last(self, unit):
-        landed(self.steps[unit]["near"])
-        landed(self.steps[unit]["far"])
+        landed(self.steps[unit][5])
+        landed(self.steps[unit][6])
 
     def close(self, units):
         for unit in units:
@@ -599,12 +618,8 @@
                 sent(copies)
 
 
-def gather_pack(unit, peers, squares, inner, outer, mats, pool, whole_outer):
+def gather_pack(unit, peers, squares, inner, held):
     x, c, y, z = peers.x, peers.c, peers.y, peers.z
-    if unit >= 6:
-        half = slice(48 * (unit - 6), 48 * (unit - 6) + 48)
-        whole_outer[x, c, z, y, half] = outer[half]
-        return
     rests = []
     for k in range(2):
         m = 2 * unit + k
@@ -612,8 +627,8 @@
         values = values.astype(WIDE)
         body = jnp.where(y == 0, values[0:16], values[8:24])
         rests.append(jnp.where(y == 0, values[16:24], values[0:8]))
-        mats[m, x, c, z, pl.ds(pl.multiple_of(32 * y, 16), 16), :] = body.astype(LOW)
-    pool[4 * c + z, x, 2 * (unit % 2) + y, unit // 2] = jnp.concatenate(rests, axis=0).astype(LOW)
+        held[2 * unit + c, x, z, y, k] = body.astype(LOW)
+    held[2 * unit + c, x, z, y, 2] = jnp.concatenate(rests, axis=0).astype(LOW)
 
 
 def gather_vectors(peers, smalls, board, vectors):
@@ -629,18 +644,17 @@
     vectors[peers.x, peers.c, peers.z, peers.y] = rolled
 
 
-def merge_rests(unit, mats, pool):
+def assemble(unit, held, mats):
     def one(step, carry):
         x, c, z = lax.div(step, 8), lax.rem(lax.div(step, 4), 2), lax.rem(step, 4)
-        side = 2 * (unit % 2)
-        low_half = pool[4 * c + z, x, side, unit // 2].astype(WIDE)
-        high_half = pool[4 * c + z, x, side + 1, unit // 2].astype(WIDE)
-        mats[2 * unit, x, c, z, 16:32, :] = jnp.concatenate(
-            [low_half[0:8], high_half[0:8]], axis=0
-        ).astype(LOW)
-        mats[2 * unit + 1, x, c, z, 16:32, :] = jnp.concatenate(
-            [low_half[8:16], high_half[8:16]], axis=0
-        ).astype(LOW)
+        low_half = held[2 * unit + c, x, z, 0, 2].astype(WIDE)
+        high_half = held[2 * unit + c, x, z, 1, 2].astype(WIDE)
+        for k in range(2):
+            part = slice(8 * k, 8 * k + 8)
+            middle = jnp.concatenate([low_half[part], high_half[part]], axis=0)
+            mats[2 * unit + k, x, c, z, 0:16, :] = held[2 * unit + c, x, z, 0, k]
+            mats[2 * unit + k, x, c, z, 16:32, :] = middle.astype(LOW)
+            mats[2 * unit + k, x, c, z, 32:48, :] = held[2 * unit + c, x, z, 1, k]
         return carry
 
     lax.fori_loop(0, 16, one, 0)
@@ -793,10 +807,11 @@
 class Grads:
     ORDER = (6, 7, 4, 5, 2, 3, 0, 1)
 
-    def __init__(self, peers, wires, held, r0, pool, r2, out, mine, credit):
+    def __init__(self, peers, wires, held, r0, shared, pool, r2, r3, out, mine, credit, move):
         self.peers, self.wires, self.held = peers, wires, held
-        self.r0, self.pool, self.r2, self.out = r0, pool, r2, out
-        self.mine, self.credit = mine, credit
+        self.r0, self.pool, self.r2, self.r3, self.out = r0, pool, r2, r3, out
+        self.shared, self.mine, self.credit, self.move = shared, mine, credit, move
+        self.kept = []
         self.stage = {}
         self.open = []
         self.first_sends = {}
@@ -828,63 +843,66 @@
         self.first_sends[unit] = copies
         self.stage[unit] = copies
 
-    def step1(self, unit):
+    def corner(self, unit, depth):
+        p, landing = self.peers, self.r2.at[unit, pl.ds(0, depth.size)]
+        self.stage[unit] = []
+        for columns, target in zip(shares(unit), (p.across_x, p.across_y)):
+            source = self.held.at[unit, 1 - p.x, depth, 1 - p.y, ALL3, ALL16, columns]
+            self.stage[unit] += self.ship([(source, landing.at[:, :, :, columns])], target)
+
+    def hop(self, unit, k):
         p, held = self.peers, self.held
+        x, y, z = p.x, p.y, p.z
         landed(self.stage[unit])
-        turn = self.at(unit)
-        ring = turn % 4
-
-        def add(i, carry):
-            j, k = lax.div(i, 4), lax.rem(i, 4)
-            held[unit, j, k] = held[unit, j, k] + self.r0[ring, j, k]
-            return carry
-
-        lax.fori_loop(0, 8, add, 0)
-        if turn < 4:
-            pl.semaphore_signal(self.credit, inc=1, device_id=p.sibling, device_id_type=MESH)
-        if unit % 2:
-            pairs = [(held.at[unit, 1 - p.x, ALL4, k], self.pool.at[unit, k]) for k in range(2)]
+        if k == 0:
+            turn = self.at(unit)
+            ring = turn % 4
+
+            def add(i, carry):
+                j, d = lax.div(i, 4), lax.rem(i, 4)
+                held[unit, j, d] = held[unit, j, d] + self.r0[ring, j, d]
+                return carry
+
+            lax.fori_loop(0, 8, add, 0)
+            if turn < 4:
+                pl.semaphore_signal(self.credit, inc=1, device_id=p.sibling, device_id_type=MESH)
+            if unit in SHARED:
+                pairs = [(held.at[unit, 1 - x, p.twin_share_z, 1 - y], self.shared.at[unit - SHARED[0]])]
+                self.stage[unit] = self.ship(pairs, p.beside_z)
+            else:
+                self.corner(unit, ALL4)
+        elif k == 0.5:
+            for i in range(2):
+                d = p.share_z.start + i
+                block = held[unit, 1 - x, d, 1 - y] + self.shared[unit - SHARED[0], i]
+                held[unit, 1 - x, d, 1 - y] = block
+            self.corner(unit, p.share_z)
+        elif k == 1:
+            over_x, over_y = shares(unit)
+            depth = p.share_z if unit in SHARED else ALL4
+            for i in range(depth.size):
+                d = depth.start + i
+                here = (unit, x, d, 1 - y, ALL3, ALL16, over_x)
+                held[here] = held[here] + self.r2[unit, i, :, :, over_x]
+                here = (unit, 1 - x, d, y, ALL3, ALL16, over_y)
+                held[here] = held[here] + self.r2[unit, i, :, :, over_y]
+            pairs = [(held.at[unit, 1 - x, ALL4, y], self.pool.at[unit, 0])]
             self.stage[unit] = self.ship(pairs, p.across_x)
+            pairs = [(held.at[unit, x, ALL4, 1 - y], self.pool.at[unit, 1])]
+            self.stage[unit] += self.ship(pairs, p.across_y)
+        elif k == 2:
+            for d in range(4):
+                total = held[unit, x, d, y].astype(WIDE) + self.pool[unit, 0, d].astype(WIDE)
+                held[unit, x, d, y] = (total + self.pool[unit, 1, d].astype(WIDE)).astype(LOW)
+            pairs = [(held.at[unit, x, d, y], self.r3.at[unit, i]) for i, d in enumerate((p.twin, 3 - p.twin))]
+            self.stage[unit] = self.ship(pairs, p.beside_z)
         else:
-            pairs = [(held.at[unit, ALL2, ALL4, 1 - p.y], self.pool.at[unit])]
-            self.stage[unit] = self.ship(pairs, p.across_y)
-
-    def step2(self, unit):
-        p, held = self.peers, self.held
-        landed(self.stage[unit])
-
-        def add(i, carry):
-            if unit % 2:
-                for k in range(2):
-                    held[unit, p.x, i, k] = held[unit, p.x, i, k] + self.pool[unit, k, i]
-            else:
-                for j in range(2):
-                    held[unit, j, i, p.y] = held[unit, j, i, p.y] + self.pool[unit, j, i]
-            return carry
-
-        lax.fori_loop(0, 4, add, 0)
-        if unit % 2:
-            pairs = [(held.at[unit, p.x, ALL4, 1 - p.y], self.r2.at[unit])]
-            self.stage[unit] = self.ship(pairs, p.across_y)
-        else:
-            pairs = [(held.at[unit, 1 - p.x, ALL4, p.y], self.r2.at[unit])]
-            self.stage[unit] = self.ship(pairs, p.across_x)
-
-    def step3(self, unit):
-        p, held = self.peers, self.held
-        landed(self.stage[unit])
-
-        def add(i, carry):
-            held[unit, p.x, i, p.y] = held[unit, p.x, i, p.y] + self.r2[unit, i]
-            return carry
-
-        lax.fori_loop(0, 4, add, 0)
-        copies = []
-        for k in (1, 2, 3):
-            source = held.at[unit, p.x, lax.rem(p.z + k, 4), p.y]
-            copies += self.ship([(source, self.out.at[unit, k - 1])], p.along_z[k - 1])
-        self.stage[unit] = copies
-        self.mine[unit] = held[unit, p.x, p.z, p.y]
+            for i, d in enumerate((z, 3 - z)):
+                held[unit, x, d, y] = held[unit, x, d, y] + self.r3[unit, i]
+            pairs = [(held.at[unit, x, 3 - z, y], self.out.at[unit])]
+            self.stage[unit] = self.ship(pairs, p.across_z)
+            self.kept.append(self.move(held.at[unit, x, z, y], self.mine.at[unit]))
+            start(self.kept[-1:])
 
     def finish(self):
         for unit in self.ORDER:
@@ -892,6 +910,8 @@
         for copies in self.first_sends.values():
             sent(copies)
         sent(self.open)
+        for copy in self.kept:
+            copy.wait()
 
     def pair_grad(self, unit, first_left, first_right, second_left, second_right):
         self.ready(unit)
@@ -935,128 +955,147 @@
 
 
 def layer_kernel(*refs):
-    squares, inner_own, outer_own, smalls = refs[0:8], refs[8], refs[9], refs[10:24]
-    tokens_own, memory_own, cotangent, target_ids, source_ids = refs[24:29]
+    squares_in, inner_in, outer_in, smalls_in = refs[0:8], refs[8], refs[9], refs[10:24]
+    tokens_in, memory_in, cotangent_in, target_in, source_in = refs[24:29]
     output, out, mine, vout, left_out, memory_out, tokens_part = refs[29:36]
+    squares, inner_own, smalls, refs = refs[36:44], refs[44], refs[45:59], refs[59:]
     (
+        cotangent, target_ids, source_ids, output_low, tokens_sum,
         mats, outer, vectors, tokens, memory, board, mask_self, mask_cross,
         vec, inner_bias, query, key, value, probs, context, unit1, first_low,
         query2, key2, value2, probs2, context2, unit2, second_low,
         hidden, slope, total, grad, branch, upstream, dquery, dkey, dvalue,
         gvec, ginner,
-        held, r0, pool, r2, vheld, v0, v1, v2, left_part, memory_parts,
-        credit, free, send, recv, local,
-    ) = refs[36:]
+        held, r0, shared, pool, r2, r3, vheld, v0, v1, v2, v3, left_part, memory_parts,
+        credit, send, recv, local,
+    ) = refs
     peers = Peers()
     peers.greet()
+    c, x, y, z = peers.c, peers.x, peers.y, peers.z
     wires = Wires(send, recv)
-    weights = Gather(peers, wires, mats, pool, outer, vectors)
-    grads = Grads(peers, wires, held, r0, pool, r2, out, mine, credit)
+    weights = Gather(peers, wires, held, outer, vectors)
+    moves = []
+
+    def move(source, target):
+        copy = pltpu.make_async_copy(source, target, local.at[len(moves)])
+        moves.append(copy)
+        return copy
+
+    grads = Grads(peers, wires, held, r0, shared, pool, r2, r3, out, mine, credit, move)
     own = slice(128, 256)
+    early = [move(a, b) for a, b in zip(squares_in[0:2], squares[0:2])]
+    early += [move(a, b) for a, b in zip(smalls_in, smalls)]
+    loads = [move(a, b) for a, b in zip(squares_in[2:], squares[2:])]
+    loads += [move(inner_in, inner_own), move(outer_in, outer.at[x, c, z, y])]
+    loads += [move(target_in, target_ids), move(source_in, source_ids)]
+    loads += [move(tokens_in, tokens.at[pl.ds(128, 128)]), move(cotangent_in, cotangent)]
+    start(early + loads)
+    state = {}
+
+    def reduce_hop(unit, k):
+        grads.hop(unit, (0, 0.5, 1, 2, 3)[k] if unit in SHARED else k)
+
+    def follow(plan, hop, chunks):
+        for step in plan:
+            if step in chunks:
+                chunks[step]()
+            else:
+                hop(step // 10, step % 10)
+
+    def vector(j):
+        return vec[j : j + 1, :]
 
     def pack(unit):
-        gather_pack(unit, peers, squares, inner_own, outer_own, mats, pool, outer)
-
-    pack(0)
-    gather_vectors(peers, smalls, board, vectors)
-    peers.meet()
-    weights.z_start(0)
-    pack(1)
-    weights.z_start(1)
-    tokens[own, :] = tokens_own[...]
-    left = wires.copies([(tokens_own, tokens.at[pl.ds(0, 128)])], peers.after)
-    mirrored = wires.copies([(memory_own, memory.at[pl.ds(128, 128)])], peers.mirror)
-    start(left + mirrored)
-    folds = [
-        wires.copies([(memory_own, memory.at[pl.ds(256 * k, 128)])], peers.folds[k]) for k in range(2)
-    ]
-    for k in range(2):
-        @pl.when(jnp.logical_not(peers.alone[k]))
-        def _():
-            start(folds[k])
-
-        @pl.when(peers.alone[k])
-        def _():
-            memory[pl.ds(256 * k, 128), :] = memory_own[...]
-
-    for unit in range(2, 8):
-        pack(unit)
-    fill_masks(peers, target_ids, source_ids, mask_self, mask_cross)
-
-    def turn(t):
-        if t < 4:
-            weights.first(2 * t)
-            weights.first(2 * t + 1)
-            if t < 3:
-                weights.z_start(2 * t + 2)
-                weights.z_start(2 * t + 3)
-        if 1 <= t < 5:
-            weights.second(2 * t - 2)
-            weights.second(2 * t - 1)
-        if t >= 2:
-            weights.third(2 * t - 4)
-            weights.third(2 * t - 3)
-
-    def arrive(pair):
-        for unit in (2 * pair, 2 * pair + 1):
+        gather_pack(unit, peers, squares, inner_own, held)
+
+    def arrive(*units):
+        for unit in units:
             weights.last(unit)
             if unit < 6:
-                merge_rests(unit, mats, pool)
-
-    def vector(j):
-        return vec[j : j + 1, :]
-
-    turn(0)
-    turn(1)
-    turn(2)
-    arrive(0)
-    unpack_vectors(vectors, vec, inner_bias)
-    landed(left)
-    for n in range(3):
-        s = strip(n)
-        query[:, s] = (dot(tokens[own, :], columns(mats, 0, n)) + vec[0:1, s]).astype(LOW)
-        key[:, s] = dot(tokens[...], columns(mats, 1, n)).astype(LOW)
-        value[:, s] = (dot(tokens[...], columns(mats, 2, n)) + vec[1:2, s]).astype(LOW)
-    attention(query, key, value, mask_self, probs, context)
-    for n in range(3):
-        s = strip(n)
-        total[:, s] = (
-            tokens[own, s].astype(WIDE) + dot(context[...], columns(mats, 3, n)) + vec[2:3, s]
-        )
-    unit, scale1 = centered(total[...])
-    unit1[...] = unit
-    first = unit * vector(3) + vector(4)
-    total[...] = first
-    first_low[...] = first.astype(LOW)
-    turn(3)
-    arrive(1)
-    landed(mirrored)
-    for k in range(2):
-        @pl.when(jnp.logical_not(peers.alone[k]))
-        def _():
-            landed(folds[k])
-            sent(folds[k])
-
-    for n in range(3):
-        s = strip(n)
-        query2[:, s] = (dot(first_low[...], columns(mats, 4, n)) + vec[5:6, s]).astype(LOW)
-        key2[:, s] = dot(memory[...], columns(mats, 5, n)).astype(LOW)
-        value2[:, s] = (dot(memory[...], columns(mats, 6, n)) + vec[6:7, s]).astype(LOW)
-    attention(query2, key2, value2, mask_cross, probs2, context2)
-    for n in range(3):
-        s = strip(n)
-        total[:, s] = total[:, s] + dot(context2[...], columns(mats, 7, n)) + vec[7:8, s]
-    unit, scale2 = centered(total[...])
-    unit2[...] = unit
-    second = unit * vector(8) + vector(9)
-    total[...] = second + vector(10)
-    second_low[...] = second.astype(LOW)
-    turn(4)
-    arrive(2)
-    weights.close(range(6))
-    for peer in (peers.across_x, peers.across_y):
-        pl.semaphore_signal(free, inc=1, device_id=peer, device_id_type=MESH)
-    for j in range(4):
+                assemble(unit, held, mats)
+
+    left = wires.copies([(tokens_in, tokens.at[pl.ds(0, 128)])], peers.after)
+    mirrored = wires.copies([(memory_in, memory.at[pl.ds(128, 128)])], peers.mirror)
+    folds = [
+        wires.copies([(memory_in, memory.at[pl.ds(256 * k, 128)])], peers.folds[k]) for k in range(2)
+    ]
+    kept = [move(memory_in, memory.at[pl.ds(256 * k, 128)]) for k in range(2)]
+
+    def prepare():
+        for copy in loads:
+            copy.wait()
+        for unit in range(1, 6):
+            pack(unit)
+        fill_masks(peers, target_ids, source_ids, mask_self, mask_cross)
+
+    def exchange_tokens():
+        start(left)
+
+    def exchange_memory():
+        start(mirrored)
+        for k in range(2):
+            @pl.when(jnp.logical_not(peers.alone[k]))
+            def _():
+                start(folds[k])
+
+            @pl.when(peers.alone[k])
+            def _():
+                kept[k].start()
+
+    def self_attention():
+        arrive(0, 1)
+        unpack_vectors(vectors, vec, inner_bias)
+        landed(left)
+        for n in range(3):
+            s = strip(n)
+            query[:, s] = (dot(tokens[own, :], columns(mats, 0, n)) + vec[0:1, s]).astype(LOW)
+            key[:, s] = dot(tokens[...], columns(mats, 1, n)).astype(LOW)
+            value[:, s] = (dot(tokens[...], columns(mats, 2, n)) + vec[1:2, s]).astype(LOW)
+        attention(query, key, value, mask_self, probs, context)
+        for n in range(3):
+            s = strip(n)
+            total[:, s] = (
+                tokens[own, s].astype(WIDE) + dot(context[...], columns(mats, 3, n)) + vec[2:3, s]
+            )
+        unit, state[1] = centered(total[...])
+        unit1[...] = unit
+        first = unit * vector(3) + vector(4)
+        total[...] = first
+        first_low[...] = first.astype(LOW)
+
+    def cross_projections():
+        arrive(2, 3)
+        for n in range(3):
+            s = strip(n)
+            query2[:, s] = (dot(first_low[...], columns(mats, 4, n)) + vec[5:6, s]).astype(LOW)
+        landed(mirrored)
+        for k in range(2):
+            @pl.when(jnp.logical_not(peers.alone[k]))
+            def _():
+                landed(folds[k])
+                sent(folds[k])
+
+            @pl.when(peers.alone[k])
+            def _():
+                kept[k].wait()
+
+        for n in range(3):
+            s = strip(n)
+            key2[:, s] = dot(memory[...], columns(mats, 5, n)).astype(LOW)
+            value2[:, s] = (dot(memory[...], columns(mats, 6, n)) + vec[6:7, s]).astype(LOW)
+
+    def cross_attention():
+        attention(query2, key2, value2, mask_cross, probs2, context2)
+        for n in range(3):
+            s = strip(n)
+            total[:, s] = total[:, s] + dot(context2[...], columns(mats, 7, n)) + vec[7:8, s]
+        unit, state[2] = centered(total[...])
+        unit2[...] = unit
+        second = unit * vector(8) + vector(9)
+        total[...] = second + vector(10)
+        second_low[...] = second.astype(LOW)
+
+    def feed(j):
         for n in range(3):
             s = slice(768 * j + 256 * n, 768 * j + 256 * n + 256)
             pre = dot(second_low[...], columns(mats, 8 + j, n)) + inner_bias[0:1, s]
@@ -1065,10 +1104,35 @@
             slope[:, s] = (
                 normal + pre * (0.3989422804014327 * jnp.exp(-0.5 * pre * pre))
             ).astype(LOW)
-    turn(5)
-    arrive(3)
-    weights.close(range(6, 8))
-    sent(left + mirrored)
+
+    def feed_one():
+        arrive(4)
+        feed(0)
+        feed(1)
+
+    def feed_two():
+        arrive(5)
+        feed(2)
+        feed(3)
+        weights.close(range(6))
+
+    forward = {
+        "prepare": prepare,
+        "tokens": exchange_tokens,
+        "memory": exchange_memory,
+        "self": self_attention,
+        "project": cross_projections,
+        "cross": cross_attention,
+        "feed1": feed_one,
+        "feed2": feed_two,
+    }
+    for copy in early:
+        copy.wait()
+    pack(0)
+    gather_vectors(peers, smalls, board, vectors)
+    peers.meet()
+    follow(FORWARD, weights.hop, forward)
+    arrive(6, 7)
     for n in range(3):
         s = strip(n)
         summed = total[:, s]
@@ -1077,147 +1141,183 @@
             summed = summed + dot(hidden[:, here], outer_columns(outer, j, n))
         total[:, s] = summed
     unit, scale3 = centered(total[...])
-    output[...] = (unit * vector(11) + vector(12)).astype(LOW)
     arrived = cotangent[...].astype(WIDE)
-    gvec[11:12, :] = total_rows(arrived * unit)
-    gvec[12:13, :] = total_rows(arrived)
     dhidden = norm_grad(unit, scale3, vector(11), arrived)
     grad[...] = dhidden
     branch[...] = dhidden.astype(LOW)
-    gvec[10:11, :] = total_rows(branch[...])
     grads.outer_grad(hidden, branch)
     grads.step0(6)
     grads.step0(7)
-    for j in range(4):
-        for half in range(2):
-            s = slice(768 * j + 384 * half, 768 * j + 384 * half + 384)
-            raised = dot_nt(branch[...], outer_rows(outer, j, half)) * slope[:, s].astype(WIDE)
-            raised = raised.astype(LOW)
-            slope[:, s] = raised
-            ginner[0:1, s] = total_rows(raised)
-    for unit in (4, 5):
-        spans_of = [slope.at[:, pl.ds(768 * j, 768)] for j in (2 * unit - 8, 2 * unit - 7)]
-        grads.pair_grad(unit, second_low, spans_of[0], second_low, spans_of[1])
+    output_low[...] = (unit * vector(11) + vector(12)).astype(LOW)
+    ends = [move(output_low, output)]
+    start(ends)
+    gvec[11:12, :] = total_rows(arrived * unit)
+    gvec[12:13, :] = total_rows(arrived)
+    gvec[10:11, :] = total_rows(branch[...])
+    weights.close(range(6, 8))
+    sent(left + mirrored)
+
+    def slopes():
+        for j in range(4):
+            for half in range(2):
+                s = slice(768 * j + 384 * half, 768 * j + 384 * half + 384)
+                raised = dot_nt(branch[...], outer_rows(outer, j, half)) * slope[:, s].astype(WIDE)
+                raised = raised.astype(LOW)
+                slope[:, s] = raised
+                ginner[0:1, s] = total_rows(raised)
+
+    def inner_grad(unit):
+        one, two = [slope.at[:, pl.ds(768 * j, 768)] for j in (2 * unit - 8, 2 * unit - 7)]
+        grads.pair_grad(unit, second_low, one, second_low, two)
         grads.step0(unit)
-    for x in range(2):
-        s = slice(384 * x, 384 * x + 384)
-        summed = grad[:, s]
-        for j in range(4):
-            summed = summed + dot_nt(slope[:, 768 * j : 768 * j + 768], rows(mats, 8 + j, x))
-        grad[:, s] = summed
-    pl.semaphore_wait(free, 2)
-    grads.step1(6)
-    grads.step1(7)
-    arrived = grad[...]
-    unit = unit2[...]
-    gvec[8:9, :] = total_rows(arrived * unit)
-    gvec[9:10, :] = total_rows(arrived)
-    dhidden = norm_grad(unit, scale2, vector(8), arrived)
-    grad[...] = dhidden
-    branch[...] = dhidden.astype(LOW)
-    gvec[7:8, :] = total_rows(branch[...])
-    for x in range(2):
-        upstream[:, 384 * x : 384 * x + 384] = dot_nt(branch[...], rows(mats, 7, x)).astype(LOW)
-    grads.step1(4)
-    grads.step1(5)
-    attention_back(query2, key2, value2, upstream, probs2, dquery, dkey, dvalue, 384)
-    grads.step2(6)
-    grads.step2(7)
-    gvec[5:6, :] = total_rows(dquery[...])
-    gvec[6:7, :] = total_rows(dvalue[...])
-    for x in range(2):
-        s = slice(384 * x, 384 * x + 384)
-        grad[:, s] = grad[:, s] + dot_nt(dquery[...], rows(mats, 4, x))
-        backed = dot_nt(dkey[...], rows(mats, 5, x)) + dot_nt(dvalue[...], rows(mats, 6, x))
-        for block in range(3):
-            memory_parts[block, :, s] = backed[128 * block : 128 * block + 128].astype(LOW)
-    home = grads.ship([(memory_parts.at[1], memory_out.at[1])], peers.mirror)
+
+    def inner_back():
+        for x in range(2):
+            s = slice(384 * x, 384 * x + 384)
+            summed = grad[:, s]
+            for j in range(4):
+                summed = summed + dot_nt(slope[:, 768 * j : 768 * j + 768], rows(mats, 8 + j, x))
+            grad[:, s] = summed
+
+    def norm_back_at(held_unit, scale, gain, gain_row):
+        arrived = grad[...]
+        unit = held_unit[...]
+        gvec[gain_row : gain_row + 1, :] = total_rows(arrived * unit)
+        gvec[gain_row + 1 : gain_row + 2, :] = total_rows(arrived)
+        dhidden = norm_grad(unit, scale, gain, arrived)
+        grad[...] = dhidden
+        branch[...] = dhidden.astype(LOW)
+        gvec[gain_row - 1 : gain_row, :] = total_rows(branch[...])
+
+    def cross_norm():
+        norm_back_at(unit2, state[2], vector(8), 8)
+        for x in range(2):
+            upstream[:, 384 * x : 384 * x + 384] = dot_nt(branch[...], rows(mats, 7, x)).astype(LOW)
+
+    def cross_back():
+        attention_back(query2, key2, value2, upstream, probs2, dquery, dkey, dvalue, 384)
+
+    def cross_grads():
+        grads.pair_grad(2, first_low, dquery, memory, dkey)
+        grads.step0(2)
+        grads.pair_grad(3, memory, dvalue, context2, branch)
+        grads.step0(3)
+
+    def cross_inputs():
+        gvec[5:6, :] = total_rows(dquery[...])
+        gvec[6:7, :] = total_rows(dvalue[...])
+        for x in range(2):
+            s = slice(384 * x, 384 * x + 384)
+            grad[:, s] = grad[:, s] + dot_nt(dquery[...], rows(mats, 4, x))
+            backed = dot_nt(dkey[...], rows(mats, 5, x)) + dot_nt(dvalue[...], rows(mats, 6, x))
+            for block in range(3):
+                memory_parts[block, :, s] = backed[128 * block : 128 * block + 128].astype(LOW)
+
     back = [
         wires.copies([(memory_parts.at[2 * k], memory_out.at[2 * k])], peers.folds[k]) for k in range(2)
     ]
     stay = [
-        pltpu.make_async_copy(memory_parts.at[2 * k], memory_out.at[2 * k], local.at[k]) for k in range(2)
+        move(memory_parts.at[2 * k], memory_out.at[2 * k]) for k in range(2)
     ]
-    for k in range(2):
-        @pl.when(jnp.logical_not(peers.alone[k]))
-        def _():
-            start(back[k])
-
-        @pl.when(peers.alone[k])
-        def _():
-            stay[k].start()
-
-    grads.pair_grad(2, first_low, dquery, memory, dkey)
-    grads.step0(2)
-    grads.pair_grad(3, memory, dvalue, context2, branch)
-    grads.step0(3)
-    grads.step2(4)
-    grads.step2(5)
-    grads.step3(6)
-    grads.step3(7)
-    arrived = grad[...]
-    unit = unit1[...]
-    gvec[3:4, :] = total_rows(arrived * unit)
-    gvec[4:5, :] = total_rows(arrived)
-    dhidden = norm_grad(unit, scale1, vector(3), arrived)
-    grad[...] = dhidden
-    branch[...] = dhidden.astype(LOW)
-    gvec[2:3, :] = total_rows(branch[...])
-    for x in range(2):
-        upstream[:, 384 * x : 384 * x + 384] = dot_nt(branch[...], rows(mats, 3, x)).astype(LOW)
-    grads.step1(2)
-    grads.step1(3)
-    attention_back(query, key, value, upstream, probs, dquery, dkey, dvalue, 256)
+
+    def memory_home():
+        state["home"] = grads.ship([(memory_parts.at[1], memory_out.at[1])], peers.mirror)
+        for k in range(2):
+            @pl.when(jnp.logical_not(peers.alone[k]))
+            def _():
+                start(back[k])
+
+            @pl.when(peers.alone[k])
+            def _():
+                stay[k].start()
+
+    def self_norm():
+        norm_back_at(unit1, state[1], vector(3), 3)
+        for x in range(2):
+            upstream[:, 384 * x : 384 * x + 384] = dot_nt(branch[...], rows(mats, 3, x)).astype(LOW)
+
     dkey_two, dvalue_two = dkey.at[pl.ds(0, 256)], dvalue.at[pl.ds(0, 256)]
-    grads.pair_grad(0, tokens.at[pl.ds(128, 128)], dquery, tokens, dkey_two)
-    grads.step0(0)
-    grads.pair_grad(1, tokens, dvalue_two, context, branch)
-    grads.step0(1)
-    gvec[0:1, :] = total_rows(dquery[...])
-    gvec[1:2, :] = total_rows(dvalue_two[...])
-    gvec[13:16, :] = jnp.zeros((3, 768), WIDE)
-
-    def put(c, x, z, y, block):
-        vheld[c, x, z, y] = block
-
-    pack_vectors(gvec, ginner, peers.c, put)
-    c, x, y, z = peers.c, peers.x, peers.y, peers.z
-    vstage = grads.ship([(vheld.at[1 - c], v0)], peers.sibling)
-    grads.step3(4)
-    grads.step3(5)
-    grads.step2(2)
-    grads.step2(3)
-    for x_ in range(2):
-        s = slice(384 * x_, 384 * x_ + 384)
-        backed = dot_nt(dkey_two[...], rows(mats, 1, x_)) + dot_nt(dvalue_two[...], rows(mats, 2, x_))
-        left_part[:, s] = backed[0:128].astype(LOW)
-        tokens_part[:, s] = grad[:, s] + dot_nt(dquery[...], rows(mats, 0, x_)) + backed[128:256]
-    left = grads.ship([(left_part, left_out)], peers.before)
-    grads.step1(0)
-    grads.step1(1)
-    landed(vstage)
-    vheld[c] = vheld[c] + v0[...]
-    vstage = grads.ship([(vheld.at[c, ALL2, ALL4, 1 - y], v1)], peers.across_y)
-    grads.step3(2)
-    grads.step3(3)
-    grads.step2(0)
-    grads.step2(1)
-    landed(vstage)
-    for j in range(2):
+
+    def self_back():
+        attention_back(query, key, value, upstream, probs, dquery, dkey, dvalue, 256)
+
+    def self_grads():
+        grads.pair_grad(0, tokens.at[pl.ds(128, 128)], dquery, tokens, dkey_two)
+        grads.step0(0)
+        grads.pair_grad(1, tokens, dvalue_two, context, branch)
+        grads.step0(1)
+
+    def vectors_near():
+        gvec[0:1, :] = total_rows(dquery[...])
+        gvec[1:2, :] = total_rows(dvalue_two[...])
+        gvec[13:16, :] = jnp.zeros((3, 768), WIDE)
+
+        def put(c, x, z, y, block):
+            vheld[c, x, z, y] = block
+
+        pack_vectors(gvec, ginner, peers.c, put)
+        state["v"] = grads.ship([(vheld.at[1 - c], v0)], peers.sibling)
+
+    def vectors_y():
+        landed(state["v"])
+        vheld[c] = vheld[c] + v0[...]
+        state["v"] = grads.ship([(vheld.at[c, ALL2, ALL4, 1 - y], v1)], peers.across_y)
+
+    def vectors_x():
+        landed(state["v"])
+        for j in range(2):
+            for k in range(4):
+                vheld[c, j, k, y] = vheld[c, j, k, y] + v1[j, k]
+        state["v"] = grads.ship([(vheld.at[c, 1 - x, ALL4, y], v2)], peers.across_x)
+
+    def vectors_p():
+        landed(state["v"])
         for k in range(4):
-            vheld[c, j, k, y] = vheld[c, j, k, y] + v1[j, k]
-    vstage = grads.ship([(vheld.at[c, 1 - x, ALL4, y], v2)], peers.across_x)
-    grads.step3(0)
-    grads.step3(1)
-    landed(vstage)
-    for k in range(4):
-        vheld[c, x, k, y] = vheld[c, x, k, y] + v2[k]
-    vstage = []
-    for k in (1, 2, 3):
-        source = vheld.at[c, x, lax.rem(z + k, 4), y]
-        vstage += grads.ship([(source, vout.at[k])], peers.along_z[k - 1])
-    vout[0] = vheld[c, x, z, y]
-    landed(vstage + left + home)
+            vheld[c, x, k, y] = vheld[c, x, k, y] + v2[k]
+        twin = peers.twin
+        pairs = [(vheld.at[c, x, twin, y], v3.at[0]), (vheld.at[c, x, 3 - twin, y], v3.at[1])]
+        state["v"] = grads.ship(pairs, peers.beside_z)
+
+    def vectors_m():
+        landed(state["v"])
+        vheld[c, x, z, y] = vheld[c, x, z, y] + v3[0]
+        vheld[c, x, 3 - z, y] = vheld[c, x, 3 - z, y] + v3[1]
+        state["v"] = grads.ship([(vheld.at[c, x, 3 - z, y], vout.at[1])], peers.across_z)
+        ends.append(move(vheld.at[c, x, z, y], vout.at[0]))
+        start(ends[-1:])
+
+    def self_inputs():
+        for k in range(2):
+            s = slice(384 * k, 384 * k + 384)
+            backed = dot_nt(dkey_two[...], rows(mats, 1, k)) + dot_nt(dvalue_two[...], rows(mats, 2, k))
+            left_part[:, s] = backed[0:128].astype(LOW)
+            tokens_sum[:, s] = grad[:, s] + dot_nt(dquery[...], rows(mats, 0, k)) + backed[128:256]
+        ends.append(move(tokens_sum, tokens_part))
+        start(ends[-1:])
+        state["left"] = grads.ship([(left_part, left_out)], peers.before)
+
+    backward = {
+        "slopes": slopes,
+        "inner4": partial(inner_grad, 4),
+        "inner5": partial(inner_grad, 5),
+        "inner": inner_back,
+        "norm2": cross_norm,
+        "cross": cross_back,
+        "grads2": cross_grads,
+        "inputs2": cross_inputs,
+        "home": memory_home,
+        "norm1": self_norm,
+        "self": self_back,
+        "grads1": self_grads,
+        "inputs1": self_inputs,
+        "v": vectors_near,
+        "vy": vectors_y,
+        "vx": vectors_x,
+        "vp": vectors_p,
+        "vm": vectors_m,
+    }
+    follow(BACKWARD, reduce_hop, backward)
+    landed(state["v"] + state["left"] + state["home"])
     for k in range(2):
         @pl.when(jnp.logical_not(peers.alone[k]))
         def _():
@@ -1229,6 +1329,8 @@
             stay[k].wait()
 
     grads.finish()
+    for copy in ends:
+        copy.wait()
 
 
 def fill_masks(peers, target_ids, source_ids, mask_self, mask_cross):
@@ -1253,9 +1355,9 @@
 def layer_call(*inputs):
     shapes = [
         jax.ShapeDtypeStruct((128, 768), LOW),
-        jax.ShapeDtypeStruct((8, 3, 3, 16, 768), LOW),
         jax.ShapeDtypeStruct((8, 3, 16, 768), LOW),
-        jax.ShapeDtypeStruct((4, 16, 128), WIDE),
+        jax.ShapeDtypeStruct((8, 3, 16, 768), LOW),
+        jax.ShapeDtypeStruct((2, 16, 128), WIDE),
         jax.ShapeDtypeStruct((128, 768), LOW),
         jax.ShapeDtypeStruct((3, 128, 768), LOW),
         jax.ShapeDtypeStruct((128, 768), WIDE),
@@ -1267,7 +1369,13 @@
     def wide(*shape):
         return pltpu.VMEM(shape, WIDE)
 
-    scratch = [
+    scratch = [low(24, 768)] * 8 + [low(24, 3072)] + [low(1, 24)] * 13 + [low(1, 96)]
+    scratch += [
+        low(128, 768),
+        pltpu.VMEM((1, 1024), jnp.int32),
+        pltpu.VMEM((1, 1024), jnp.int32),
+        low(128, 768),
+        wide(128, 768),
         low(12, 2, 2, 4, 48, 768),
         low(2, 2, 4, 2, 96, 768),
         low(2, 2, 4, 2, 16, 128),
@@ -1305,26 +1413,28 @@
         wide(8, 3072),
         low(12, 2, 4, 2, 3, 16, 768),
         low(4, 2, 4, 2, 3, 16, 768),
+        low(4, 2, 3, 16, 768),
         low(8, 2, 4, 3, 16, 768),
         low(8, 4, 3, 16, 768),
+        low(8, 2, 3, 16, 768),
         wide(2, 2, 4, 2, 16, 128),
         wide(2, 4, 2, 16, 128),
         wide(2, 4, 16, 128),
         wide(4, 16, 128),
+        wide(2, 16, 128),
         low(128, 768),
         low(3, 128, 768),
         pltpu.SemaphoreType.REGULAR,
-        pltpu.SemaphoreType.REGULAR,
-        pltpu.SemaphoreType.DMA((240,)),
-        pltpu.SemaphoreType.DMA((240,)),
-        pltpu.SemaphoreType.DMA((2,)),
+        pltpu.SemaphoreType.DMA((WIRES,)),
+        pltpu.SemaphoreType.DMA((WIRES,)),
+        pltpu.SemaphoreType.DMA((44,)),
     ]
     anywhere = pl.BlockSpec(memory_space=pl.ANY)
     return pl.pallas_call(
         layer_kernel,
         out_shape=shapes,
-        in_specs=[vmem()] * 29,
-        out_specs=[vmem(), anywhere, vmem(), vmem(), anywhere, anywhere, vmem()],
+        in_specs=[anywhere] * 29,
+        out_specs=[anywhere] * 7,
         scratch_shapes=scratch,
         compiler_params=pltpu.CompilerParams(
             collective_id=0, has_side_effects=True, vmem_limit_bytes=VMEM_BYTES
@@ -1333,8 +1443,8 @@
 
 
 def final_kernel(output_low, parts, mine, vparts, left, memory_low, tokens_part, *outs):
-    output, tokens_grad, memory_grad, small = outs[:4]
-    squares, inner, outer = outs[4:12], outs[12], outs[13]
+    output, tokens_grad, memory_grad = outs[:3]
+    squares, inner, outer, smalls = outs[3:11], outs[11], outs[12], outs[13:]
     output[...] = output_low[...]
     b, s = lax.axis_index(BATCH), lax.axis_index(SEQ)
     even = lax.rem(s, 2) == 0
@@ -1345,8 +1455,7 @@
 
     def summed(unit):
         total = (
-            mine[unit].astype(WIDE) + parts[unit, 0].astype(WIDE)
-            + parts[unit, 1].astype(WIDE) + parts[unit, 2].astype(WIDE)
+            mine[unit].astype(WIDE) + parts[unit].astype(WIDE)
         )
         return total.reshape(48, 768)
 
@@ -1365,11 +1474,13 @@
     outer[0:48, :] = summed(6)
     outer[48:96, :] = summed(7)
     index = 8 * b + s
-    vectors = vparts[0] + vparts[1] + vparts[2] + vparts[3]
+    vectors = vparts[0] + vparts[1]
     row = lax.broadcasted_iota(jnp.int32, (16, 128), 0)
     by24 = pltpu.roll(vectors, lax.rem(128 * 24 - 24 * index, 128), 1)
     by96 = pltpu.roll(vectors, lax.rem(128 * 96 - 96 * index, 128), 1)
-    small[...] = jnp.where(row == 13, by96, by24)
+    small = jnp.where(row == 13, by96, by24)
+    for j, ref in enumerate(smalls):
+        ref[...] = small[j : j + 1, 0 : ref.shape[1]]
 
 
 def final_call(*inputs):
@@ -1377,15 +1488,15 @@
         jax.ShapeDtypeStruct((128, 768), LOW),
         jax.ShapeDtypeStruct((128, 768), WIDE),
         jax.ShapeDtypeStruct((128, 768), WIDE),
-        jax.ShapeDtypeStruct((16, 128), WIDE),
     ]
     shapes += [jax.ShapeDtypeStruct((24, 768), WIDE)] * 8
     shapes += [jax.ShapeDtypeStruct((24, 3072), WIDE), jax.ShapeDtypeStruct((96, 768), WIDE)]
+    shapes += [jax.ShapeDtypeStruct((1, 24), WIDE)] * 13 + [jax.ShapeDtypeStruct((1, 96), WIDE)]
     return pl.pallas_call(
         final_kernel,
         out_shape=shapes,
         in_specs=[vmem()] * 7,
-        out_specs=[vmem()] * 14,
+        out_specs=[vmem()] * 27,
         compiler_params=pltpu.CompilerParams(vmem_limit_bytes=VMEM_BYTES),
     )(*inputs)
 
@@ -1406,16 +1517,16 @@
         memory_segments,
     )
     results = final_call(*results)
-    output, tokens_grad, memory_grad, small = results[:4]
-    matrices, inner_grad, outer_grad = results[4:12], results[12], results[13]
-    vector = [small[j, 0:24] for j in range(13)]
+    output, tokens_grad, memory_grad = results[:3]
+    matrices, inner_grad, outer_grad = results[3:11], results[11], results[12]
+    vector = [small.reshape(-1) for small in results[13:]]
     return (
         (output[None], tokens_grad[None], memory_grad[None])
         + tuple(matrices[0:4])
         + tuple(vector[0:5])
         + tuple(matrices[4:8])
         + tuple(vector[5:10])
-        + (inner_grad, small[13, 0:96], outer_grad)
+        + (inner_grad, vector[13], outer_grad)
         + tuple(vector[10:13])
     )
 

time: 258 us -> 208 us (0.81)
  Pallas kernels: 254 us -> 207 us
  local copies, waits for them, and re-layouts: 2.72 us -> 0 us
    pallas_call x1, Pallas kernels: 250 us -> 203 us  [layer_call(): pl.pallas_call(layer_kernel, out_shape=shapes, in_specs=[anywhere] * 29,...]
    squeeze x2 -> x0, local copies, waits for them, and re-layouts: 2.72 us -> none  [the longest x1 1.53 us: fast_shards(): vector = [small[j, 0:24] for j in range(13)]]
where the time goes in v3:
time: 208 us; the launch traced here: 207 us
  Pallas kernels  207 us (100%)
    pallas_call x1, Pallas kernels, layer_call(): pl.pallas_call(layer_kernel, out_shape=shapes, in_specs=[anywhere] * 29,...  203 us

profile of v3, /device:TPU:0, one launch (start us, length us, event | category | flops | bytes accessed | tf_op | source)
XLA Modules:
  0.0 207.5 jit_solution(8515941828387397166)
XLA Ops:
  0.7 203.5 %shard_map.484 = (bf16[128,768]{1,0:T(8,128)(2,1)}, bf16[8,3,16,768]{3,2,1,0:T(8,128)(2,1)}, bf16[8,3,16,768]{3,2,1,0:T(8,128)(2,1)}, f32[2,16,128]{2,1,0:T(8,12...) custom-call(bf16[24,768]{1,0:T(8,128)(2,1)} %refs_0_.1, bf16[24,768]{1,0:T(8,128)(2,1)} %refs_1_.1, ...), custom_call_target="tpu_custom_call" | custom-call | tf_op jit(solution)/shard_map/pallas_call | solution.py:1433
  204.2 3.1 %shard_map.485 = (bf16[128,768]{1,0:T(8,128)(2,1)}, f32[128,768]{1,0:T(8,128)}, f32[128,768]{1,0:T(8,128)}, f32[24,768]{1,0:T(8,128)}, f32[24,768]{1,0:T(8,128)}...) custom-call(bf16[128,768]{1,0:T(8,128)(2,1)} %get-tuple-element.61.o, ...), custom_call_target="tpu_custom_call" | custom-call | tf_op jit(solution)/shard_map/pallas_call | solution.py:1495

commit v4 on v3

--- a/solution.py
+++ b/solution.py
@@ -472,9 +472,9 @@
 
 
 FORWARD = (
-    0, "prepare", 10, 1, 20, 11, 2, 30, 21, 12, 3, "tokens", 40, 31, 22, 13, 4, 50, 41, 32, 23, 14,
-    "memory", 60, 51, 42, 33, 24, 70, 61, 52, 43, 34, 25, "self", 71, 62, 53, 44, 35, 72, "project",
-    63, "cross", 54, 45, 73, 55, "feed1", "feed2", 64, 74,
+    0, "prepare", 10, 1, 20, 11, 2, 30, 21, 12, 3, "tokens", 40, 31, 22, 13, 4, 50, "memory", 41,
+    32, 23, 14, 60, 51, 42, 33, 24, 70, 61, 52, 43, 34, 25, "self", 71, 62, 53, 44, 35, 72,
+    "project", 63, "cross", 54, 45, 73, 55, "feed1", "feed2", 64, 74,
 )
 BACKWARD = (
     "slopes", 60, 70, "inner4", 61, 40, "inner5", 50, 41, 51, 71, "inner", "norm2", "cross",

time: 208 us -> 207 us (level)
  no operation moved by 1% of the time
where the time goes in v4:
time: 207 us; the launch traced here: 205 us
  Pallas kernels  205 us (99%)
    pallas_call x1, Pallas kernels, layer_call(): pl.pallas_call(layer_kernel, out_shape=shapes, in_specs=[anywhere] * 29,...  201 us

profile of v4, /device:TPU:0, one launch (start us, length us, event | category | flops | bytes accessed | tf_op | source)
XLA Modules:
  0.0 205.4 jit_solution(8158140462347523070)
XLA Ops:
  0.7 201.4 %shard_map.484 = (bf16[128,768]{1,0:T(8,128)(2,1)}, bf16[8,3,16,768]{3,2,1,0:T(8,128)(2,1)}, bf16[8,3,16,768]{3,2,1,0:T(8,128)(2,1)}, f32[2,16,128]{2,1,0:T(8,12...) custom-call(bf16[24,768]{1,0:T(8,128)(2,1)} %refs_0_.1, bf16[24,768]{1,0:T(8,128)(2,1)} %refs_1_.1, ...), custom_call_target="tpu_custom_call" | custom-call | tf_op jit(solution)/shard_map/pallas_call | solution.py:1433
  202.1 3.1 %shard_map.485 = (bf16[128,768]{1,0:T(8,128)(2,1)}, f32[128,768]{1,0:T(8,128)}, f32[128,768]{1,0:T(8,128)}, f32[24,768]{1,0:T(8,128)}, f32[24,768]{1,0:T(8,128)}...) custom-call(bf16[128,768]{1,0:T(8,128)(2,1)} %get-tuple-element.61.o, ...), custom_call_target="tpu_custom_call" | custom-call | tf_op jit(solution)/shard_map/pallas_call | solution.py:1495
